TPU v7x, 32 devices: a whole 2x2x4 slice. The times are simulated.
32 devices in a mesh: groups: 2 (over x), seq: 16 (over z, y, core).
Axes of the slice: x: 2, y: 2, z: 4, core: 2. Of those that a mesh axis runs over, the one named last changes fastest.
Arguments:
- tokens: bfloat16 [4096, 3072], P(('groups', 'seq')), parts along dimension 0
- grad_out: bfloat16 [4096, 3072], P(('groups', 'seq')), parts along dimension 0, may hold values from -6 to 6
- event_type: int32 [4096, 1], P(('groups', 'seq')), parts along dimension 0, may hold values from 0 to 3; in each aligned block of 128 rows (0 to 127, 128 to 255, ...) at most 36 rows name the same one
- type_gain: float32 [4, 3072], replicated, may hold values from 0.1 to 1.9
- up_weight: bfloat16 [3072, 24576], P(None, 'seq'), may hold values from -0.109375 to 0.109375
- down_weight: bfloat16 [24576, 3072], P('seq'), may hold values from -0.078125 to 0.078125
Outputs:
- grad_tokens: bfloat16 [4096, 3072], P(('groups', 'seq')), parts along dimension 0
- grad_gain: float32 [8, 3072], P('groups'), parts along dimension 0
- grad_up: bfloat16 [6144, 24576], P('groups', 'seq'), parts along dimension 0
- grad_down: bfloat16 [49152, 3072], P(('groups', 'seq')), parts along dimension 0
There are 2 independent parts, one for each index of `groups`. A program takes and returns all parts, laid end to end along the dimension named above; an argument that names none is the same for every part. Nothing has to cross between parts.
Inputs may be any that keep to these rules, and one draw needn't show every extreme that they name: `event_type`: among the events of one index of seq, at most 36 have the same type, and some index reaches 36 in every draw.
All inputs are finite; a program needn't handle non-finite values.
Results may differ from a plain program's by a relative error of at most 0.006.
Values may be sent and summed in bfloat16 or wider, within the bound.
No kernel may reach another device: no remote copies, remote signals or barrier semaphores. Data moves between devices by JAX's collectives and lax.ppermute only.
A program may use at most 128 MiB of HBM per device.

v0:
```python
import jax
import jax.numpy as jnp
from jax import lax
from jax.sharding import PartitionSpec as P

TYPES = 4
CAP = 36


EPS = 1e-06


def owner_pass(recv_normed, recv_grad, up_weight, down_weight):
    sources, slots, model_width = recv_normed.shape
    rows_normed = recv_normed.reshape(sources * slots, model_width)
    rows_grad = recv_grad.reshape(sources * slots, model_width)
    preact = jnp.dot(rows_normed, up_weight, preferred_element_type=jnp.float32)
    gate_sig = jax.nn.sigmoid(preact)
    activation = (preact * gate_sig).astype(jnp.bfloat16)
    grad_act = lax.dot_general(
        rows_grad, down_weight, (((1,), (1,)), ((), ())), preferred_element_type=jnp.float32
    )
    grad_pre = (grad_act * (gate_sig * (1.0 + preact * (1.0 - gate_sig)))).astype(jnp.bfloat16)
    part_dx = lax.dot_general(
        grad_pre, up_weight, (((1,), (1,)), ((), ())), preferred_element_type=jnp.float32
    ).astype(jnp.bfloat16)
    hidden_count = up_weight.shape[1]
    return (
        part_dx.reshape(sources, slots, model_width),
        activation.reshape(sources, slots, hidden_count),
        grad_pre.reshape(sources, slots, hidden_count),
    )


def local(tokens, grad_out, event_type, type_gain, up_weight, down_weight):
    seq_count = lax.axis_size("seq")
    owners = seq_count // TYPES
    tok_rows, model_width = tokens.shape
    hidden_count = up_weight.shape[1]
    type_ids = event_type[:, 0]
    onehot_int = (type_ids[:, None] == jnp.arange(TYPES, dtype=jnp.int32)[None, :]).astype(
        jnp.int32
    )
    running = jnp.cumsum(onehot_int, axis=0) - 1
    slot_rank = jnp.sum(running * onehot_int, axis=1)
    slot_index = type_ids * CAP + slot_rank
    placement = jnp.arange(TYPES * CAP, dtype=jnp.int32)[:, None] == slot_index[None, :]
    place_half = placement.astype(jnp.bfloat16)
    onehot_f32 = onehot_int.astype(jnp.float32)
    tok_f32 = tokens.astype(jnp.float32)
    inverse = lax.rsqrt(jnp.mean(tok_f32 * tok_f32, axis=1, keepdims=True) + EPS)
    gain_rows = jnp.dot(
        onehot_f32, type_gain, precision=lax.Precision.HIGHEST, preferred_element_type=jnp.float32
    )
    normed = (tok_f32 * inverse * gain_rows).astype(jnp.bfloat16)
    packed_normed = jnp.dot(place_half, normed, preferred_element_type=jnp.float32).astype(
        jnp.bfloat16
    )
    packed_grad = jnp.dot(place_half, grad_out, preferred_element_type=jnp.float32).astype(
        jnp.bfloat16
    )
    send_normed = jnp.repeat(packed_normed.reshape(TYPES, CAP, model_width), owners, axis=0)
    send_grad = jnp.repeat(packed_grad.reshape(TYPES, CAP, model_width), owners, axis=0)
    recv_normed, recv_grad = (
        lax.all_to_all(send_normed, "seq", split_axis=0, concat_axis=0, tiled=True),
        lax.all_to_all(send_grad, "seq", split_axis=0, concat_axis=0, tiled=True),
    )
    part_dx, activation, grad_pre = owner_pass(recv_normed, recv_grad, up_weight, down_weight)
    returned_dx = lax.all_to_all(part_dx, "seq", split_axis=0, concat_axis=0, tiled=True)
    rows_normed = recv_normed.reshape(-1, model_width)
    rows_grad = recv_grad.reshape(-1, model_width)
    grad_up = lax.dot_general(
        rows_normed,
        grad_pre.reshape(-1, hidden_count),
        (((0,), (0,)), ((), ())),
        preferred_element_type=jnp.float32,
    ).astype(jnp.bfloat16)
    grad_down = lax.dot_general(
        activation.reshape(-1, hidden_count),
        rows_grad,
        (((0,), (0,)), ((), ())),
        preferred_element_type=jnp.float32,
    ).astype(jnp.bfloat16)
    summed = returned_dx.reshape(TYPES, owners, CAP, model_width).astype(jnp.float32).sum(axis=1)
    summed = summed.reshape(TYPES * CAP, model_width)
    grad_normed = lax.dot_general(
        placement.astype(jnp.float32),
        summed,
        (((0,), (0,)), ((), ())),
        precision=lax.Precision.HIGHEST,
        preferred_element_type=jnp.float32,
    )
    scaled = grad_normed * gain_rows
    inner_sum = jnp.sum(scaled * tok_f32, axis=1, keepdims=True)
    branch = scaled * inverse - tok_f32 * inner_sum * inverse * inverse * inverse / model_width
    grad_tokens = (grad_out.astype(jnp.float32) + branch).astype(jnp.bfloat16)
    gain_term = lax.dot_general(
        onehot_f32,
        grad_normed * tok_f32 * inverse,
        (((0,), (0,)), ((), ())),
        precision=lax.Precision.HIGHEST,
        preferred_element_type=jnp.float32,
    )
    grad_gain = lax.psum(gain_term, "seq")
    return (grad_tokens, grad_gain, grad_up, grad_down)


def solution(mesh):
    placed = (
        P(("groups", "seq"), None),
        P(("groups", "seq"), None),
        P(("groups", "seq"), None),
        P(),
        P(None, "seq"),
        P("seq", None),
    )
    return jax.shard_map(
        local,
        mesh=mesh,
        in_specs=placed,
        out_specs=(
            P(("groups", "seq"), None),
            P("groups", None),
            P("groups", "seq"),
            P(("groups", "seq"), None),
        ),
        check_vma=False,
    )
```

profile of v0, /device:TPU:0, one launch (start us, length us, event | category | flops | bytes accessed | tf_op | source)
XLA Modules:
  0.0 396.0 jit_solution(493970869049641956)
XLA Ops:
  0.6 1.4 fusion.1
  4.5 2.1 fusion.20
  6.6 1.6 convolution_convert_fusion.3
  8.3 2.4 broadcast_in_dim.5
  10.8 7.6 %all-to-all-start.1 = ((bf16[16,36,3072]{2,1,0:T(8,128)(2,1)}), bf16[16,36,3072]{2,1,0:T(8,128)(2,1)}, u32[]{:S(2)}, u32[]{:S(2)}) async-start(bf16[16,36,3072]{2,1,0:T(8,128)(2,1)} %bitcast.19), calls=%async_computation.1 | async-start | bytes 7864320 | tf_op jit(solution)/shard_map/all_to_all | solution.py:65
  18.9 72.5 %all-to-all-done.1 = bf16[16,36,3072]{2,1,0:T(8,128)(2,1)} async-done(((bf16[16,36,3072]{2,1,0:T(8,128)(2,1)}), bf16[16,36,3072]{2,1,0:T(8,128)(2,1)}, u32[]{:S(2)}, u32[]{:S(2)}) %all-to-all-start.1) | async-done | bytes 3538976 | tf_op jit(solution)/shard_map/all_to_all | solution.py:65
  91.4 2.4 broadcast_in_dim.4
  93.9 18.6 %all-to-all-start = ((bf16[16,36,3072]{2,1,0:T(8,128)(2,1)}), bf16[16,36,3072]{2,1,0:T(8,128)(2,1)}, u32[]{:S(2)}, u32[]{:S(2)}) async-start(bf16[16,36,3072]{2,1,0:T(8,128)(2,1)} %bitcast.20), calls=%async_computation | async-start | bytes 7864320 | tf_op jit(solution)/shard_map/all_to_all | solution.py:66
  112.5 4.7 %reshape.59 = bf16[576,3072]{1,0:T(8,128)(2,1)} reshape(bf16[16,36,3072]{2,1,0:T(8,128)(2,1)} %all-to-all-done.1) | data formatting | bytes 7077888 | tf_op jit(solution)/shard_map/reshape | solution.py:15
  117.2 10.6 %fusion.31 = f32[576,1536]{1,0:T(8,128)} fusion(bf16[576,3072]{1,0:T(8,128)(2,1)} %reshape.59, bf16[3072,1536]{1,0:T(8,128)(2,1)} %param.10), kind=kOutput, calls=%fused_computation.46 | convolution fusion | flops 5435817984 | bytes 16515072 | tf_op jit(solution)/shard_map/dot_general | solution.py:17
  127.8 57.8 %all-to-all-done = bf16[16,36,3072]{2,1,0:T(8,128)(2,1)} async-done(((bf16[16,36,3072]{2,1,0:T(8,128)(2,1)}), bf16[16,36,3072]{2,1,0:T(8,128)(2,1)}, u32[]{:S(2)}, u32[]{:S(2)}) %all-to-all-start) | async-done | bytes 3538976 | tf_op jit(solution)/shard_map/all_to_all | solution.py:66
  185.6 4.7 %reshape.56 = bf16[576,3072]{1,0:T(8,128)(2,1)} reshape(bf16[16,36,3072]{2,1,0:T(8,128)(2,1)} %all-to-all-done) | data formatting | bytes 7077888 | tf_op jit(solution)/shard_map/reshape | solution.py:16
  190.3 10.4 %multiply_convert_fusion.1 = bf16[576,1536]{1,0:T(8,128)(2,1)S(1)} fusion(f32[576,1536]{1,0:T(8,128)} %fusion.31, bf16[576,3072]{1,0:T(8,128)(2,1)} %reshape.56, bf16[1536,3072]{1,0:T(8,128)(2,1)} %param.11), kind=kOutput, calls=%fused_computation.7 | convolution fusion | flops 5443780608 | bytes 18284544 | tf_op jit(solution)/shard_map/dot_general | solution.py:20
  200.7 10.8 %convolution_convert_fusion.2 = bf16[576,3072]{1,0:T(8,128)(2,1)} fusion(bf16[576,1536]{1,0:T(8,128)(2,1)S(1)} %multiply_convert_fusion.1, bf16[3072,1536]{1,0:T(8,128)(2,1)} %param.10), kind=kOutput, calls=%fused_computation.3 | convolution fusion | flops 5437587456 | bytes 14745600 | tf_op jit(solution)/shard_map/dot_general | solution.py:24
  211.4 4.7 %reshape.60 = bf16[16,36,3072]{2,1,0:T(8,128)(2,1)} reshape(bf16[576,3072]{1,0:T(8,128)(2,1)} %convolution_convert_fusion.2) | data formatting | bytes 7077888 | tf_op jit(solution)/shard_map/reshape | solution.py:29
  216.1 18.6 %all-to-all-start.2 = ((bf16[16,36,3072]{2,1,0:T(8,128)(2,1)}), bf16[16,36,3072]{2,1,0:T(8,128)(2,1)}, u32[]{:S(2)}, u32[]{:S(2)}) async-start(bf16[16,36,3072]{2,1,0:T(8,128)(2,1)} %reshape.60), calls=%async_computation.2 | async-start | bytes 7864320 | tf_op jit(solution)/shard_map/all_to_all | solution.py:69
  234.8 11.8 %convolution_convert_fusion.1 = bf16[3072,1536]{1,0:T(8,128)(2,1)} fusion(bf16[576,3072]{1,0:T(8,128)(2,1)} %reshape.59, bf16[576,1536]{1,0:T(8,128)(2,1)S(1)} %multiply_convert_fusion.1), kind=kOutput, calls=%fused_computation.1 | convolution fusion | flops 5440536576 | bytes 14745600 | tf_op jit(solution)/shard_map/dot_general | solution.py:72
  246.6 9.9 %convolution_convert_fusion = bf16[1536,3072]{1,0:T(8,128)(2,1)} fusion(bf16[576,3072]{1,0:T(8,128)(2,1)S(1)} %copy-done.3, f32[576,1536]{1,0:T(8,128)S(1)} %copy-done.7), kind=kOutput, calls=%fused_computation | convolution fusion | flops 5444960256 | bytes 16515072 | tf_op jit(solution)/shard_map/dot_general | solution.py:78
  256.5 51.3 %all-to-all-done.2 = bf16[16,36,3072]{2,1,0:T(8,128)(2,1)} async-done(((bf16[16,36,3072]{2,1,0:T(8,128)(2,1)}), bf16[16,36,3072]{2,1,0:T(8,128)(2,1)}, u32[]{:S(2)}, u32[]{:S(2)}) %all-to-all-start.2) | async-done | bytes 3538976 | tf_op jit(solution)/shard_map/all_to_all | solution.py:69
  307.9 4.3 %convert_reduce_fusion = f32[4,36,3072]{2,1,0:T(8,128)} fusion(bf16[16,36,3072]{2,1,0:T(8,128)(2,1)} %all-to-all-done.2), kind=kLoop, calls=%fused_computation.2 | loop fusion | flops 3096576 | bytes 5308416 | tf_op jit(solution)/shard_map/reduce_sum | solution.py:84
  312.2 2.9 reshape.61
  315.1 2.9 fusion.4
  319.1 1.6 fusion.11
  320.7 75.3 %psum.7 = f32[4,3072]{1,0:T(4,128)} all-reduce(f32[4,3072]{1,0:T(4,128)S(1)} %fusion.13), channel_id=1, replica_groups=mesh['groups'=2,'seq'=16] {'seq'}, use_global_device_ids=true, to_apply=%region_5.6 | all-reduce | flops 12288 | bytes 98304 | tf_op jit(solution)/shard_map/psum | solution.py:104
  (25 shorter events, 4.2 us)
Async XLA Ops:
  0.6 3.8 copy-start
  10.8 7.6 %copy-start.4 = (bf16[128,3072]{1,0:T(8,128)(2,1)S(1)}, bf16[128,3072]{1,0:T(8,128)(2,1)}, u32[]{:S(2)}) copy-start(bf16[128,3072]{1,0:T(8,128)(2,1)} %param.7) | copy-start | bytes 2359300
  10.8 80.7 %all-to-all-start.1 = ((bf16[16,36,3072]{2,1,0:T(8,128)(2,1)}), bf16[16,36,3072]{2,1,0:T(8,128)(2,1)}, u32[]{:S(2)}, u32[]{:S(2)}) async-start(bf16[16,36,3072]{2,1,0:T(8,128)(2,1)} %bitcast.19), calls=%async_computation.1 | async-start | bytes 7864320 | tf_op jit(solution)/shard_map/all_to_all | solution.py:65
  93.9 91.8 %all-to-all-start = ((bf16[16,36,3072]{2,1,0:T(8,128)(2,1)}), bf16[16,36,3072]{2,1,0:T(8,128)(2,1)}, u32[]{:S(2)}, u32[]{:S(2)}) async-start(bf16[16,36,3072]{2,1,0:T(8,128)(2,1)} %bitcast.20), calls=%async_computation | async-start | bytes 7864320 | tf_op jit(solution)/shard_map/all_to_all | solution.py:66
  216.1 91.8 %all-to-all-start.2 = ((bf16[16,36,3072]{2,1,0:T(8,128)(2,1)}), bf16[16,36,3072]{2,1,0:T(8,128)(2,1)}, u32[]{:S(2)}, u32[]{:S(2)}) async-start(bf16[16,36,3072]{2,1,0:T(8,128)(2,1)} %reshape.60), calls=%async_computation.2 | async-start | bytes 7864320 | tf_op jit(solution)/shard_map/all_to_all | solution.py:69
  234.8 11.9 %copy-start.3 = (bf16[576,3072]{1,0:T(8,128)(2,1)S(1)}, bf16[576,3072]{1,0:T(8,128)(2,1)}, u32[]{:S(2)}) copy-start(bf16[576,3072]{1,0:T(8,128)(2,1)} %reshape.56) | copy-start | bytes 10616836
  234.8 11.8 %copy-start.7 = (f32[576,1536]{1,0:T(8,128)S(1)}, f32[576,1536]{1,0:T(8,128)}, u32[]{:S(2)}) copy-start(f32[576,1536]{1,0:T(8,128)} %fusion.31) | copy-start | bytes 10616836
  256.5 58.6 %copy-start.2 = (bf16[128,3072]{1,0:T(8,128)(2,1)S(1)}, bf16[128,3072]{1,0:T(8,128)(2,1)}, u32[]{:S(2)}) copy-start(bf16[128,3072]{1,0:T(8,128)(2,1)} %param.6) | copy-start | bytes 2359300
  315.1 2.9 copy-start.6
  315.1 4.0 %copy-start.5 = (bf16[128,3072]{1,0:T(8,128)(2,1)S(1)}, bf16[128,3072]{1,0:T(8,128)(2,1)}, u32[]{:S(2)}) copy-start(bf16[128,3072]{1,0:T(8,128)(2,1)} %param.7) | copy-start | bytes 2359300
  318.0 78.0 %copy-start.1 = (f32[4,3072]{1,0:T(4,128)S(1)}, f32[4,3072]{1,0:T(4,128)}, u32[]{:S(2)}) copy-start(f32[4,3072]{1,0:T(4,128)} %param.9) | copy-start | bytes 147460
where the time goes:
time: 397 us; the launch traced here: 396 us
  waiting for transfers between devices  182 us (46%)
  blocking collectives  75.3 us (19%)
  matrix products  61.5 us (15%)
  starting transfers between devices  44.8 us (11%)
  local copies, waits for them, and re-layouts  22.2 us (6%)
  other arithmetic  9.72 us (2%)
    psum x1, blocking collectives, local(): grad_gain = lax.psum(gain_term, 'seq')  75.3 us
    all_to_all x1, waiting for transfers between devices, local(): lax.all_to_all(send_normed, 'seq', split_axis=0, concat_axis=0, tiled=True)  72.5 us
    all_to_all x1, waiting for transfers between devices, local(): lax.all_to_all(send_grad, 'seq', split_axis=0, concat_axis=0, tiled=True)  57.8 us
    all_to_all x1, waiting for transfers between devices, local(): lax.all_to_all(part_dx, 'seq', split_axis=0, concat_axis=0, tiled=True)  51.3 us
    all_to_all x1, starting transfers between devices, local(): lax.all_to_all(part_dx, 'seq', split_axis=0, concat_axis=0, tiled=True)  18.6 us
    all_to_all x1, starting transfers between devices, local(): lax.all_to_all(send_grad, 'seq', split_axis=0, concat_axis=0, tiled=True)  18.6 us
    dot_general x1, matrix products, local(): lax.dot_general(rows_normed, grad_pre.reshape(-1, hidden_count), (((0,),...  11.8 us
    dot_general x1, matrix products, owner_pass(): lax.dot_general(grad_pre, up_weight, (((1,), (1,)), ((), ())), preferred_...  10.8 us
  transfers between devices with their start and end apart: 3, of which 3 were waited for; matrix products, arithmetic and copies ran while one was open for 10% of the time, Pallas kernels for 0%

commit v1 on v0

v1 whole, which is shorter than its diff:
```python
import functools

import jax
import jax.numpy as jnp
from jax import lax
from jax.experimental import pallas as pl
from jax.experimental.pallas import tpu as pltpu
from jax.sharding import PartitionSpec as P

TYPES = 4
CAP = 36
MAIN = 32
TAIL = CAP - MAIN
BLOCK = 2 * CAP
EPS = 1e-06
CORES = 2

GROUPS = ((0, 1), (2,), (3,))

F32 = jnp.float32
BF16 = jnp.bfloat16
VMEM_LIMIT = 56 << 20
NT = (((1,), (1,)), ((), ()))
TN = (((0,), (0,)), ((), ()))


def params(limit=VMEM_LIMIT):
    return pltpu.CompilerParams(vmem_limit_bytes=limit)


def cost(flops, moved):
    return pl.CostEstimate(flops=int(flops), bytes_accessed=int(moved), transcendentals=0)


def token_terms(tokens_ref, type_ref, gain_ref):
    tok = tokens_ref[...].astype(F32)
    inverse = lax.rsqrt(jnp.mean(tok * tok, axis=1, keepdims=True) + EPS)
    types = type_ref[...]
    gain_rows = jnp.zeros_like(tok)
    for k in range(TYPES):
        gain_rows = jnp.where(types == k, gain_ref[k : k + 1, :], gain_rows)
    rows = tok.shape[0]
    lanes = lax.broadcasted_iota(jnp.int32, (rows, 128), 1)
    onehot = jnp.where(lanes == types, 1.0, 0.0)
    below = lax.broadcasted_iota(jnp.int32, (rows, rows), 1)
    above = lax.broadcasted_iota(jnp.int32, (rows, rows), 0)
    earlier = jnp.where(below < above, 1.0, 0.0).astype(BF16)
    running = jnp.dot(earlier, onehot.astype(BF16), preferred_element_type=F32)
    rank = jnp.sum(running * onehot, axis=1, keepdims=True).astype(jnp.int32)
    return tok, inverse, types, gain_rows, rank


def wide_mod(value):
    return jnp.where(value >= TYPES, value - TYPES, value)


def pack_kernel(plane_ref, tokens_ref, grad_ref, type_ref, gain_ref, *outs):
    tok, inverse, types, gain_rows, rank = token_terms(tokens_ref, type_ref, gain_ref)
    normed = (tok * inverse * gain_rows).astype(BF16)
    both = jnp.concatenate([normed, grad_ref[...]], axis=0)
    rows = tok.shape[0]
    lane = lax.broadcasted_iota(jnp.int32, (rows, BLOCK), 1)
    tail_n = lane - MAIN
    tail_g = lane - CAP
    slot_n = jnp.where(lane < MAIN, lane, jnp.where((lane >= 2 * MAIN) & (tail_n < CAP), tail_n, -1))
    slot_g = jnp.where((lane >= MAIN) & (lane < 2 * MAIN), lane - MAIN, jnp.where(tail_g >= MAIN, tail_g, -1))
    for shift, out in enumerate(outs):
        kind = wide_mod(plane_ref[0] + shift)
        here = types == kind
        pick_n = jnp.where(here & (rank == slot_n), 1.0, 0.0)
        pick_g = jnp.where(here & (rank == slot_g), 1.0, 0.0)
        pick = jnp.concatenate([pick_n, pick_g], axis=0).astype(BF16)
        out[...] = lax.dot_general(pick, both, TN, preferred_element_type=F32).astype(BF16)


def finish_kernel(plane_ref, tokens_ref, grad_ref, type_ref, gain_ref, *refs):
    returned = refs[:TYPES]
    gains = refs[TYPES : 2 * TYPES]
    out, gain_out = refs[2 * TYPES :]
    tok, inverse, types, gain_rows, rank = token_terms(tokens_ref, type_ref, gain_ref)
    rows, width = tok.shape
    lane = lax.broadcasted_iota(jnp.int32, (rows, BLOCK), 1)
    in_tail = lane >= 2 * MAIN
    slot_l = jnp.where(lane < MAIN, lane, jnp.where(in_tail & (lane < 2 * MAIN + TAIL), lane - MAIN, -1))
    slot_r = jnp.where(
        (lane >= MAIN) & ~in_tail, lane - MAIN, jnp.where(lane >= 2 * MAIN + TAIL, lane - CAP, -1)
    )
    left = jnp.zeros((rows, width // 2), F32)
    right = jnp.zeros((rows, width // 2), F32)
    for shift in range(TYPES):
        here = types == wide_mod(plane_ref[0] + shift)
        block = returned[shift][...]
        pick_l = jnp.where(here & (rank == slot_l), 1.0, 0.0).astype(BF16)
        pick_r = jnp.where(here & (rank == slot_r), 1.0, 0.0).astype(BF16)
        left += jnp.dot(pick_l, block, preferred_element_type=F32)
        right += jnp.dot(pick_r, block, preferred_element_type=F32)
    scaled = jnp.concatenate([left, right], axis=1) * gain_rows
    inner = jnp.sum(scaled * tok, axis=1, keepdims=True)
    branch = scaled * inverse - tok * (inner * inverse * inverse * inverse / width)
    out[...] = (grad_ref[...].astype(F32) + branch).astype(BF16)
    row = lax.broadcasted_iota(jnp.int32, (TYPES, width), 0)
    total = jnp.zeros((TYPES, width), F32)
    for shift in range(TYPES):
        kind = wide_mod(plane_ref[0] + TYPES - shift)
        total = jnp.where(row == kind, gains[shift][...], total)
    gain_out[...] = total / gain_ref[...]


def chunk_kernel(shifts, pairs, tile, out_tile, *refs):
    blocks = 2 * pairs * shifts
    ins = refs[:blocks]
    up, down, keep, send, normed, grads, act, pre, gain = refs[blocks : blocks + 9]
    blk, up_v, down_v, n_v, g_v, act_v, pre_v, keep_v, send_v, gain_v, in_sem, w_sem, o_sem = refs[blocks + 9 :]
    width, hidden = up.shape
    tiles = hidden // tile
    half = blocks // 2
    in_copies = [pltpu.make_async_copy(ins[i], blk.at[i], in_sem.at[i]) for i in range(blocks)]
    for copy in in_copies:
        copy.start()

    def up_copy(t):
        cols = pl.ds(pl.multiple_of(t * tile, tile), tile)
        return pltpu.make_async_copy(up.at[:, cols], up_v.at[:, cols], w_sem.at[0, t])

    def down_copy(t):
        rows = pl.ds(pl.multiple_of(t * tile, tile), tile)
        return pltpu.make_async_copy(down.at[rows, :], down_v.at[rows, :], w_sem.at[1, t])

    for t in range(tiles):
        up_copy(t).start()
        down_copy(t).start()
    for copy in in_copies:
        copy.wait()
    low = lax.broadcasted_iota(jnp.int32, (8, width), 0) < TAIL
    tails_n, tails_g = [], []
    for i in range(blocks):
        n_v[i * MAIN : (i + 1) * MAIN, :] = blk[i, 0:MAIN, :]
        g_v[i * MAIN : (i + 1) * MAIN, :] = blk[i, MAIN : 2 * MAIN, :]
    for i in range(0, blocks, 2):
        a = blk[i, 2 * MAIN : BLOCK, :].astype(F32)
        b = blk[i + 1, 2 * MAIN : BLOCK, :].astype(F32)
        tails_n.append(jnp.where(low, a, pltpu.roll(b, TAIL, 0)))
        tails_g.append(jnp.where(low, pltpu.roll(a, TAIL, 0), b))
    n_v[blocks * MAIN :, :] = jnp.concatenate(tails_n, axis=0).astype(BF16)
    g_v[blocks * MAIN :, :] = jnp.concatenate(tails_g, axis=0).astype(BF16)
    n_copy = pltpu.make_async_copy(n_v, normed, o_sem.at[0])
    g_copy = pltpu.make_async_copy(g_v, grads, o_sem.at[1])
    n_copy.start()
    g_copy.start()

    def forward(t, carry):
        cols = pl.ds(pl.multiple_of(t * tile, tile), tile)
        up_copy(t).wait()
        preact = jnp.dot(n_v[...], up_v[:, cols], preferred_element_type=F32)
        down_copy(t).wait()
        grad_act = lax.dot_general(g_v[...], down_v[cols, :], NT, preferred_element_type=F32)
        sig = jax.nn.sigmoid(preact)
        act_v[:, cols] = (preact * sig).astype(BF16)
        pre_v[:, cols] = (grad_act * (sig * (1.0 + preact * (1.0 - sig)))).astype(BF16)
        return carry

    lax.fori_loop(0, tiles, forward, 0)
    act_copy = pltpu.make_async_copy(act_v, act, o_sem.at[2])
    pre_copy = pltpu.make_async_copy(pre_v, pre, o_sem.at[3])
    act_copy.start()
    pre_copy.start()
    m, t4 = half * MAIN, half * TAIL

    def backward(t, carry):
        cols = pl.ds(pl.multiple_of(t * out_tile, out_tile), out_tile)
        dx = lax.dot_general(pre_v[...], up_v[cols, :], NT, preferred_element_type=F32)
        keep_v[0:m, cols] = dx[0:m]
        keep_v[m:, cols] = dx[2 * m : 2 * m + t4]
        send_v[:, cols] = jnp.concatenate([dx[m : 2 * m], dx[2 * m + t4 :]], axis=0).astype(BF16)
        gain_v[:, cols] = jnp.sum(dx * n_v[:, cols].astype(F32), axis=0, keepdims=True)
        return carry

    lax.fori_loop(0, width // out_tile, backward, 0)
    last = [
        pltpu.make_async_copy(send_v, send, o_sem.at[4]),
        pltpu.make_async_copy(keep_v, keep, o_sem.at[5]),
        pltpu.make_async_copy(gain_v, gain, o_sem.at[6]),
    ]
    for copy in last:
        copy.start()
    for copy in [n_copy, g_copy, act_copy, pre_copy] + last:
        copy.wait()


def run_chunk(blocks, up, down, shifts, pairs):
    width, hidden = up.shape
    rows = len(blocks) * CAP
    tile = min(512, hidden)
    out_tile = min(512, width)
    any_spec = pl.BlockSpec(memory_space=pl.ANY)
    shapes = [
        ((rows // 2, width), F32),
        ((rows // 2, width), BF16),
        ((rows, width), BF16),
        ((rows, width), BF16),
        ((rows, hidden), BF16),
        ((rows, hidden), BF16),
        ((1, width), F32),
    ]
    return pl.pallas_call(
        functools.partial(chunk_kernel, shifts, pairs, tile, out_tile),
        in_specs=[any_spec] * (len(blocks) + 2),
        out_specs=[any_spec] * len(shapes),
        out_shape=[jax.ShapeDtypeStruct(s, d) for s, d in shapes],
        scratch_shapes=[
            pltpu.VMEM((len(blocks), BLOCK, width), BF16),
            pltpu.VMEM((width, hidden), BF16),
            pltpu.VMEM((hidden, width), BF16),
            pltpu.VMEM((rows, width), BF16),
            pltpu.VMEM((rows, width), BF16),
            pltpu.VMEM((rows, hidden), BF16),
            pltpu.VMEM((rows, hidden), BF16),
            pltpu.VMEM((rows // 2, width), F32),
            pltpu.VMEM((rows // 2, width), BF16),
            pltpu.VMEM((1, width), F32),
            pltpu.SemaphoreType.DMA((len(blocks),)),
            pltpu.SemaphoreType.DMA((2, hidden // tile)),
            pltpu.SemaphoreType.DMA((7,)),
        ],
        compiler_params=params(),
        cost_estimate=cost(6 * rows * width * hidden, 4 * width * hidden),
    )(*blocks, up, down)


def split_kernel(shifts, pairs, keep_ref, recv_ref, *outs):
    half = keep_ref.shape[1] // 2
    low = lax.broadcasted_iota(jnp.int32, (8, half), 0) < TAIL
    base = shifts * pairs * MAIN
    for s in range(shifts):
        for i in range(pairs):
            at = s * pairs + i
            main = keep_ref[at * MAIN : (at + 1) * MAIN, :] + recv_ref[at * MAIN : (at + 1) * MAIN, :].astype(F32)
            first = base + (at // 2) * 8
            tail = keep_ref[first : first + 8, :] + recv_ref[first : first + 8, :].astype(F32)
            if at % 2 == 0:
                joined = jnp.where(low, tail[:, :half], pltpu.roll(tail[:, half:], TAIL, 0))
            else:
                joined = jnp.where(low, pltpu.roll(tail[:, :half], TAIL, 0), tail[:, half:])
            whole = jnp.concatenate([main[:, :half], main[:, half:], joined], axis=0)
            outs[i][s * BLOCK : (s + 1) * BLOCK, :] = whole.astype(outs[i].dtype)


def split_sum(keep, recv, shifts, pairs):
    width = keep.shape[1]
    shape = (shifts * BLOCK, width // 2)
    return pl.pallas_call(
        functools.partial(split_kernel, shifts, pairs),
        out_shape=[jax.ShapeDtypeStruct(shape, F32 if i == 0 else BF16) for i in range(pairs)],
        compiler_params=params(),
    )(keep, recv)


def weight_kernel(count, tile, *refs):
    lefts, rights, out = refs[:count], refs[count : 2 * count], refs[2 * count]
    stacked = refs[2 * count + 1]

    @pl.when(pl.program_id(0) == 0)
    def _():
        first = 0
        for right in rights:
            stacked[first : first + right.shape[0], :] = right[...]
            first += right.shape[0]

    left = jnp.concatenate([ref[...] for ref in lefts], axis=0)
    out[...] = lax.dot_general(left, stacked[...], TN, preferred_element_type=F32).astype(BF16)


def weight_grad(lefts, rights):
    rows = sum(x.shape[0] for x in lefts)
    long, wide = lefts[0].shape[1], rights[0].shape[1]
    tile = min(512, long)
    return pl.pallas_call(
        functools.partial(weight_kernel, len(lefts), tile),
        grid=(long // tile,),
        in_specs=[pl.BlockSpec((x.shape[0], tile), lambda j: (0, j)) for x in lefts]
        + [pl.BlockSpec(x.shape, lambda j: (0, 0)) for x in rights],
        out_specs=pl.BlockSpec((tile, wide), lambda j: (j, 0)),
        out_shape=jax.ShapeDtypeStruct((long, wide), BF16),
        scratch_shapes=[pltpu.VMEM((rows, wide), BF16)],
        compiler_params=params(),
        cost_estimate=cost(2 * rows * long * wide, 2 * long * wide),
    )(*lefts, *rights)


def local(tokens, grad_out, event_type, type_gain, up_weight, down_weight):
    seq = lax.axis_size("seq")
    owners = seq // TYPES
    pairs = owners // CORES
    width = tokens.shape[1]
    plane = (lax.axis_index("seq") // owners).astype(jnp.int32).reshape(1)

    def moved(x, to):
        return lax.ppermute(x, "seq", [(i, to(i)) for i in range(seq)])

    def to_plane(x, shift):
        return moved(x, lambda i: (i + shift * owners) % seq)

    def to_pair(x, shift):
        return moved(x, lambda i: i // owners * owners + (i % owners + CORES * shift) % owners)

    def to_core(x):
        return moved(x, lambda i: i ^ 1)

    smem = pl.BlockSpec(memory_space=pltpu.SMEM)
    vmem = pl.BlockSpec(memory_space=pltpu.VMEM)
    packed = pl.pallas_call(
        pack_kernel,
        in_specs=[smem] + [vmem] * 4,
        out_shape=[jax.ShapeDtypeStruct((BLOCK, width), BF16)] * TYPES,
        compiler_params=params(),
    )(plane, tokens, grad_out, event_type, type_gain)

    blocks = {}
    for shift in range(TYPES):
        own = to_plane(packed[shift], shift) if shift else packed[shift]
        mine = [own] + [to_pair(own, j) for j in range(1, pairs)]
        blocks[shift] = (mine, [to_core(x) for x in mine])

    acts, pres, norms, grads, returned = [], [], [], [], [None] * TYPES
    gain = jnp.zeros((1, width), F32)
    for group in GROUPS:
        order = [x for part in (0, 1) for shift in group for x in blocks[shift][part]]
        keep, send, normed, grad, act, pre, gain_part = run_chunk(
            order, up_weight, down_weight, len(group), pairs
        )
        acts.append(act)
        pres.append(pre)
        norms.append(normed)
        grads.append(grad)
        gain = gain + gain_part
        parts = split_sum(keep, to_core(send), len(group), pairs)
        total = parts[0]
        for j in range(1, pairs):
            total = total + to_pair(parts[j], pairs - j).astype(F32)
        for at, shift in enumerate(group):
            back = total[at * BLOCK : (at + 1) * BLOCK].astype(BF16)
            returned[shift] = to_plane(back, TYPES - shift) if shift else back

    gain = gain + to_core(gain)
    plane_gain = gain
    for j in range(1, pairs):
        plane_gain = plane_gain + to_pair(gain, j)
    gains = [plane_gain] + [to_plane(plane_gain, shift) for shift in range(1, TYPES)]

    grad_up = weight_grad(norms, pres)
    grad_down = weight_grad(acts, grads)
    grad_tokens, grad_gain = pl.pallas_call(
        finish_kernel,
        in_specs=[smem] + [vmem] * (4 + 2 * TYPES),
        out_shape=[
            jax.ShapeDtypeStruct(tokens.shape, BF16),
            jax.ShapeDtypeStruct((TYPES, width), F32),
        ],
        compiler_params=params(),
    )(plane, tokens, grad_out, event_type, type_gain, *returned, *gains)
    return (grad_tokens, grad_gain, grad_up, grad_down)


def solution(mesh):
    placed = (
        P(("groups", "seq"), None),
        P(("groups", "seq"), None),
        P(("groups", "seq"), None),
        P(),
        P(None, "seq"),
        P("seq", None),
    )
    return jax.shard_map(
        local,
        mesh=mesh,
        in_specs=placed,
        out_specs=(
            P(("groups", "seq"), None),
            P("groups", None),
            P("groups", "seq"),
            P(("groups", "seq"), None),
        ),
        check_vma=False,
    )
```

time: 397 us -> 191 us (0.48)
  waiting for transfers between devices: 182 us -> 60.9 us
  Pallas kernels: 0 us -> 92.6 us
  blocking collectives: 75.3 us -> 0 us
  matrix products: 61.5 us -> 0 us
  starting transfers between devices: 44.8 us -> 26.7 us
  local copies, waits for them, and re-layouts: 22.2 us -> 6.22 us
  other arithmetic: 9.72 us -> 3.1 us
    all_to_all x3 -> x0, waiting for transfers between devices: 182 us -> none  [the longest x1 72.5 us: local(): lax.all_to_all(send_normed, 'seq', split_axis=0, concat_axis=0, tiled=True)]
    pallas_call x0 -> x10, Pallas kernels: none -> 92.6 us  [the longest x3 52.7 us: run_chunk(): pl.pallas_call(functools.partial(chunk_kernel, shifts, pairs, tile, out_t...]
    psum x1 -> x0, blocking collectives: 75.3 us -> none  [local(): grad_gain = lax.psum(gain_term, 'seq')]
    dot_general x10 -> x0, matrix products: 61.5 us -> none  [the longest x1 11.8 us: local(): lax.dot_general(rows_normed, grad_pre.reshape(-1, hidden_count), (((0,),...]
    ppermute x0 -> x29, waiting for transfers between devices: none -> 60.9 us  [moved(): return lax.ppermute(x, 'seq', [(i, to(i)) for i in range(seq)])]
    all_to_all x3 -> x0, starting transfers between devices: 44.8 us -> none  [the longest x1 18.6 us: local(): lax.all_to_all(part_dx, 'seq', split_axis=0, concat_axis=0, tiled=True)]
    ppermute x0 -> x29, starting transfers between devices: none -> 26.7 us  [moved(): return lax.ppermute(x, 'seq', [(i, to(i)) for i in range(seq)])]
    reshape x6 -> x0, local copies, waits for them, and re-layouts: 17.4 us -> none  [the longest x1 4.73 us: owner_pass(): rows_normed = recv_normed.reshape(sources * slots, model_width)]
  transfers between devices with their start and end apart: 3 -> 29, of which waited for: 3 -> 7; matrix products, arithmetic and copies ran while one was open for 10% -> 2% of each run, Pallas kernels for 0% -> 44%
where the time goes in v1:
time: 191 us
  Pallas kernels  92.6 us (48%)
  waiting for transfers between devices  60.9 us (32%)
  starting transfers between devices  26.7 us (14%)
  local copies, waits for them, and re-layouts  6.22 us (3%)
  other arithmetic  3.1 us (2%)
    ppermute x29, waiting for transfers between devices, moved(): return lax.ppermute(x, 'seq', [(i, to(i)) for i in range(seq)])  60.9 us
    pallas_call x3, Pallas kernels, run_chunk(): pl.pallas_call(functools.partial(chunk_kernel, shifts, pairs, tile, out_t...  52.7 us
    ppermute x29, starting transfers between devices, moved(): return lax.ppermute(x, 'seq', [(i, to(i)) for i in range(seq)])  26.7 us
    pallas_call x2, Pallas kernels, weight_grad(): pl.pallas_call(functools.partial(weight_kernel, len(lefts), tile), grid=(...  24.2 us
    pallas_call x3, Pallas kernels, split_sum(): pl.pallas_call(functools.partial(split_kernel, shifts, pairs), out_shape=...  7.32 us
    unnamed x59, local copies, waits for them, and re-layouts  5.5 us
    pallas_call x1, Pallas kernels, local(): pl.pallas_call(finish_kernel, in_specs=[smem] + [vmem] * (4 + 2 * TYPES),...  4.29 us
    pallas_call x1, Pallas kernels, local(): pl.pallas_call(pack_kernel, in_specs=[smem] + [vmem] * 4, out_shape=[jax....  4.03 us
  transfers between devices with their start and end apart: 29, of which 7 were waited for; matrix products, arithmetic and copies ran while one was open for 2% of the time, Pallas kernels for 44%

profile of v1, /device:TPU:0, one launch (start us, length us, event | category | flops | bytes accessed | tf_op | source)
XLA Modules:
  0.0 190.5 jit_solution(7526315834098920963)
XLA Ops:
  2.0 4.0 %shard_map.93 = (bf16[72,3072]{1,0:T(8,128)(2,1)}, bf16[72,3072]{1,0:T(8,128)(2,1)}, bf16[72,3072]{1,0:T(8,128)(2,1)}, bf16[72,3072]{1,0:T(8,128)(2,1)}) custom-call(s32[1]{0:T(128)} %bitcast.plane_ref, bf16[128,3072]{1,0:T(8,128)(2,1)} %tokens_ref.3, bf16[128,3072]{1,0:T(8,128)(2,1)} %grad_ref.3, s32[128,1]{1,0:T(8,128)} %copy.11.type_ref, f32[4,3072]{1,0:T(4,128)} %gain_ref.3), custom_call_target="tpu_custom_call" | custom-call | tf_op jit(solution)/shard_map/pallas_call | solution.py:311
  6.1 5.0 %collective-permute-start.17 = (bf16[72,3072]{1,0:T(8,128)(2,1)}, bf16[72,3072]{1,0:T(8,128)(2,1)S(1)}, u32[]{:S(2)}, u32[]{:S(2)}) collective-permute-start(bf16[72,3072]{1,0:T(8,128)(2,1)} %get-tuple-element.48), channel_id=1, source_target_pairs={{0,12},{1,13},{2,14},{3,15},{4,0},{5,1},{6,2},{7,3},{8,4},{9,5},{1... | collective-permute-start | bytes 1327112 | tf_op jit(solution)/shard_map/ppermute | solution.py:298
  12.1 1.5 collective-permute-start
  13.6 8.4 %collective-permute-done.17.refs_0_ = bf16[72,3072]{1,0:T(8,128)(2,1)S(1)} collective-permute-done((bf16[72,3072]{1,0:T(8,128)(2,1)}, bf16[72,3072]{1,0:T(8,128)(2,1)S(1)}, u32[]{:S(2)}, u32[]{:S(2)}) %collective-permute-start.17) | collective-permute-done | bytes 442400 | tf_op jit(solution)/shard_map/ppermute | solution.py:298
  22.0 1.5 collective-permute-start.18
  23.6 25.5 %collective-permute-done.10.refs_0_ = bf16[72,3072]{1,0:T(8,128)(2,1)S(1)} collective-permute-done((bf16[72,3072]{1,0:T(8,128)(2,1)}, bf16[72,3072]{1,0:T(8,128)(2,1)S(1)}, u32[]{:S(2)}, u32[]{:S(2)}) %collective-permute-start.10) | collective-permute-done | bytes 442400 | tf_op jit(solution)/shard_map/ppermute | solution.py:298
  49.1 1.5 collective-permute-start.11
  51.7 10.5 %collective-permute-done.11.refs_1_ = bf16[72,3072]{1,0:T(8,128)(2,1)S(1)} collective-permute-done((bf16[72,3072]{1,0:T(8,128)(2,1)S(1)}, bf16[72,3072]{1,0:T(8,128)(2,1)S(1)}, u32[]{:S(2)}, u32[]{:S(2)}) %collective-permute-start.11) | collective-permute-done | bytes 442400 | tf_op jit(solution)/shard_map/ppermute | solution.py:298
  62.2 7.4 %collective-permute-done.2.refs_3_ = bf16[72,3072]{1,0:T(8,128)(2,1)S(1)} collective-permute-done((bf16[72,3072]{1,0:T(8,128)(2,1)S(1)}, bf16[72,3072]{1,0:T(8,128)(2,1)S(1)}, u32[]{:S(2)}, u32[]{:S(2)}) %collective-permute-start.2) | collective-permute-done | bytes 442400 | tf_op jit(solution)/shard_map/ppermute | solution.py:298
  71.0 16.7 %shard_map.98 = (f32[72,3072]{1,0:T(8,128)}, bf16[72,3072]{1,0:T(8,128)(2,1)}, bf16[144,3072]{1,0:T(8,128)(2,1)}, bf16[144,3072]{1,0:T(8,128)(2,1)}, bf16[144,15...) custom-call(bf16[72,3072]{1,0:T(8,128)(2,1)} %copy-done.2, bf16[72,3072]{1,0:T(8,128)(2,1)} %copy-done.4, ...), custom_call_target="tpu_custom_call" | custom-call | flops 4076863488 | bytes 18874368 | tf_op jit(solution)/shard_map/pallas_call | solution.py:205
  88.5 16.8 %shard_map.96 = (f32[72,3072]{1,0:T(8,128)}, bf16[72,3072]{1,0:T(8,128)(2,1)}, bf16[144,3072]{1,0:T(8,128)(2,1)}, bf16[144,3072]{1,0:T(8,128)(2,1)}, bf16[144,15...) custom-call(bf16[72,3072]{1,0:T(8,128)(2,1)} %copy-done.1, bf16[72,3072]{1,0:T(8,128)(2,1)} %copy-done.3, ...), custom_call_target="tpu_custom_call" | custom-call | flops 4076863488 | bytes 18874368 | tf_op jit(solution)/shard_map/pallas_call | solution.py:205
  107.2 19.2 %shard_map.94 = (f32[144,3072]{1,0:T(8,128)}, bf16[144,3072]{1,0:T(8,128)(2,1)}, bf16[288,3072]{1,0:T(8,128)(2,1)}, bf16[288,3072]{1,0:T(8,128)(2,1)}, bf16[288,...) custom-call(bf16[72,3072]{1,0:T(8,128)(2,1)} %get-tuple-element.37.refs_0_, ...), custom_call_target="tpu_custom_call" | custom-call | flops 8153726976 | bytes 18874368 | tf_op jit(solution)/shard_map/pallas_call | solution.py:205
  128.5 1.6 collective-permute-start.25
  130.8 2.2 %shard_map.99 = (f32[72,1536]{1,0:T(8,128)}, bf16[72,1536]{1,0:T(8,128)(2,1)}) custom-call(f32[72,3072]{1,0:T(8,128)} %get-tuple-element.49.keep_ref, bf16[72,3072]{1,0:T(8,128)(2,1)} %copy-done.10), custom_call_target="tpu_custom_call" | custom-call | tf_op jit(solution)/shard_map/pallas_call | solution.py:251
  133.6 12.1 %shard_map.101 = bf16[3072,1536]{1,0:T(8,128)(2,1)} custom-call(bf16[288,3072]{1,0:T(8,128)(2,1)} %get-tuple-element.58.refs_0_, bf16[144,3072]{1,0:T(8,128)(2,1)} %get-tuple-element.59.refs_1_, bf16[144,3072]{1,0:T(8,128)(2,1)} %get-tuple-element.60.refs_2_, bf16[288,1536]{1,0:T(8,128)(2,1)} %get-tuple-element.61.refs_3_, ...), custom_call_target="tpu_custom_call" | custom-call | flops 5435817984 | bytes 9437184 | tf_op jit(solution)/shard_map/pallas_call | solution.py:277
  145.8 2.0 %collective-permute-start.26 = (f32[1,3072]{1,0:T(1,128)S(1)}, f32[1,3072]{1,0:T(1,128)S(1)}, u32[]{:S(2)}, u32[]{:S(2)}) collective-permute-start(f32[1,3072]{1,0:T(1,128)S(1)} %add.28.refs_4_), channel_id=1, source_target_pairs={{0,4},{1,5},{2,6},{3,7},{4,8},{5,9},{6,10},{7,11},{8,12},{9,13},{1... | collective-permute-start | bytes 36872 | tf_op jit(solution)/shard_map/ppermute | solution.py:298
  147.8 2.2 %shard_map.97 = (f32[72,1536]{1,0:T(8,128)}, bf16[72,1536]{1,0:T(8,128)(2,1)}) custom-call(f32[72,3072]{1,0:T(8,128)} %get-tuple-element.44.keep_ref, bf16[72,3072]{1,0:T(8,128)(2,1)} %copy-done.11), custom_call_target="tpu_custom_call" | custom-call | tf_op jit(solution)/shard_map/pallas_call | solution.py:251
  151.6 1.5 collective-permute-start.23
  153.1 2.9 %shard_map.95 = (f32[144,1536]{1,0:T(8,128)}, bf16[144,1536]{1,0:T(8,128)(2,1)}) custom-call(f32[144,3072]{1,0:T(8,128)} %get-tuple-element.39.keep_ref, bf16[144,3072]{1,0:T(8,128)(2,1)} %copy-done), custom_call_target="tpu_custom_call" | custom-call | tf_op jit(solution)/shard_map/pallas_call | solution.py:251
  159.4 8.0 %collective-permute-done.8 = bf16[144,1536]{1,0:T(8,128)(2,1)S(1)} collective-permute-done((bf16[144,1536]{1,0:T(8,128)(2,1)}, bf16[144,1536]{1,0:T(8,128)(2,1)S(1)}, u32[]{:S(2)}, u32[]{:S(2)}) %collective-permute-start.8) | collective-permute-done | bytes 442400 | tf_op jit(solution)/shard_map/ppermute | solution.py:298
  167.4 2.3 %collective-permute-start.16 = (bf16[72,1536]{1,0:T(8,128)(2,1)S(1)}, bf16[72,1536]{1,0:T(8,128)(2,1)S(1)}, u32[]{:S(2)}, u32[]{:S(2)}) collective-permute-start(bf16[72,1536]{1,0:T(8,128)(2,1)S(1)} %add_convert_fusion.2), channel_id=1, source_target_pairs={{0,8},{1,9},{2,10},{3,11},{4,12},{5,13},{6,14},{7,15},{8,0},{9,1},... | collective-permute-start | bytes 663560 | tf_op jit(solution)/shard_map/ppermute | solution.py:298
  171.6 1.5 collective-permute-start.9
  173.2 12.2 %shard_map.102 = bf16[1536,3072]{1,0:T(8,128)(2,1)} custom-call(bf16[288,1536]{1,0:T(8,128)(2,1)} %get-tuple-element.64.refs_0_, bf16[144,1536]{1,0:T(8,128)(2,1)} %get-tuple-element.65.refs_1_, bf16[144,1536]{1,0:T(8,128)(2,1)} %get-tuple-element.66.refs_2_, bf16[288,3072]{1,0:T(8,128)(2,1)} %get-tuple-element.67.refs_3_, ...), custom_call_target="tpu_custom_call" | custom-call | flops 5435817984 | bytes 9437184 | tf_op jit(solution)/shard_map/pallas_call | solution.py:277
  186.3 4.3 %shard_map.100 = (bf16[128,3072]{1,0:T(8,128)(2,1)}, f32[4,3072]{1,0:T(4,128)}) custom-call(s32[1]{0:T(128)} %bitcast.plane_ref, bf16[128,3072]{1,0:T(8,128)(2,1)} %tokens_ref.3, bf16[128,3072]{1,0:T(8,128)(2,1)} %grad_ref.3, s32[128,1]{1,0:T(8,128)} %copy.11.type_ref, f32[4,3072]{1,0:T(4,128)} %gain_ref.3, bf16[72,1536]{1,0:T(8,128)(2,1)} %get-tuple-element.71.refs_0_, ...), custom_call_target="tpu_custom_call" | custom-call | tf_op jit(solution)/shard_map/pallas_call | solution.py:352
  (110 shorter events, 18.6 us)
Async XLA Ops:
  6.1 16.0 %collective-permute-start.17 = (bf16[72,3072]{1,0:T(8,128)(2,1)}, bf16[72,3072]{1,0:T(8,128)(2,1)S(1)}, u32[]{:S(2)}, u32[]{:S(2)}) collective-permute-start(bf16[72,3072]{1,0:T(8,128)(2,1)} %get-tuple-element.48), channel_id=1, source_target_pairs={{0,12},{1,13},{2,14},{3,15},{4,0},{5,1},{6,2},{7,3},{8,4},{9,5},{1... | collective-permute-start | bytes 1327112 | tf_op jit(solution)/shard_map/ppermute | solution.py:298
  11.1 38.0 %collective-permute-start.10 = (bf16[72,3072]{1,0:T(8,128)(2,1)}, bf16[72,3072]{1,0:T(8,128)(2,1)S(1)}, u32[]{:S(2)}, u32[]{:S(2)}) collective-permute-start(bf16[72,3072]{1,0:T(8,128)(2,1)} %get-tuple-element.43), channel_id=1, source_target_pairs={{0,8},{1,9},{2,10},{3,11},{4,12},{5,13},{6,14},{7,15},{8,0},{9,1},... | collective-permute-start | bytes 1327112 | tf_op jit(solution)/shard_map/ppermute | solution.py:298
  11.1 39.5 %collective-permute-start.1 = (bf16[72,3072]{1,0:T(8,128)(2,1)}, bf16[72,3072]{1,0:T(8,128)(2,1)S(1)}, u32[]{:S(2)}, u32[]{:S(2)}) collective-permute-start(bf16[72,3072]{1,0:T(8,128)(2,1)} %get-tuple-element.38), channel_id=1, source_target_pairs={{0,4},{1,5},{2,6},{3,7},{4,8},{5,9},{6,10},{7,11},{8,12},{9,13},{1... | collective-permute-start | bytes 1327112 | tf_op jit(solution)/shard_map/ppermute | solution.py:298
  12.1 39.0 %collective-permute-start = (bf16[72,3072]{1,0:T(8,128)(2,1)}, bf16[72,3072]{1,0:T(8,128)(2,1)S(1)}, u32[]{:S(2)}, u32[]{:S(2)}) collective-permute-start(bf16[72,3072]{1,0:T(8,128)(2,1)} %get-tuple-element.37.refs_0_), channel_id=1, source_target_pairs={{0,2},{1,3},{2,0},{3,1},{4,6},{5,7},{6,4},{7,5},{8,10},{9,11},{10,... | collective-permute-start | bytes 1327112 | tf_op jit(solution)/shard_map/ppermute | solution.py:298
  22.0 29.6 %collective-permute-start.18 = (bf16[72,3072]{1,0:T(8,128)(2,1)S(1)}, bf16[72,3072]{1,0:T(8,128)(2,1)S(1)}, u32[]{:S(2)}, u32[]{:S(2)}) collective-permute-start(bf16[72,3072]{1,0:T(8,128)(2,1)S(1)} %collective-permute-done.17.refs_0_), channel_id=1, source_target_pairs={{0,2},{1,3},{2,0},{3,1},{4,6},{5,7},{6,4},{7,5},{8,10},{9,11},{10,... | collective-permute-start | bytes 1327112 | tf_op jit(solution)/shard_map/ppermute | solution.py:298
  50.6 19.0 %collective-permute-start.2 = (bf16[72,3072]{1,0:T(8,128)(2,1)S(1)}, bf16[72,3072]{1,0:T(8,128)(2,1)S(1)}, u32[]{:S(2)}, u32[]{:S(2)}) collective-permute-start(bf16[72,3072]{1,0:T(8,128)(2,1)S(1)} %collective-permute-done.1.refs_2_), channel_id=1, source_target_pairs={{0,2},{1,3},{2,0},{3,1},{4,6},{5,7},{6,4},{7,5},{8,10},{9,11},{10,... | collective-permute-start | bytes 1327112 | tf_op jit(solution)/shard_map/ppermute | solution.py:298
  51.1 18.5 %collective-permute-start.12 = (bf16[72,3072]{1,0:T(8,128)(2,1)S(1)}, bf16[72,3072]{1,0:T(8,128)(2,1)S(1)}, u32[]{:S(2)}, u32[]{:S(2)}) collective-permute-start(bf16[72,3072]{1,0:T(8,128)(2,1)S(1)} %collective-permute-done.10.refs_0_), channel_id=1, source_target_pairs={{0,1},{1,0},{2,3},{3,2},{4,5},{5,4},{6,7},{7,6},{8,9},{9,8},{10,11... | collective-permute-start | bytes 1327112 | tf_op jit(solution)/shard_map/ppermute | solution.py:298
  51.1 19.0 %collective-permute-start.19 = (bf16[72,3072]{1,0:T(8,128)(2,1)S(1)}, bf16[72,3072]{1,0:T(8,128)(2,1)S(1)}, u32[]{:S(2)}, u32[]{:S(2)}) collective-permute-start(bf16[72,3072]{1,0:T(8,128)(2,1)S(1)} %collective-permute-done.17.refs_0_), channel_id=1, source_target_pairs={{0,1},{1,0},{2,3},{3,2},{4,5},{5,4},{6,7},{7,6},{8,9},{9,8},{10,11... | collective-permute-start | bytes 1327112 | tf_op jit(solution)/shard_map/ppermute | solution.py:298
  51.6 18.6 %collective-permute-start.20 = (bf16[72,3072]{1,0:T(8,128)(2,1)S(1)}, bf16[72,3072]{1,0:T(8,128)(2,1)S(1)}, u32[]{:S(2)}, u32[]{:S(2)}) collective-permute-start(bf16[72,3072]{1,0:T(8,128)(2,1)S(1)} %collective-permute-done.18.refs_1_), channel_id=1, source_target_pairs={{0,1},{1,0},{2,3},{3,2},{4,5},{5,4},{6,7},{7,6},{8,9},{9,8},{10,11... | collective-permute-start | bytes 1327112 | tf_op jit(solution)/shard_map/ppermute | solution.py:298
  62.2 25.6 %collective-permute-start.13 = (bf16[72,3072]{1,0:T(8,128)(2,1)S(1)}, bf16[72,3072]{1,0:T(8,128)(2,1)S(1)}, u32[]{:S(2)}, u32[]{:S(2)}) collective-permute-start(bf16[72,3072]{1,0:T(8,128)(2,1)S(1)} %collective-permute-done.11.refs_1_), channel_id=1, source_target_pairs={{0,1},{1,0},{2,3},{3,2},{4,5},{5,4},{6,7},{7,6},{8,9},{9,8},{10,11... | collective-permute-start | bytes 1327112 | tf_op jit(solution)/shard_map/ppermute | solution.py:298
  69.6 35.8 %collective-permute-start.3 = (bf16[72,3072]{1,0:T(8,128)(2,1)}, bf16[72,3072]{1,0:T(8,128)(2,1)S(1)}, u32[]{:S(2)}, u32[]{:S(2)}) collective-permute-start(bf16[72,3072]{1,0:T(8,128)(2,1)} %get-tuple-element.37.refs_0_), channel_id=1, source_target_pairs={{0,1},{1,0},{2,3},{3,2},{4,5},{5,4},{6,7},{7,6},{8,9},{9,8},{10,11... | collective-permute-start | bytes 1327112 | tf_op jit(solution)/shard_map/ppermute | solution.py:298
  69.6 35.8 %collective-permute-start.5 = (bf16[72,3072]{1,0:T(8,128)(2,1)S(1)}, bf16[72,3072]{1,0:T(8,128)(2,1)S(1)}, u32[]{:S(2)}, u32[]{:S(2)}) collective-permute-start(bf16[72,3072]{1,0:T(8,128)(2,1)S(1)} %collective-permute-done.1.refs_2_), channel_id=1, source_target_pairs={{0,1},{1,0},{2,3},{3,2},{4,5},{5,4},{6,7},{7,6},{8,9},{9,8},{10,11... | collective-permute-start | bytes 1327112 | tf_op jit(solution)/shard_map/ppermute | solution.py:298
  70.1 35.3 %collective-permute-start.4 = (bf16[72,3072]{1,0:T(8,128)(2,1)S(1)}, bf16[72,3072]{1,0:T(8,128)(2,1)S(1)}, u32[]{:S(2)}, u32[]{:S(2)}) collective-permute-start(bf16[72,3072]{1,0:T(8,128)(2,1)S(1)} %collective-permute-done.refs_1_), channel_id=1, source_target_pairs={{0,1},{1,0},{2,3},{3,2},{4,5},{5,4},{6,7},{7,6},{8,9},{9,8},{10,11... | collective-permute-start | bytes 1327112 | tf_op jit(solution)/shard_map/ppermute | solution.py:298
  70.2 35.2 %collective-permute-start.6 = (bf16[72,3072]{1,0:T(8,128)(2,1)S(1)}, bf16[72,3072]{1,0:T(8,128)(2,1)S(1)}, u32[]{:S(2)}, u32[]{:S(2)}) collective-permute-start(bf16[72,3072]{1,0:T(8,128)(2,1)S(1)} %collective-permute-done.2.refs_3_), channel_id=1, source_target_pairs={{0,1},{1,0},{2,3},{3,2},{4,5},{5,4},{6,7},{7,6},{8,9},{9,8},{10,11... | collective-permute-start | bytes 1327112 | tf_op jit(solution)/shard_map/ppermute | solution.py:298
  87.8 42.3 %collective-permute-start.21 = (bf16[72,3072]{1,0:T(8,128)(2,1)}, bf16[72,3072]{1,0:T(8,128)(2,1)S(1)}, u32[]{:S(2)}, u32[]{:S(2)}) collective-permute-start(bf16[72,3072]{1,0:T(8,128)(2,1)} %get-tuple-element.50), channel_id=1, source_target_pairs={{0,1},{1,0},{2,3},{3,2},{4,5},{5,4},{6,7},{7,6},{8,9},{9,8},{10,11... | collective-permute-start | bytes 1327112 | tf_op jit(solution)/shard_map/ppermute | solution.py:298
  127.6 18.2 %collective-permute-start.14 = (bf16[72,3072]{1,0:T(8,128)(2,1)S(1)}, bf16[72,3072]{1,0:T(8,128)(2,1)S(1)}, u32[]{:S(2)}, u32[]{:S(2)}) collective-permute-start(bf16[72,3072]{1,0:T(8,128)(2,1)S(1)} %copy-done.24), channel_id=1, source_target_pairs={{0,1},{1,0},{2,3},{3,2},{4,5},{5,4},{6,7},{7,6},{8,9},{9,8},{10,11... | collective-permute-start | bytes 1327112 | tf_op jit(solution)/shard_map/ppermute | solution.py:298
  127.8 23.8 %collective-permute-start.7 = (bf16[144,3072]{1,0:T(8,128)(2,1)}, bf16[144,3072]{1,0:T(8,128)(2,1)S(1)}, u32[]{:S(2)}, u32[]{:S(2)}) collective-permute-start(bf16[144,3072]{1,0:T(8,128)(2,1)} %get-tuple-element.40), channel_id=1, source_target_pairs={{0,1},{1,0},{2,3},{3,2},{4,5},{5,4},{6,7},{7,6},{8,9},{9,8},{10,11... | collective-permute-start | bytes 2654216 | tf_op jit(solution)/shard_map/ppermute | solution.py:298
  128.5 17.1 %collective-permute-start.25 = (f32[1,3072]{1,0:T(1,128)S(1)}, f32[1,3072]{1,0:T(1,128)S(1)}, u32[]{:S(2)}, u32[]{:S(2)}) collective-permute-start(f32[1,3072]{1,0:T(1,128)S(1)} %add.27), channel_id=1, source_target_pairs={{0,2},{1,3},{2,0},{3,1},{4,6},{5,7},{6,4},{7,5},{8,10},{9,11},{10,... | collective-permute-start | bytes 36872 | tf_op jit(solution)/shard_map/ppermute | solution.py:298
  133.0 17.0 %collective-permute-start.22 = (bf16[72,1536]{1,0:T(8,128)(2,1)}, bf16[72,1536]{1,0:T(8,128)(2,1)S(1)}, u32[]{:S(2)}, u32[]{:S(2)}) collective-permute-start(bf16[72,1536]{1,0:T(8,128)(2,1)} %get-tuple-element.52), channel_id=1, source_target_pairs={{0,2},{1,3},{2,0},{3,1},{4,6},{5,7},{6,4},{7,5},{8,10},{9,11},{10,... | collective-permute-start | bytes 663560 | tf_op jit(solution)/shard_map/ppermute | solution.py:298
  145.6 26.0 %collective-permute-start.28 = (f32[1,3072]{1,0:T(1,128)S(1)}, f32[1,3072]{1,0:T(1,128)S(1)}, u32[]{:S(2)}, u32[]{:S(2)}) collective-permute-start(f32[1,3072]{1,0:T(1,128)S(1)} %add.28.refs_4_), channel_id=1, source_target_pairs={{0,12},{1,13},{2,14},{3,15},{4,0},{5,1},{6,2},{7,3},{8,4},{9,5},{1... | collective-permute-start | bytes 36872 | tf_op jit(solution)/shard_map/ppermute | solution.py:298
  145.7 39.6 %collective-permute-start.27 = (f32[1,3072]{1,0:T(1,128)S(1)}, f32[1,3072]{1,0:T(1,128)S(1)}, u32[]{:S(2)}, u32[]{:S(2)}) collective-permute-start(f32[1,3072]{1,0:T(1,128)S(1)} %add.28.refs_4_), channel_id=1, source_target_pairs={{0,8},{1,9},{2,10},{3,11},{4,12},{5,13},{6,14},{7,15},{8,0},{9,1},... | collective-permute-start | bytes 36872 | tf_op jit(solution)/shard_map/ppermute | solution.py:298
  145.8 39.6 %collective-permute-start.26 = (f32[1,3072]{1,0:T(1,128)S(1)}, f32[1,3072]{1,0:T(1,128)S(1)}, u32[]{:S(2)}, u32[]{:S(2)}) collective-permute-start(f32[1,3072]{1,0:T(1,128)S(1)} %add.28.refs_4_), channel_id=1, source_target_pairs={{0,4},{1,5},{2,6},{3,7},{4,8},{5,9},{6,10},{7,11},{8,12},{9,13},{1... | collective-permute-start | bytes 36872 | tf_op jit(solution)/shard_map/ppermute | solution.py:298
  151.6 33.8 %collective-permute-start.23 = (bf16[72,1536]{1,0:T(8,128)(2,1)S(1)}, bf16[72,1536]{1,0:T(8,128)(2,1)S(1)}, u32[]{:S(2)}, u32[]{:S(2)}) collective-permute-start(bf16[72,1536]{1,0:T(8,128)(2,1)S(1)} %add_convert_fusion.1), channel_id=1, source_target_pairs={{0,4},{1,5},{2,6},{3,7},{4,8},{5,9},{6,10},{7,11},{8,12},{9,13},{1... | collective-permute-start | bytes 663560 | tf_op jit(solution)/shard_map/ppermute | solution.py:298
  167.4 18.0 %collective-permute-start.16 = (bf16[72,1536]{1,0:T(8,128)(2,1)S(1)}, bf16[72,1536]{1,0:T(8,128)(2,1)S(1)}, u32[]{:S(2)}, u32[]{:S(2)}) collective-permute-start(bf16[72,1536]{1,0:T(8,128)(2,1)S(1)} %add_convert_fusion.2), channel_id=1, source_target_pairs={{0,8},{1,9},{2,10},{3,11},{4,12},{5,13},{6,14},{7,15},{8,0},{9,1},... | collective-permute-start | bytes 663560 | tf_op jit(solution)/shard_map/ppermute | solution.py:298
  (34 other events, 490.2 us)

commit v2 on v1

v2 whole, which is shorter than its diff:
```python
import functools

import jax
import jax.numpy as jnp
from jax import lax
from jax.experimental import pallas as pl
from jax.experimental.pallas import tpu as pltpu
from jax.sharding import PartitionSpec as P

TYPES = 4
CAP = 36
MAIN = 32
TAIL = CAP - MAIN
HALF = 2 * CAP
PAIR = 2 * HALF
EPS = 1e-06
CORES = 2

F32 = jnp.float32
BF16 = jnp.bfloat16
VMEM_LIMIT = 8 << 20
FORWARD_TILE = 512
HASTE = 100000
TILES_FIRST = 2
NT = (((1,), (1,)), ((), ()))
TN = (((0,), (0,)), ((), ()))
HBM = pl.BlockSpec(memory_space=pltpu.HBM)
VMEM = pl.BlockSpec(memory_space=pltpu.VMEM)
SMEM = pl.BlockSpec(memory_space=pltpu.SMEM)


def params(rows=0):
    return pltpu.CompilerParams(vmem_limit_bytes=VMEM_LIMIT + rows * 40 * 1024)


def cost(flops, moved):
    return pl.CostEstimate(flops=int(flops) // HASTE, bytes_accessed=int(moved) // HASTE, transcendentals=0)


def sum_kernel(count, *refs):
    refs[-1][...] = sum(ref[...] for ref in refs[:count])


def summed(parts, after):
    return pl.pallas_call(
        functools.partial(sum_kernel, len(parts)),
        in_specs=[VMEM] * len(parts) + [HBM] * len(after),
        out_specs=VMEM,
        out_shape=jax.ShapeDtypeStruct(parts[0].shape, F32),
        compiler_params=params(),
    )(*parts, *after)


def token_terms(tokens_ref, type_ref, gain_ref):
    tok = tokens_ref[...].astype(F32)
    inverse = lax.rsqrt(jnp.mean(tok * tok, axis=1, keepdims=True) + EPS)
    types = type_ref[...]
    gain_rows = jnp.zeros_like(tok)
    for k in range(TYPES):
        gain_rows = jnp.where(types == k, gain_ref[k : k + 1, :], gain_rows)
    rows = tok.shape[0]
    lanes = lax.broadcasted_iota(jnp.int32, (rows, 128), 1)
    onehot = jnp.where(lanes == types, 1.0, 0.0)
    below = lax.broadcasted_iota(jnp.int32, (rows, rows), 1)
    above = lax.broadcasted_iota(jnp.int32, (rows, rows), 0)
    earlier = jnp.where(below < above, 1.0, 0.0).astype(BF16)
    running = jnp.dot(earlier, onehot.astype(BF16), preferred_element_type=F32)
    rank = jnp.sum(running * onehot, axis=1, keepdims=True).astype(jnp.int32)
    return tok, inverse, types, gain_rows, rank


def wide_mod(value):
    return jnp.where(value >= TYPES, value - TYPES, value)


def slots(lane):
    in_tail = lane >= 2 * MAIN
    left = jnp.where(lane < MAIN, lane, jnp.where(in_tail & (lane < 2 * MAIN + TAIL), lane - MAIN, -1))
    right = jnp.where(
        (lane >= MAIN) & ~in_tail, lane - MAIN, jnp.where(lane >= 2 * MAIN + TAIL, lane - CAP, -1)
    )
    return left, right


def pack_kernel(plane_ref, tokens_ref, grad_ref, type_ref, gain_ref, *outs):
    tok, inverse, types, gain_rows, rank = token_terms(tokens_ref, type_ref, gain_ref)
    rows, width = tok.shape
    half = width // 2
    normed = (tok * inverse * gain_rows).astype(BF16)
    grad = grad_ref[...]
    both_n = jnp.concatenate([normed[:, :half], normed[:, half:]], axis=0)
    both_g = jnp.concatenate([grad[:, :half], grad[:, half:]], axis=0)
    slot_l, slot_r = slots(lax.broadcasted_iota(jnp.int32, (rows, HALF), 1))
    for shift, out in enumerate(outs):
        here = types == wide_mod(plane_ref[0] + shift)
        pick_l = jnp.where(here & (rank == slot_l), 1.0, 0.0)
        pick_r = jnp.where(here & (rank == slot_r), 1.0, 0.0)
        pick = jnp.concatenate([pick_l, pick_r], axis=0).astype(BF16)
        out_n = lax.dot_general(pick, both_n, TN, preferred_element_type=F32)
        out_g = lax.dot_general(pick, both_g, TN, preferred_element_type=F32)
        out[...] = jnp.concatenate(
            [out_n[: 2 * MAIN], out_g[: 2 * MAIN], out_n[2 * MAIN :], out_g[2 * MAIN :]], axis=0
        ).astype(BF16)


def finish_kernel(plane_ref, tokens_ref, grad_ref, type_ref, gain_ref, *refs):
    returned = refs[:TYPES]
    gains = refs[TYPES : 2 * TYPES]
    out, gain_out = refs[2 * TYPES :]
    tok, inverse, types, gain_rows, rank = token_terms(tokens_ref, type_ref, gain_ref)
    rows, width = tok.shape
    slot_l, slot_r = slots(lax.broadcasted_iota(jnp.int32, (rows, HALF), 1))
    left = jnp.zeros((rows, width // 2), F32)
    right = jnp.zeros((rows, width // 2), F32)
    for shift in range(TYPES):
        here = types == wide_mod(plane_ref[0] + shift)
        block = returned[shift][...]
        pick_l = jnp.where(here & (rank == slot_l), 1.0, 0.0).astype(BF16)
        pick_r = jnp.where(here & (rank == slot_r), 1.0, 0.0).astype(BF16)
        left += jnp.dot(pick_l, block, preferred_element_type=F32)
        right += jnp.dot(pick_r, block, preferred_element_type=F32)
    scaled = jnp.concatenate([left, right], axis=1) * gain_rows
    inner = jnp.sum(scaled * tok, axis=1, keepdims=True)
    branch = scaled * inverse - tok * (inner * inverse * inverse * inverse / width)
    out[...] = (grad_ref[...].astype(F32) + branch).astype(BF16)
    row = lax.broadcasted_iota(jnp.int32, (TYPES, width), 0)
    total = jnp.zeros((TYPES, width), F32)
    for shift in range(TYPES):
        kind = wide_mod(plane_ref[0] + TYPES - shift)
        total = jnp.where(row == kind, gains[shift][...], total)
    gain_out[...] = total / gain_ref[...]


def pass_kernel(*refs):
    pass


def gated(value, after):
    return pl.pallas_call(
        pass_kernel,
        in_specs=[HBM] * (1 + len(after)),
        out_specs=HBM,
        out_shape=jax.ShapeDtypeStruct(value.shape, value.dtype),
        input_output_aliases={0: 0},
        compiler_params=params(),
    )(value, *after)


def warm_kernel(up, down, after, out):
    out[...] = jnp.zeros_like(out)


def warmed(up, down, after):
    return pl.pallas_call(
        warm_kernel,
        in_specs=[VMEM] * 2 + [HBM],
        out_specs=VMEM,
        out_shape=jax.ShapeDtypeStruct((8, 128), F32),
        compiler_params=params(),
        cost_estimate=cost(8e9, 8),
    )(up, down, after)


def assemble(blk, normed, grads):
    count, half = blk.shape[0], blk.shape[2]
    low = lax.broadcasted_iota(jnp.int32, (8, half), 0) < TAIL
    for i in range(count):
        into = slice(i * MAIN, (i + 1) * MAIN)
        normed[into, :half] = blk[i, 0:MAIN, :]
        normed[into, half:] = blk[i, MAIN : 2 * MAIN, :]
        grads[into, :half] = blk[i, 2 * MAIN : 3 * MAIN, :]
        grads[into, half:] = blk[i, 3 * MAIN : 4 * MAIN, :]
    tails_n, tails_g = [], []
    for i in range(0, count, 2):
        a = blk[i, 4 * MAIN :, :].astype(F32)
        b = blk[i + 1, 4 * MAIN :, :].astype(F32)
        for first, tails in ((0, tails_n), (8, tails_g)):
            u, v = a[first : first + 8], b[first : first + 8]
            left = jnp.where(low, u, pltpu.roll(v, TAIL, 0))
            right = jnp.where(low, pltpu.roll(u, TAIL, 0), v)
            tails.append(jnp.concatenate([left, right], axis=1))
    normed[count * MAIN :, :] = jnp.concatenate(tails_n, axis=0).astype(BF16)
    grads[count * MAIN :, :] = jnp.concatenate(tails_g, axis=0).astype(BF16)


def forward_kernel(blocks, tile, afters, *refs):
    ins = refs[:blocks]
    up, down = refs[blocks : blocks + 2]
    normed, grads, act, pre, blk, n_v, g_v, act_v, pre_v, in_sem, o_sem = refs[blocks + 2 + afters :]
    hidden = up.shape[1]
    in_copies = [pltpu.make_async_copy(ins[i], blk.at[i], in_sem.at[i]) for i in range(blocks)]
    for copy in in_copies:
        copy.start()
    for copy in in_copies:
        copy.wait()
    assemble(blk, n_v, g_v)
    n_copy = pltpu.make_async_copy(n_v, normed, o_sem.at[0])
    g_copy = pltpu.make_async_copy(g_v, grads, o_sem.at[1])
    for t in range(hidden // tile):
        cols = slice(t * tile, (t + 1) * tile)
        preact = jnp.dot(n_v[...], up[:, cols], preferred_element_type=F32)
        grad_act = lax.dot_general(g_v[...], down[cols, :], NT, preferred_element_type=F32)
        sig = jax.nn.sigmoid(preact)
        act_v[:, cols] = (preact * sig).astype(BF16)
        pre_v[:, cols] = (grad_act * (sig * (1.0 + preact * (1.0 - sig)))).astype(BF16)
        if t == 0:
            n_copy.start()
            g_copy.start()
    last = [
        pltpu.make_async_copy(pre_v, pre, o_sem.at[2]),
        pltpu.make_async_copy(act_v, act, o_sem.at[3]),
    ]
    for copy in last:
        copy.start()
    for copy in [n_copy, g_copy] + last:
        copy.wait()


def forward(blocks, up, down, after):
    width, hidden = up.shape
    rows = len(blocks) * CAP
    tile = FORWARD_TILE if hidden % FORWARD_TILE == 0 else hidden // 2
    shapes = [(rows, width), (rows, width), (rows, hidden), (rows, hidden)]
    return pl.pallas_call(
        functools.partial(forward_kernel, len(blocks), tile, len(after)),
        in_specs=[HBM] * len(blocks) + [VMEM] * 2 + [HBM] * len(after),
        out_specs=[HBM] * len(shapes),
        out_shape=[jax.ShapeDtypeStruct(s, BF16) for s in shapes],
        scratch_shapes=[
            pltpu.VMEM((len(blocks), PAIR, width // 2), BF16),
        ]
        + [pltpu.VMEM(s, BF16) for s in shapes]
        + [
            pltpu.SemaphoreType.DMA((len(blocks),)),
            pltpu.SemaphoreType.DMA((4,)),
        ],
        compiler_params=params(rows),
        cost_estimate=cost(4 * rows * width * hidden, 2 * width * hidden),
    )(*blocks, up, down, *after)


def backward_kernel(shifts, pairs, tile, afters, pre, up, normed, *refs):
    refs = refs[afters:]
    keeps, sends, gain = refs[:pairs], refs[pairs : 2 * pairs], refs[2 * pairs]
    pre_v, n_v, out_v, gain_v, tail_v, in_sem, o_sem = refs[2 * pairs + 1 :]
    width = up.shape[0]
    half = width // 2
    blocks = 2 * shifts * pairs
    sides = blocks // 2
    low = lax.broadcasted_iota(jnp.int32, (8, half), 0) < TAIL
    pre_copy = pltpu.make_async_copy(pre, pre_v, in_sem.at[0])
    pre_copy.start()
    n_copy = pltpu.make_async_copy(normed, n_v, in_sem.at[1])
    n_copy.start()
    pre_copy.wait()
    for t in range(width // tile):
        first = t * tile
        cols = slice(first, first + tile)
        dx = lax.dot_general(pre_v[...], up[cols, :], NT, preferred_element_type=F32)
        if t == 0:
            n_copy.wait()
        gain_v[:, cols] = jnp.sum(dx * n_v[:, cols].astype(F32), axis=0, keepdims=True)
        tail_v[:, cols] = dx[blocks * MAIN :]
        row = MAIN if first >= half else 0
        into = slice(first % half, first % half + tile)
        for number in range(blocks):
            side, at = number // sides, number % sides
            base = at // pairs * 2 * MAIN + row
            block = dx[number * MAIN : (number + 1) * MAIN].astype(BF16)
            out_v[side * pairs + at % pairs, base : base + MAIN, into] = block
    last = []
    for side in (1, 0):
        for j in reversed(range(pairs)):
            tails = []
            for shift in range(shifts):
                number = side * sides + shift * pairs + j
                tail = tail_v[number // 2 * 8 : number // 2 * 8 + 8, :]
                if number % 2 == 0:
                    joined = jnp.where(low, tail[:, :half], pltpu.roll(tail[:, half:], TAIL, 0))
                else:
                    joined = jnp.where(low, pltpu.roll(tail[:, :half], TAIL, 0), tail[:, half:])
                tails.append(joined)
            block = side * pairs + j
            out_v[block, shifts * 2 * MAIN :, :] = jnp.concatenate(tails, axis=0).astype(BF16)
            to = (sends if side else keeps)[j]
            last.append(pltpu.make_async_copy(out_v.at[block], to, o_sem.at[block]))
            last[-1].start()
    last.append(pltpu.make_async_copy(gain_v, gain, o_sem.at[2 * pairs]))
    last[-1].start()
    for copy in last:
        copy.wait()


def backward(pre, up, normed, shifts, pairs, after):
    width, hidden = up.shape
    rows = pre.shape[0]
    tile = min(512, width // 2)
    shape = (shifts * HALF, width // 2)
    outs = [jax.ShapeDtypeStruct(shape, BF16)] * (2 * pairs) + [jax.ShapeDtypeStruct((1, width), F32)]
    result = pl.pallas_call(
        functools.partial(backward_kernel, shifts, pairs, tile, len(after)),
        in_specs=[HBM, VMEM, HBM] + [HBM] * len(after),
        out_specs=[HBM] * len(outs),
        out_shape=outs,
        scratch_shapes=[
            pltpu.VMEM(pre.shape, BF16),
            pltpu.VMEM(normed.shape, BF16),
            pltpu.VMEM((2 * pairs,) + shape, BF16),
            pltpu.VMEM((1, width), F32),
            pltpu.VMEM((2 * shifts * pairs * TAIL, width), F32),
            pltpu.SemaphoreType.DMA((2,)),
            pltpu.SemaphoreType.DMA((len(outs),)),
        ],
        compiler_params=params(rows),
        cost_estimate=cost(2 * rows * width * hidden, 2 * width * hidden),
    )(pre, up, normed, *after)
    return result[:pairs], result[pairs : 2 * pairs], result[2 * pairs]


def merge_kernel(first_ref, second_ref, *refs):
    refs[-1][...] = (first_ref[...].astype(F32) + second_ref[...].astype(F32)).astype(BF16)


def merged(keep, got, after):
    return pl.pallas_call(
        merge_kernel,
        in_specs=[VMEM, VMEM] + [HBM] * len(after),
        out_specs=VMEM,
        out_shape=jax.ShapeDtypeStruct(keep.shape, BF16),
        compiler_params=params(),
    )(keep, got, *after)


def total_kernel(shifts, parts, *refs):
    outs = refs[-shifts:]
    total = refs[0][...].astype(F32)
    for part in refs[1:parts]:
        total = total + part[...].astype(F32)
    mains = shifts * 2 * MAIN
    for s, out in enumerate(outs):
        out[: 2 * MAIN] = total[s * 2 * MAIN : (s + 1) * 2 * MAIN].astype(BF16)
        out[2 * MAIN :] = total[mains + s * 2 * TAIL : mains + (s + 1) * 2 * TAIL].astype(BF16)


def totals(parts, shifts, after):
    return pl.pallas_call(
        functools.partial(total_kernel, shifts, len(parts)),
        in_specs=[VMEM] * len(parts) + [HBM] * len(after),
        out_specs=[VMEM] * shifts,
        out_shape=[jax.ShapeDtypeStruct((HALF, parts[0].shape[1]), BF16)] * shifts,
        compiler_params=params(),
    )(*parts, *after)


def weight_kernel(count, tile, *refs):
    lefts, rights, out, done = refs[:count], refs[count : 2 * count], refs[-3], refs[-2]
    stacked = refs[-1]

    @pl.when(pl.program_id(0) == 0)
    def _():
        first = 0
        for right in rights:
            stacked[first : first + right.shape[0], :] = right[...]
            first += right.shape[0]

    left = jnp.concatenate([ref[...] for ref in lefts], axis=0)
    out[...] = lax.dot_general(left, stacked[...], TN, preferred_element_type=F32).astype(BF16)
    done[...] = jnp.zeros_like(done)


def weight_grad(lefts, rights, after, first=0, count=None, into=None):
    rows = sum(x.shape[0] for x in lefts)
    long, wide = lefts[0].shape[1], rights[0].shape[1]
    tile = min(512, long // 2)
    count = long // tile if count is None else count
    given = [] if into is None else [into]
    operands = [*lefts, *rights, *given, *after]
    return pl.pallas_call(
        functools.partial(weight_kernel, len(lefts), tile),
        grid=(count,),
        in_specs=[pl.BlockSpec((x.shape[0], tile), lambda j: (0, j + first)) for x in lefts]
        + [pl.BlockSpec(x.shape, lambda j: (0, 0)) for x in rights]
        + [HBM] * (len(given) + len(after)),
        out_specs=[pl.BlockSpec((tile, wide), lambda j: (j + first, 0)), pl.BlockSpec((8, 128), lambda j: (0, 0))],
        out_shape=[jax.ShapeDtypeStruct((long, wide), BF16), jax.ShapeDtypeStruct((8, 128), F32)],
        scratch_shapes=[pltpu.VMEM((rows, wide), BF16)],
        input_output_aliases={2 * len(lefts): 0} if given else {},
        compiler_params=params(rows // 2),
        cost_estimate=cost(2 * rows * tile * count * wide, 2 * tile * count * wide),
    )(*operands)


def local(tokens, grad_out, event_type, type_gain, up_weight, down_weight):
    seq = lax.axis_size("seq")
    owners = seq // TYPES
    pairs = owners // CORES
    width = tokens.shape[1]
    plane = (lax.axis_index("seq") // owners).astype(jnp.int32).reshape(1)

    def moved(x, to):
        return lax.ppermute(x, "seq", [(i, to(i)) for i in range(seq)])

    def to_plane(x, shift):
        return moved(x, lambda i: (i + shift * owners) % seq)

    def to_pair(x, shift):
        return moved(x, lambda i: i // owners * owners + (i % owners + CORES * shift) % owners)

    def to_core(x):
        return moved(x, lambda i: i ^ 1)

    packed = pl.pallas_call(
        pack_kernel,
        in_specs=[SMEM] + [VMEM] * 4,
        out_shape=[jax.ShapeDtypeStruct((PAIR, width // 2), BF16)] * TYPES,
        compiler_params=params(2 * tokens.shape[0]),
    )(plane, tokens, grad_out, event_type, type_gain)
    acts, pres, norms, grads, gain_parts, returned = [], [], [], [], [], {}

    def work(rows, cross, after):
        normed, grad, act, pre = forward(rows + cross, up_weight, down_weight, after)
        acts.append(act)
        pres.append(pre)
        norms.append(normed)
        grads.append(grad)
        return pre, normed

    def leave(pre, normed, shifts, after):
        keep, send, gain = backward(pre, up_weight, normed, shifts, pairs, after)
        gain_parts.append(gain)
        return keep, [to_core(x) for x in send[::-1]][::-1]

    def over_cores(kept, after):
        keep, got = kept
        sent = [merged(keep[j], got[j], after) for j in range(1, pairs)]
        return [keep[0], got[0]] + [to_pair(sent[j - 1], pairs - j) for j in range(1, pairs)], sent

    def over_planes(shifts, parts, after):
        sums = totals(parts, len(shifts), after)
        for shift, total in zip(shifts, sums):
            returned[shift] = to_plane(total, TYPES - shift) if shift else total
        return list(sums)[:1]

    def spread(x, after):
        row = [x] + [gated(to_pair(x, j), after) for j in range(1, pairs)]
        return row, [to_core(y) for y in row]

    one, two = to_plane(packed[1], 1), to_plane(packed[2], 2)
    warm = warmed(up_weight, down_weight, packed[0])
    row0, cross0 = spread(packed[0], [warm])
    row1, cross1 = spread(one, [warm])
    two = gated(two, [warm])
    last = gated(packed[3], [two])
    three = to_plane(last, 3)
    pre1, normed1 = work(row0 + row1, cross0 + cross1, [last])
    row2, cross2 = spread(two, [pre1])
    three = gated(three, [pre1])
    kept1 = leave(pre1, normed1, 2, row2[1:] + [three])
    pre2, normed2 = work(row2, cross2, [gain_parts[0]])
    row3, cross3 = spread(three, [pre2])
    parts1, sent1 = over_cores(kept1, [pre2])
    kept2 = leave(pre2, normed2, 1, row3[1:] + sent1)
    pre3, normed3 = work(row3, cross3, [gain_parts[1]])
    parts2, sent2 = over_cores(kept2, [pre3])
    total1 = over_planes((0, 1), parts1, [pre3])
    kept3 = leave(pre3, normed3, 1, sent2 + total1)
    total2 = over_planes((2,), parts2, [gain_parts[2]])
    gain = summed(gain_parts, total2)
    gain = [gain, to_core(gain)]
    tiles = max(2, width // 512)
    split = TILES_FIRST
    grad_up, done = weight_grad(norms, pres, total2 + [gain[0], returned[1]], 0, split)
    parts3, sent3 = over_cores(kept3, [done])
    gain = summed(gain, [done])
    gain = [gain] + [to_pair(gain, j) for j in range(1, pairs)]
    grad_up, done = weight_grad(norms, pres, sent3 + [gain[0]], split, tiles - split, grad_up)
    total3 = over_planes((3,), parts3, [done])
    gain = summed(gain, total3)
    gains = [gain] + [to_plane(gain, shift) for shift in range(1, TYPES)]
    grad_down, done = weight_grad(acts, grads, [gain, returned[2]])
    grad_tokens, grad_gain = pl.pallas_call(
        finish_kernel,
        in_specs=[SMEM] + [VMEM] * (4 + 2 * TYPES),
        out_shape=[
            jax.ShapeDtypeStruct(tokens.shape, BF16),
            jax.ShapeDtypeStruct((TYPES, width), F32),
        ],
        compiler_params=params(2 * tokens.shape[0]),
    )(plane, tokens, grad_out, event_type, type_gain, *[returned[shift] for shift in range(TYPES)], *gains)
    return (grad_tokens, grad_gain, grad_up, grad_down)


def solution(mesh):
    placed = (
        P(("groups", "seq"), None),
        P(("groups", "seq"), None),
        P(("groups", "seq"), None),
        P(),
        P(None, "seq"),
        P("seq", None),
    )
    return jax.shard_map(
        local,
        mesh=mesh,
        in_specs=placed,
        out_specs=(
            P(("groups", "seq"), None),
            P("groups", None),
            P("groups", "seq"),
            P(("groups", "seq"), None),
        ),
        check_vma=False,
    )
```

time: 191 us -> 136 us (0.71)
  waiting for transfers between devices: 60.9 us -> 25.8 us
  Pallas kernels: 92.6 us -> 64.6 us
  local copies, waits for them, and re-layouts: 6.22 us -> 14.9 us
  other arithmetic: 3.1 us -> 0 us
  starting transfers between devices: 26.7 us -> 28.9 us
    ppermute x29 -> x32, waiting for transfers between devices: 60.9 us -> 25.8 us  [moved(): return lax.ppermute(x, 'seq', [(i, to(i)) for i in range(seq)])]
    pallas_call x8 -> x25, Pallas kernels: 68.3 us -> 43.2 us  [the longest x3 22.9 us: forward(): pl.pallas_call(functools.partial(forward_kernel, len(blocks), tile, len(a...]
    unnamed x59 -> x23, local copies, waits for them, and re-layouts: 5.5 us -> 14.9 us
    pallas_call x2 -> x3, Pallas kernels: 24.2 us -> 21.4 us  [weight_grad(): pl.pallas_call(functools.partial(weight_kernel, len(lefts), tile), grid=(...]
    ppermute x29 -> x32, starting transfers between devices: 26.7 us -> 28.9 us  [moved(): return lax.ppermute(x, 'seq', [(i, to(i)) for i in range(seq)])]
  transfers between devices with their start and end apart: 29 -> 32, of which waited for: 7 -> 6; matrix products, arithmetic and copies ran while one was open for 2% -> 0% of each run, Pallas kernels for 44% -> 44%
where the time goes in v2:
time: 136 us; the launch traced here: 135 us
  Pallas kernels  64.6 us (47%)
  starting transfers between devices  28.9 us (21%)
  waiting for transfers between devices  25.8 us (19%)
  local copies, waits for them, and re-layouts  14.9 us (11%)
    ppermute x32, starting transfers between devices, moved(): return lax.ppermute(x, 'seq', [(i, to(i)) for i in range(seq)])  28.9 us
    ppermute x32, waiting for transfers between devices, moved(): return lax.ppermute(x, 'seq', [(i, to(i)) for i in range(seq)])  25.8 us
    pallas_call x3, Pallas kernels, forward(): pl.pallas_call(functools.partial(forward_kernel, len(blocks), tile, len(a...  22.9 us
    pallas_call x3, Pallas kernels, weight_grad(): pl.pallas_call(functools.partial(weight_kernel, len(lefts), tile), grid=(...  21.4 us
    pallas_call x3, Pallas kernels, backward(): pl.pallas_call(functools.partial(backward_kernel, shifts, pairs, tile, le...  15.1 us
    unnamed x23, local copies, waits for them, and re-layouts  14.9 us
  transfers between devices with their start and end apart: 32, of which 6 were waited for; matrix products, arithmetic and copies ran while one was open for 0% of the time, Pallas kernels for 44%

profile of v2, /device:TPU:0, one launch (start us, length us, event | category | flops | bytes accessed | tf_op | source)
XLA Modules:
  0.0 135.2 jit_solution(14544956320736961386)
XLA Ops:
  4.5 1.9 %shard_map.93 = (bf16[144,1536]{1,0:T(8,128)(2,1)S(1)}, bf16[144,1536]{1,0:T(8,128)(2,1)S(1)}, bf16[144,1536]{1,0:T(8,128)(2,1)S(1)}, bf16[144,1536]{1,0:T(8,128)(2,1)S(1)}) custom-call(s32[1]{0:T(128)} %bitcast.plane_ref, bf16[128,3072]{1,0:T(8,128)(2,1)S(1)} %copy-done.5, bf16[128,3072]{1,0:T(8,128)(2,1)S(1)} %copy-done.7, s32[128,1]{1,0:T(8,128)S(1)} %copy.19.type_ref, ...), custom_call_target="tpu_custom_call" | custom-call | tf_op jit(solution)/shard_map/pallas_call | solution.py:412
  6.4 3.1 %collective-permute-start.1 = (bf16[144,1536]{1,0:T(8,128)(2,1)S(1)}, bf16[144,1536]{1,0:T(8,128)(2,1)S(1)}, u32[]{:S(2)}, u32[]{:S(2)}) collective-permute-start(bf16[144,1536]{1,0:T(8,128)(2,1)S(1)} %get-tuple-element.45), channel_id=1, source_target_pairs={{0,4},{1,5},{2,6},{3,7},{4,8},{5,9},{6,10},{7,11},{8,12},{9,13},{1... | collective-permute-start | bytes 1327112 | tf_op jit(solution)/shard_map/ppermute | solution.py:401
  11.0 10.7 %collective-permute-done.1.refs_2_ = bf16[144,1536]{1,0:T(8,128)(2,1)S(1)} collective-permute-done((bf16[144,1536]{1,0:T(8,128)(2,1)S(1)}, bf16[144,1536]{1,0:T(8,128)(2,1)S(1)}, u32[]{:S(2)}, u32[]{:S(2)}) %collective-permute-start.1) | collective-permute-done | bytes 442400 | tf_op jit(solution)/shard_map/ppermute | solution.py:401
  23.9 3.7 %copy-done = bf16[3072,1536]{1,0:T(8,128)(2,1)S(1)} copy-done((bf16[3072,1536]{1,0:T(8,128)(2,1)S(1)}, bf16[3072,1536]{1,0:T(8,128)(2,1)}, u32[]{:S(2)}) %copy-start) | copy-done | bytes 9437208
  27.6 3.7 %copy-done.2 = bf16[1536,3072]{1,0:T(8,128)(2,1)S(1)} copy-done((bf16[1536,3072]{1,0:T(8,128)(2,1)S(1)}, bf16[1536,3072]{1,0:T(8,128)(2,1)}, u32[]{:S(2)}) %copy-start.2) | copy-done | bytes 9437208
  33.0 10.4 %collective-permute-done.7.refs_0_ = bf16[144,1536]{1,0:T(8,128)(2,1)S(1)} collective-permute-done((bf16[144,1536]{1,0:T(8,128)(2,1)S(1)}, bf16[144,1536]{1,0:T(8,128)(2,1)S(1)}, u32[]{:S(2)}, u32[]{:S(2)}) %collective-permute-start.7) | collective-permute-done | bytes 442400 | tf_op jit(solution)/shard_map/ppermute | solution.py:401
  44.0 2.5 %collective-permute-start.9 = (bf16[144,1536]{1,0:T(8,128)(2,1)S(1)}, bf16[144,1536]{1,0:T(8,128)(2,1)S(1)}, u32[]{:S(2)}, u32[]{:S(2)}) collective-permute-start(bf16[144,1536]{1,0:T(8,128)(2,1)S(1)} %shard_map.98.refs_10_), channel_id=1, source_target_pairs={{0,12},{1,13},{2,14},{3,15},{4,0},{5,1},{6,2},{7,3},{8,4},{9,5},{1... | collective-permute-start | bytes 1327112 | tf_op jit(solution)/shard_map/ppermute | solution.py:401
  46.5 9.3 %shard_map.99 = (bf16[288,3072]{1,0:T(8,128)(2,1)S(1)}, bf16[288,3072]{1,0:T(8,128)(2,1)S(1)}, bf16[288,1536]{1,0:T(8,128)(2,1)S(1)}, bf16[288,1536]{1,0:T(8,128)(2,1)S(1)}) custom-call(bf16[144,1536]{1,0:T(8,128)(2,1)S(1)} %get-tuple-element.44.after.refs_0_, bf16[144,1536]{1,0:T(8,128)(2,1)S(1)} %shard_map.95.refs_1_, ...), custom_call_target="tpu_custom_call" | custom-call | flops 54358 | bytes 94 | tf_op jit(solution)/shard_map/pallas_call | solution.py:224
  56.3 1.5 %collective-permute-start.15 = (bf16[144,1536]{1,0:T(8,128)(2,1)S(1)}, bf16[144,1536]{1,0:T(8,128)(2,1)S(1)}, u32[]{:S(2)}, u32[]{:S(2)}) collective-permute-start(bf16[144,1536]{1,0:T(8,128)(2,1)S(1)} %shard_map.101.refs_1_.refs_0_), channel_id=1, source_target_pairs={{0,2},{1,3},{2,0},{3,1},{4,6},{5,7},{6,4},{7,5},{8,10},{9,11},{10,... | collective-permute-start | bytes 1327112 | tf_op jit(solution)/shard_map/ppermute | solution.py:401
  57.9 4.8 %shard_map.102 = (bf16[144,1536]{1,0:T(8,128)(2,1)S(1)}, bf16[144,1536]{1,0:T(8,128)(2,1)S(1)}, bf16[144,1536]{1,0:T(8,128)(2,1)S(1)}, bf16[144,1536]{1,0:T(8,128)(2,1)S(1)}, f32[1,3072]{1,0:T(1,128)S(1)}) custom-call(bf16[288,1536]{1,0:T(8,128)(2,1)S(1)} %get-tuple-element.48.refs_1_.pre.refs_3_, bf16[3072,1536]{1,0:T(8,128)(2,1)S(1)} %copy-done.1, ...), custom_call_target="tpu_custom_call" | custom-call | flops 27179 | bytes 94 | tf_op jit(solution)/shard_map/pallas_call | solution.py:300
  63.3 3.7 %copy-done.4 = bf16[1536,3072]{1,0:T(8,128)(2,1)S(1)} copy-done((bf16[1536,3072]{1,0:T(8,128)(2,1)S(1)}, bf16[1536,3072]{1,0:T(8,128)(2,1)}, u32[]{:S(2)}) %copy-start.4) | copy-done | bytes 9437208
  67.0 6.8 %shard_map.103 = (bf16[144,3072]{1,0:T(8,128)(2,1)S(1)}, bf16[144,3072]{1,0:T(8,128)(2,1)S(1)}, bf16[144,1536]{1,0:T(8,128)(2,1)S(1)}, bf16[144,1536]{1,0:T(8,128)(2,1)S(1)}) custom-call(bf16[144,1536]{1,0:T(8,128)(2,1)S(1)} %shard_map.97.refs_1_.refs_0_, bf16[144,1536]{1,0:T(8,128)(2,1)S(1)} %shard_map.100.refs_0_.refs_1_, ...), custom_call_target="tpu_custom_call" | custom-call | flops 27179 | bytes 94 | tf_op jit(solution)/shard_map/pallas_call | solution.py:224
  75.1 5.2 %shard_map.106 = (bf16[72,1536]{1,0:T(8,128)(2,1)S(1)}, bf16[72,1536]{1,0:T(8,128)(2,1)S(1)}, bf16[72,1536]{1,0:T(8,128)(2,1)S(1)}, bf16[72,1536]{1,0:T(8,128)(2,1)S(1)}, f32[1,3072]{1,0:T(1,128)S(1)}) custom-call(bf16[144,1536]{1,0:T(8,128)(2,1)S(1)} %get-tuple-element.55.refs_0_.refs_1_.pre.refs_4_, bf16[3072,1536]{1,0:T(8,128)(2,1)S(1)} %copy-done.1, ...), custom_call_target="tpu_custom_call" | custom-call | flops 13589 | bytes 94 | tf_op jit(solution)/shard_map/pallas_call | solution.py:300
  81.0 6.8 %shard_map.107 = (bf16[144,3072]{1,0:T(8,128)(2,1)S(1)}, bf16[144,3072]{1,0:T(8,128)(2,1)S(1)}, bf16[144,1536]{1,0:T(8,128)(2,1)S(1)}, bf16[144,1536]{1,0:T(8,128)(2,1)S(1)}) custom-call(bf16[144,1536]{1,0:T(8,128)(2,1)S(1)} %shard_map.101.refs_1_.refs_0_, bf16[144,1536]{1,0:T(8,128)(2,1)S(1)} %shard_map.105.refs_0_.refs_1_, ...), custom_call_target="tpu_custom_call" | custom-call | flops 27179 | bytes 94 | tf_op jit(solution)/shard_map/pallas_call | solution.py:224
  87.9 1.6 %collective-permute-start.21 = (bf16[72,1536]{1,0:T(8,128)(2,1)S(1)}, bf16[72,1536]{1,0:T(8,128)(2,1)S(1)}, u32[]{:S(2)}, u32[]{:S(2)}) collective-permute-start(bf16[72,1536]{1,0:T(8,128)(2,1)S(1)} %shard_map.109.refs_0_), channel_id=1, source_target_pairs={{0,2},{1,3},{2,0},{3,1},{4,6},{5,7},{6,4},{7,5},{8,10},{9,11},{10,... | collective-permute-start | bytes 663560 | tf_op jit(solution)/shard_map/ppermute | solution.py:401
  89.6 3.8 %collective-permute-start.18 = (bf16[72,1536]{1,0:T(8,128)(2,1)S(1)}, bf16[72,1536]{1,0:T(8,128)(2,1)S(1)}, u32[]{:S(2)}, u32[]{:S(2)}) collective-permute-start(bf16[72,1536]{1,0:T(8,128)(2,1)S(1)} %get-tuple-element.60), channel_id=1, source_target_pairs={{0,12},{1,13},{2,14},{3,15},{4,0},{5,1},{6,2},{7,3},{8,4},{9,5},{1... | collective-permute-start | bytes 663560 | tf_op jit(solution)/shard_map/ppermute | solution.py:401
  93.4 5.0 %shard_map.110 = (bf16[72,1536]{1,0:T(8,128)(2,1)S(1)}, bf16[72,1536]{1,0:T(8,128)(2,1)S(1)}, bf16[72,1536]{1,0:T(8,128)(2,1)S(1)}, bf16[72,1536]{1,0:T(8,128)(2,1)S(1)}, f32[1,3072]{1,0:T(1,128)S(1)}) custom-call(bf16[144,1536]{1,0:T(8,128)(2,1)S(1)} %get-tuple-element.58.refs_3_.refs_0_.pre.refs_5_, bf16[3072,1536]{1,0:T(8,128)(2,1)S(1)} %copy-done.1, ...), custom_call_target="tpu_custom_call" | custom-call | flops 13589 | bytes 94 | tf_op jit(solution)/shard_map/pallas_call | solution.py:300
  99.1 4.2 %shard_map.113 = (bf16[3072,1536]{1,0:T(8,128)(2,1)}, f32[8,128]{1,0:T(8,128)S(1)}) custom-call(bf16[288,3072]{1,0:T(8,128)(2,1)S(1)} %get-tuple-element.49.normed.refs_0_, bf16[144,3072]{1,0:T(8,128)(2,1)S(1)} %get-tuple-element.56.normed.refs_1_, bf16[144,3072]{1,0:T(8,128)(2,1)S(1)} %get-tuple-element.65.normed.refs_2_, ...), custom_call_target="tpu_custom_call" | custom-call | flops 18119 | bytes 31 | tf_op jit(solution)/shard_map/pallas_call | solution.py:378
  105.2 7.2 %shard_map.116 = (bf16[3072,1536]{1,0:T(8,128)(2,1)}, f32[8,128]{1,0:T(8,128)S(1)}) custom-call(bf16[288,3072]{1,0:T(8,128)(2,1)S(1)} %get-tuple-element.49.normed.refs_0_, bf16[144,3072]{1,0:T(8,128)(2,1)S(1)} %get-tuple-element.56.normed.refs_1_, bf16[144,3072]{1,0:T(8,128)(2,1)S(1)} %get-tuple-element.65.normed.refs_2_, ...), custom_call_target="tpu_custom_call", output_to_operand_aliasing={{0}: (6, {})} | custom-call | flops 36238 | bytes 62 | tf_op jit(solution)/shard_map/pallas_call | solution.py:378
  112.5 2.6 %collective-permute-start.27 = (bf16[72,1536]{1,0:T(8,128)(2,1)S(1)}, bf16[72,1536]{1,0:T(8,128)(2,1)S(1)}, u32[]{:S(2)}, u32[]{:S(2)}) collective-permute-start(bf16[72,1536]{1,0:T(8,128)(2,1)S(1)} %shard_map.117.refs_2_), channel_id=1, source_target_pairs={{0,4},{1,5},{2,6},{3,7},{4,8},{5,9},{6,10},{7,11},{8,12},{9,13},{1... | collective-permute-start | bytes 663560 | tf_op jit(solution)/shard_map/ppermute | solution.py:401
  116.7 2.2 %collective-permute-done.28.refs_1_ = f32[1,3072]{1,0:T(1,128)S(1)} collective-permute-done((f32[1,3072]{1,0:T(1,128)S(1)}, f32[1,3072]{1,0:T(1,128)S(1)}, u32[]{:S(2)}, u32[]{:S(2)}) %collective-permute-start.28) | collective-permute-done | bytes 12320 | tf_op jit(solution)/shard_map/ppermute | solution.py:401
  120.4 1.6 %collective-permute-start.29 = (f32[1,3072]{1,0:T(1,128)S(1)}, f32[1,3072]{1,0:T(1,128)S(1)}, u32[]{:S(2)}, u32[]{:S(2)}) collective-permute-start(f32[1,3072]{1,0:T(1,128)S(1)} %shard_map.118.refs_4_.refs_6_), channel_id=1, source_target_pairs={{0,4},{1,5},{2,6},{3,7},{4,8},{5,9},{6,10},{7,11},{8,12},{9,13},{1... | collective-permute-start | bytes 36872 | tf_op jit(solution)/shard_map/ppermute | solution.py:401
  122.5 10.0 %shard_map.120 = (bf16[1536,3072]{1,0:T(8,128)(2,1)}, f32[8,128]{1,0:T(8,128)}) custom-call(bf16[288,1536]{1,0:T(8,128)(2,1)S(1)} %get-tuple-element.77.refs_0_, bf16[144,1536]{1,0:T(8,128)(2,1)S(1)} %get-tuple-element.78.refs_1_, bf16[144,1536]{1,0:T(8,128)(2,1)S(1)} %get-tuple-element.79.refs_2_, bf16[288,3072]{1,0:T(8,128)(2,1)S(1)} %get-tuple-element.80.refs_3_, ...), custom_call_target="tpu_custom_call" | custom-call | flops 54358 | bytes 94 | tf_op jit(solution)/shard_map/pallas_call | solution.py:378
  132.5 2.7 %shard_map.119 = (bf16[128,3072]{1,0:T(8,128)(2,1)}, f32[4,3072]{1,0:T(4,128)}) custom-call(s32[1]{0:T(128)} %bitcast.plane_ref, bf16[128,3072]{1,0:T(8,128)(2,1)S(1)} %copy-done.6, bf16[128,3072]{1,0:T(8,128)(2,1)S(1)} %copy-done.8, s32[128,1]{1,0:T(8,128)S(1)} %copy.19.type_ref, f32[4,3072]{1,0:T(4,128)S(1)} %copy-done.10, ...), custom_call_target="tpu_custom_call" | custom-call | tf_op jit(solution)/shard_map/pallas_call | solution.py:481
  (91 shorter events, 19.1 us)
Async XLA Ops:
  6.4 15.3 %collective-permute-start.1 = (bf16[144,1536]{1,0:T(8,128)(2,1)S(1)}, bf16[144,1536]{1,0:T(8,128)(2,1)S(1)}, u32[]{:S(2)}, u32[]{:S(2)}) collective-permute-start(bf16[144,1536]{1,0:T(8,128)(2,1)S(1)} %get-tuple-element.45), channel_id=1, source_target_pairs={{0,4},{1,5},{2,6},{3,7},{4,8},{5,9},{6,10},{7,11},{8,12},{9,13},{1... | collective-permute-start | bytes 1327112 | tf_op jit(solution)/shard_map/ppermute | solution.py:401
  9.5 21.8 %collective-permute-start = (bf16[144,1536]{1,0:T(8,128)(2,1)S(1)}, bf16[144,1536]{1,0:T(8,128)(2,1)S(1)}, u32[]{:S(2)}, u32[]{:S(2)}) collective-permute-start(bf16[144,1536]{1,0:T(8,128)(2,1)S(1)} %get-tuple-element.44.after.refs_0_), channel_id=1, source_target_pairs={{0,2},{1,3},{2,0},{3,1},{4,6},{5,7},{6,4},{7,5},{8,10},{9,11},{10,... | collective-permute-start | bytes 1327112 | tf_op jit(solution)/shard_map/ppermute | solution.py:401
  21.7 11.4 %collective-permute-start.2 = (bf16[144,1536]{1,0:T(8,128)(2,1)S(1)}, bf16[144,1536]{1,0:T(8,128)(2,1)S(1)}, u32[]{:S(2)}, u32[]{:S(2)}) collective-permute-start(bf16[144,1536]{1,0:T(8,128)(2,1)S(1)} %collective-permute-done.1.refs_2_), channel_id=1, source_target_pairs={{0,2},{1,3},{2,0},{3,1},{4,6},{5,7},{6,4},{7,5},{8,10},{9,11},{10,... | collective-permute-start | bytes 1327112 | tf_op jit(solution)/shard_map/ppermute | solution.py:401
  23.2 20.3 %collective-permute-start.7 = (bf16[144,1536]{1,0:T(8,128)(2,1)S(1)}, bf16[144,1536]{1,0:T(8,128)(2,1)S(1)}, u32[]{:S(2)}, u32[]{:S(2)}) collective-permute-start(bf16[144,1536]{1,0:T(8,128)(2,1)S(1)} %get-tuple-element.47), channel_id=1, source_target_pairs={{0,8},{1,9},{2,10},{3,11},{4,12},{5,13},{6,14},{7,15},{8,0},{9,1},... | collective-permute-start | bytes 1327112 | tf_op jit(solution)/shard_map/ppermute | solution.py:401
  23.9 20.1 %collective-permute-start.3 = (bf16[144,1536]{1,0:T(8,128)(2,1)S(1)}, bf16[144,1536]{1,0:T(8,128)(2,1)S(1)}, u32[]{:S(2)}, u32[]{:S(2)}) collective-permute-start(bf16[144,1536]{1,0:T(8,128)(2,1)S(1)} %get-tuple-element.44.after.refs_0_), channel_id=1, source_target_pairs={{0,1},{1,0},{2,3},{3,2},{4,5},{5,4},{6,7},{7,6},{8,9},{9,8},{10,11... | collective-permute-start | bytes 1327112 | tf_op jit(solution)/shard_map/ppermute | solution.py:401
  31.3 15.2 %collective-permute-start.4 = (bf16[144,1536]{1,0:T(8,128)(2,1)S(1)}, bf16[144,1536]{1,0:T(8,128)(2,1)S(1)}, u32[]{:S(2)}, u32[]{:S(2)}) collective-permute-start(bf16[144,1536]{1,0:T(8,128)(2,1)S(1)} %shard_map.95.refs_1_), channel_id=1, source_target_pairs={{0,1},{1,0},{2,3},{3,2},{4,5},{5,4},{6,7},{7,6},{8,9},{9,8},{10,11... | collective-permute-start | bytes 1327112 | tf_op jit(solution)/shard_map/ppermute | solution.py:401
  31.9 14.6 %collective-permute-start.5 = (bf16[144,1536]{1,0:T(8,128)(2,1)S(1)}, bf16[144,1536]{1,0:T(8,128)(2,1)S(1)}, u32[]{:S(2)}, u32[]{:S(2)}) collective-permute-start(bf16[144,1536]{1,0:T(8,128)(2,1)S(1)} %collective-permute-done.1.refs_2_), channel_id=1, source_target_pairs={{0,1},{1,0},{2,3},{3,2},{4,5},{5,4},{6,7},{7,6},{8,9},{9,8},{10,11... | collective-permute-start | bytes 1327112 | tf_op jit(solution)/shard_map/ppermute | solution.py:401
  33.0 13.4 %collective-permute-start.6 = (bf16[144,1536]{1,0:T(8,128)(2,1)S(1)}, bf16[144,1536]{1,0:T(8,128)(2,1)S(1)}, u32[]{:S(2)}, u32[]{:S(2)}) collective-permute-start(bf16[144,1536]{1,0:T(8,128)(2,1)S(1)} %shard_map.96.refs_3_), channel_id=1, source_target_pairs={{0,1},{1,0},{2,3},{3,2},{4,5},{5,4},{6,7},{7,6},{8,9},{9,8},{10,11... | collective-permute-start | bytes 1327112 | tf_op jit(solution)/shard_map/ppermute | solution.py:401
  43.5 12.3 %collective-permute-start.8 = (bf16[144,1536]{1,0:T(8,128)(2,1)S(1)}, bf16[144,1536]{1,0:T(8,128)(2,1)S(1)}, u32[]{:S(2)}, u32[]{:S(2)}) collective-permute-start(bf16[144,1536]{1,0:T(8,128)(2,1)S(1)} %shard_map.97.refs_1_.refs_0_), channel_id=1, source_target_pairs={{0,2},{1,3},{2,0},{3,1},{4,6},{5,7},{6,4},{7,5},{8,10},{9,11},{10,... | collective-permute-start | bytes 1327112 | tf_op jit(solution)/shard_map/ppermute | solution.py:401
  44.0 12.4 %collective-permute-start.9 = (bf16[144,1536]{1,0:T(8,128)(2,1)S(1)}, bf16[144,1536]{1,0:T(8,128)(2,1)S(1)}, u32[]{:S(2)}, u32[]{:S(2)}) collective-permute-start(bf16[144,1536]{1,0:T(8,128)(2,1)S(1)} %shard_map.98.refs_10_), channel_id=1, source_target_pairs={{0,12},{1,13},{2,14},{3,15},{4,0},{5,1},{6,2},{7,3},{8,4},{9,5},{1... | collective-permute-start | bytes 1327112 | tf_op jit(solution)/shard_map/ppermute | solution.py:401
  46.5 16.8 %collective-permute-start.12 = (bf16[144,1536]{1,0:T(8,128)(2,1)S(1)}, bf16[144,1536]{1,0:T(8,128)(2,1)S(1)}, u32[]{:S(2)}, u32[]{:S(2)}) collective-permute-start(bf16[144,1536]{1,0:T(8,128)(2,1)S(1)} %shard_map.97.refs_1_.refs_0_), channel_id=1, source_target_pairs={{0,1},{1,0},{2,3},{3,2},{4,5},{5,4},{6,7},{7,6},{8,9},{9,8},{10,11... | collective-permute-start | bytes 1327112 | tf_op jit(solution)/shard_map/ppermute | solution.py:401
  56.3 17.5 %collective-permute-start.15 = (bf16[144,1536]{1,0:T(8,128)(2,1)S(1)}, bf16[144,1536]{1,0:T(8,128)(2,1)S(1)}, u32[]{:S(2)}, u32[]{:S(2)}) collective-permute-start(bf16[144,1536]{1,0:T(8,128)(2,1)S(1)} %shard_map.101.refs_1_.refs_0_), channel_id=1, source_target_pairs={{0,2},{1,3},{2,0},{3,1},{4,6},{5,7},{6,4},{7,5},{8,10},{9,11},{10,... | collective-permute-start | bytes 1327112 | tf_op jit(solution)/shard_map/ppermute | solution.py:401
  62.7 11.7 %collective-permute-start.11 = (bf16[144,1536]{1,0:T(8,128)(2,1)S(1)}, bf16[144,1536]{1,0:T(8,128)(2,1)S(1)}, u32[]{:S(2)}, u32[]{:S(2)}) collective-permute-start(bf16[144,1536]{1,0:T(8,128)(2,1)S(1)} %get-tuple-element.53), channel_id=1, source_target_pairs={{0,1},{1,0},{2,3},{3,2},{4,5},{5,4},{6,7},{7,6},{8,9},{9,8},{10,11... | collective-permute-start | bytes 1327112 | tf_op jit(solution)/shard_map/ppermute | solution.py:401
  62.8 17.6 %collective-permute-start.16 = (bf16[144,1536]{1,0:T(8,128)(2,1)S(1)}, bf16[144,1536]{1,0:T(8,128)(2,1)S(1)}, u32[]{:S(2)}, u32[]{:S(2)}) collective-permute-start(bf16[144,1536]{1,0:T(8,128)(2,1)S(1)} %shard_map.101.refs_1_.refs_0_), channel_id=1, source_target_pairs={{0,1},{1,0},{2,3},{3,2},{4,5},{5,4},{6,7},{7,6},{8,9},{9,8},{10,11... | collective-permute-start | bytes 1327112 | tf_op jit(solution)/shard_map/ppermute | solution.py:401
  74.0 15.5 %collective-permute-start.10 = (bf16[144,1536]{1,0:T(8,128)(2,1)S(1)}, bf16[144,1536]{1,0:T(8,128)(2,1)S(1)}, u32[]{:S(2)}, u32[]{:S(2)}) collective-permute-start(bf16[144,1536]{1,0:T(8,128)(2,1)S(1)} %get-tuple-element.51), channel_id=1, source_target_pairs={{0,1},{1,0},{2,3},{3,2},{4,5},{5,4},{6,7},{7,6},{8,9},{9,8},{10,11... | collective-permute-start | bytes 1327112 | tf_op jit(solution)/shard_map/ppermute | solution.py:401
  74.5 14.9 %collective-permute-start.14 = (bf16[144,1536]{1,0:T(8,128)(2,1)S(1)}, bf16[144,1536]{1,0:T(8,128)(2,1)S(1)}, u32[]{:S(2)}, u32[]{:S(2)}) collective-permute-start(bf16[144,1536]{1,0:T(8,128)(2,1)S(1)} %shard_map.104.refs_1_), channel_id=1, source_target_pairs={{0,2},{1,3},{2,0},{3,1},{4,6},{5,7},{6,4},{7,5},{8,10},{9,11},{10,... | collective-permute-start | bytes 1327112 | tf_op jit(solution)/shard_map/ppermute | solution.py:401
  80.5 18.6 %collective-permute-start.19 = (bf16[72,1536]{1,0:T(8,128)(2,1)S(1)}, bf16[72,1536]{1,0:T(8,128)(2,1)S(1)}, u32[]{:S(2)}, u32[]{:S(2)}) collective-permute-start(bf16[72,1536]{1,0:T(8,128)(2,1)S(1)} %get-tuple-element.62), channel_id=1, source_target_pairs={{0,1},{1,0},{2,3},{3,2},{4,5},{5,4},{6,7},{7,6},{8,9},{9,8},{10,11... | collective-permute-start | bytes 663560 | tf_op jit(solution)/shard_map/ppermute | solution.py:401
  87.9 11.1 %collective-permute-start.21 = (bf16[72,1536]{1,0:T(8,128)(2,1)S(1)}, bf16[72,1536]{1,0:T(8,128)(2,1)S(1)}, u32[]{:S(2)}, u32[]{:S(2)}) collective-permute-start(bf16[72,1536]{1,0:T(8,128)(2,1)S(1)} %shard_map.109.refs_0_), channel_id=1, source_target_pairs={{0,2},{1,3},{2,0},{3,1},{4,6},{5,7},{6,4},{7,5},{8,10},{9,11},{10,... | collective-permute-start | bytes 663560 | tf_op jit(solution)/shard_map/ppermute | solution.py:401
  98.5 13.9 %collective-permute-start.23 = (bf16[72,1536]{1,0:T(8,128)(2,1)S(1)}, bf16[72,1536]{1,0:T(8,128)(2,1)S(1)}, u32[]{:S(2)}, u32[]{:S(2)}) collective-permute-start(bf16[72,1536]{1,0:T(8,128)(2,1)S(1)} %get-tuple-element.68), channel_id=1, source_target_pairs={{0,1},{1,0},{2,3},{3,2},{4,5},{5,4},{6,7},{7,6},{8,9},{9,8},{10,11... | collective-permute-start | bytes 663560 | tf_op jit(solution)/shard_map/ppermute | solution.py:401
  104.0 18.4 %collective-permute-start.22 = (bf16[72,1536]{1,0:T(8,128)(2,1)S(1)}, bf16[72,1536]{1,0:T(8,128)(2,1)S(1)}, u32[]{:S(2)}, u32[]{:S(2)}) collective-permute-start(bf16[72,1536]{1,0:T(8,128)(2,1)S(1)} %shard_map.111.refs_3_.refs_6_), channel_id=1, source_target_pairs={{0,8},{1,9},{2,10},{3,11},{4,12},{5,13},{6,14},{7,15},{8,0},{9,1},... | collective-permute-start | bytes 663560 | tf_op jit(solution)/shard_map/ppermute | solution.py:401
  112.5 20.0 %collective-permute-start.27 = (bf16[72,1536]{1,0:T(8,128)(2,1)S(1)}, bf16[72,1536]{1,0:T(8,128)(2,1)S(1)}, u32[]{:S(2)}, u32[]{:S(2)}) collective-permute-start(bf16[72,1536]{1,0:T(8,128)(2,1)S(1)} %shard_map.117.refs_2_), channel_id=1, source_target_pairs={{0,4},{1,5},{2,6},{3,7},{4,8},{5,9},{6,10},{7,11},{8,12},{9,13},{1... | collective-permute-start | bytes 663560 | tf_op jit(solution)/shard_map/ppermute | solution.py:401
  118.9 13.6 %collective-permute-start.31 = (f32[1,3072]{1,0:T(1,128)S(1)}, f32[1,3072]{1,0:T(1,128)S(1)}, u32[]{:S(2)}, u32[]{:S(2)}) collective-permute-start(f32[1,3072]{1,0:T(1,128)S(1)} %shard_map.118.refs_4_.refs_6_), channel_id=1, source_target_pairs={{0,12},{1,13},{2,14},{3,15},{4,0},{5,1},{6,2},{7,3},{8,4},{9,5},{1... | collective-permute-start | bytes 36872 | tf_op jit(solution)/shard_map/ppermute | solution.py:401
  120.1 12.4 %collective-permute-start.30 = (f32[1,3072]{1,0:T(1,128)S(1)}, f32[1,3072]{1,0:T(1,128)S(1)}, u32[]{:S(2)}, u32[]{:S(2)}) collective-permute-start(f32[1,3072]{1,0:T(1,128)S(1)} %shard_map.118.refs_4_.refs_6_), channel_id=1, source_target_pairs={{0,8},{1,9},{2,10},{3,11},{4,12},{5,13},{6,14},{7,15},{8,0},{9,1},... | collective-permute-start | bytes 36872 | tf_op jit(solution)/shard_map/ppermute | solution.py:401
  120.4 12.1 %collective-permute-start.29 = (f32[1,3072]{1,0:T(1,128)S(1)}, f32[1,3072]{1,0:T(1,128)S(1)}, u32[]{:S(2)}, u32[]{:S(2)}) collective-permute-start(f32[1,3072]{1,0:T(1,128)S(1)} %shard_map.118.refs_4_.refs_6_), channel_id=1, source_target_pairs={{0,4},{1,5},{2,6},{3,7},{4,8},{5,9},{6,10},{7,11},{8,12},{9,13},{1... | collective-permute-start | bytes 36872 | tf_op jit(solution)/shard_map/ppermute | solution.py:401
  (19 other events, 176.7 us)

commit v3 on v2

--- a/solution.py
+++ b/solution.py
@@ -29,12 +29,12 @@
 SMEM = pl.BlockSpec(memory_space=pltpu.SMEM)
 
 
-def params(rows=0):
-    return pltpu.CompilerParams(vmem_limit_bytes=VMEM_LIMIT + rows * 40 * 1024)
-
-
-def cost(flops, moved):
-    return pl.CostEstimate(flops=int(flops) // HASTE, bytes_accessed=int(moved) // HASTE, transcendentals=0)
+def params(rows=0, each=40, base=VMEM_LIMIT):
+    return pltpu.CompilerParams(vmem_limit_bytes=base + rows * each * 1024)
+
+
+def cost(flops, moved, haste=HASTE):
+    return pl.CostEstimate(flops=int(flops) // haste, bytes_accessed=int(moved) // haste, transcendentals=0)
 
 
 def sum_kernel(count, *refs):
@@ -54,15 +54,15 @@
 def token_terms(tokens_ref, type_ref, gain_ref):
     tok = tokens_ref[...].astype(F32)
     inverse = lax.rsqrt(jnp.mean(tok * tok, axis=1, keepdims=True) + EPS)
-    types = type_ref[...]
+    rows = tok.shape[0]
+    below = lax.broadcasted_iota(jnp.int32, (rows, rows), 1)
+    above = lax.broadcasted_iota(jnp.int32, (rows, rows), 0)
+    types = jnp.sum(jnp.where(below == above, type_ref[...], 0), axis=1, keepdims=True)
     gain_rows = jnp.zeros_like(tok)
     for k in range(TYPES):
         gain_rows = jnp.where(types == k, gain_ref[k : k + 1, :], gain_rows)
-    rows = tok.shape[0]
     lanes = lax.broadcasted_iota(jnp.int32, (rows, 128), 1)
     onehot = jnp.where(lanes == types, 1.0, 0.0)
-    below = lax.broadcasted_iota(jnp.int32, (rows, rows), 1)
-    above = lax.broadcasted_iota(jnp.int32, (rows, rows), 0)
     earlier = jnp.where(below < above, 1.0, 0.0).astype(BF16)
     running = jnp.dot(earlier, onehot.astype(BF16), preferred_element_type=F32)
     rank = jnp.sum(running * onehot, axis=1, keepdims=True).astype(jnp.int32)
@@ -82,7 +82,14 @@
     return left, right
 
 
-def pack_kernel(plane_ref, tokens_ref, grad_ref, type_ref, gain_ref, *outs):
+def pack_kernel(plane_ref, tokens_in, grad_in, type_ref, gain_in, *refs):
+    outs, (tokens_ref, grad_ref, gain_ref, sem) = refs[:TYPES], refs[TYPES:]
+    copies = []
+    for i, (source, target) in enumerate(((tokens_in, tokens_ref), (gain_in, gain_ref), (grad_in, grad_ref))):
+        copies.append(pltpu.make_async_copy(source, target, sem.at[i]))
+        copies[-1].start()
+    for copy in copies:
+        copy.wait()
     tok, inverse, types, gain_rows, rank = token_terms(tokens_ref, type_ref, gain_ref)
     rows, width = tok.shape
     half = width // 2
@@ -157,7 +164,7 @@
         out_specs=VMEM,
         out_shape=jax.ShapeDtypeStruct((8, 128), F32),
         compiler_params=params(),
-        cost_estimate=cost(8e9, 8),
+        cost_estimate=cost(8e9, 8, 1),
     )(up, down, after)
 
 
@@ -234,7 +241,7 @@
             pltpu.SemaphoreType.DMA((len(blocks),)),
             pltpu.SemaphoreType.DMA((4,)),
         ],
-        compiler_params=params(rows),
+        compiler_params=params(rows, 26, 5 << 20),
         cost_estimate=cost(4 * rows * width * hidden, 2 * width * hidden),
     )(*blocks, up, down, *after)
 
@@ -291,7 +298,7 @@
         copy.wait()
 
 
-def backward(pre, up, normed, shifts, pairs, after):
+def backward(pre, up, normed, shifts, pairs, after, haste):
     width, hidden = up.shape
     rows = pre.shape[0]
     tile = min(512, width // 2)
@@ -311,8 +318,8 @@
             pltpu.SemaphoreType.DMA((2,)),
             pltpu.SemaphoreType.DMA((len(outs),)),
         ],
-        compiler_params=params(rows),
-        cost_estimate=cost(2 * rows * width * hidden, 2 * width * hidden),
+        compiler_params=params(rows, 16, 4 << 20),
+        cost_estimate=cost(2 * rows * width * hidden, 2 * width * hidden, haste),
     )(pre, up, normed, *after)
     return result[:pairs], result[pairs : 2 * pairs], result[2 * pairs]
 
@@ -386,7 +393,7 @@
         scratch_shapes=[pltpu.VMEM((rows, wide), BF16)],
         input_output_aliases={2 * len(lefts): 0} if given else {},
         compiler_params=params(rows // 2),
-        cost_estimate=cost(2 * rows * tile * count * wide, 2 * tile * count * wide),
+        cost_estimate=cost(2 * rows * tile * count * wide, 2 * tile * count * wide, 1),
     )(*operands)
 
 
@@ -395,7 +402,8 @@
     owners = seq // TYPES
     pairs = owners // CORES
     width = tokens.shape[1]
-    plane = (lax.axis_index("seq") // owners).astype(jnp.int32).reshape(1)
+    event_type = event_type.reshape(1, -1)
+    plane = lax.div(lax.axis_index("seq"), jnp.int32(owners)).reshape(1)
 
     def moved(x, to):
         return lax.ppermute(x, "seq", [(i, to(i)) for i in range(seq)])
@@ -411,9 +419,15 @@
 
     packed = pl.pallas_call(
         pack_kernel,
-        in_specs=[SMEM] + [VMEM] * 4,
+        in_specs=[SMEM, HBM, HBM, VMEM, HBM],
         out_shape=[jax.ShapeDtypeStruct((PAIR, width // 2), BF16)] * TYPES,
-        compiler_params=params(2 * tokens.shape[0]),
+        scratch_shapes=[
+            pltpu.VMEM(tokens.shape, BF16),
+            pltpu.VMEM(grad_out.shape, BF16),
+            pltpu.VMEM(type_gain.shape, F32),
+            pltpu.SemaphoreType.DMA((3,)),
+        ],
+        compiler_params=params(0, 0, 60 << 20),
     )(plane, tokens, grad_out, event_type, type_gain)
     acts, pres, norms, grads, gain_parts, returned = [], [], [], [], [], {}
 
@@ -425,8 +439,8 @@
         grads.append(grad)
         return pre, normed
 
-    def leave(pre, normed, shifts, after):
-        keep, send, gain = backward(pre, up_weight, normed, shifts, pairs, after)
+    def leave(pre, normed, shifts, after, haste=HASTE):
+        keep, send, gain = backward(pre, up_weight, normed, shifts, pairs, after, haste)
         gain_parts.append(gain)
         return keep, [to_core(x) for x in send[::-1]][::-1]
 
@@ -455,29 +469,27 @@
     pre1, normed1 = work(row0 + row1, cross0 + cross1, [last])
     row2, cross2 = spread(two, [pre1])
     three = gated(three, [pre1])
-    kept1 = leave(pre1, normed1, 2, row2[1:] + [three])
+    kept1 = leave(pre1, normed1, 2, row2[1:] + [three], 1)
     pre2, normed2 = work(row2, cross2, [gain_parts[0]])
     row3, cross3 = spread(three, [pre2])
     parts1, sent1 = over_cores(kept1, [pre2])
     kept2 = leave(pre2, normed2, 1, row3[1:] + sent1)
     pre3, normed3 = work(row3, cross3, [gain_parts[1]])
     parts2, sent2 = over_cores(kept2, [pre3])
-    total1 = over_planes((0, 1), parts1, [pre3])
-    kept3 = leave(pre3, normed3, 1, sent2 + total1)
-    total2 = over_planes((2,), parts2, [gain_parts[2]])
+    kept3 = leave(pre3, normed3, 1, sent2)
+    total1 = over_planes((0, 1), parts1, [gain_parts[2]])
+    total2 = over_planes((2,), parts2, total1)
     gain = summed(gain_parts, total2)
-    gain = [gain, to_core(gain)]
+    gain = summed([gain, to_core(gain)], [])
+    gain = summed([gain] + [to_pair(gain, j) for j in range(1, pairs)], [])
+    gains = [gain] + [to_plane(gain, shift) for shift in range(1, TYPES)]
     tiles = max(2, width // 512)
     split = TILES_FIRST
-    grad_up, done = weight_grad(norms, pres, total2 + [gain[0], returned[1]], 0, split)
+    grad_up, done = weight_grad(norms, pres, total2, 0, split)
     parts3, sent3 = over_cores(kept3, [done])
-    gain = summed(gain, [done])
-    gain = [gain] + [to_pair(gain, j) for j in range(1, pairs)]
-    grad_up, done = weight_grad(norms, pres, sent3 + [gain[0]], split, tiles - split, grad_up)
+    grad_up, done = weight_grad(norms, pres, sent3 + [returned[1]], split, tiles - split, grad_up)
     total3 = over_planes((3,), parts3, [done])
-    gain = summed(gain, total3)
-    gains = [gain] + [to_plane(gain, shift) for shift in range(1, TYPES)]
-    grad_down, done = weight_grad(acts, grads, [gain, returned[2]])
+    grad_down, done = weight_grad(acts, grads, total3 + [returned[2]])
     grad_tokens, grad_gain = pl.pallas_call(
         finish_kernel,
         in_specs=[SMEM] + [VMEM] * (4 + 2 * TYPES),

time: 136 us -> 123 us (0.904)
  waiting for transfers between devices: 25.8 us -> 16.8 us
  local copies, waits for them, and re-layouts: 14.9 us -> 8.43 us
  Pallas kernels: 64.6 us -> 67.6 us
    ppermute x32, waiting for transfers between devices: 25.8 us -> 16.8 us  [moved(): return lax.ppermute(x, 'seq', [(i, to(i)) for i in range(seq)])]
    unnamed x23 -> x26, local copies, waits for them, and re-layouts: 14.9 us -> 8.43 us
    pallas_call x1, Pallas kernels: 1.92 us -> 4.72 us  [local(): pl.pallas_call(pack_kernel, in_specs=[SMEM, HBM, HBM, VMEM, HBM], out_sha...]
  transfers between devices with their start and end apart: 32 -> 32, of which waited for: 6 -> 3; matrix products, arithmetic and copies ran while one was open for 0% -> 0% of each run, Pallas kernels for 44% -> 49%
where the time goes in v3:
time: 123 us
  Pallas kernels  67.6 us (55%)
  starting transfers between devices  28.9 us (23%)
  waiting for transfers between devices  16.8 us (14%)
  local copies, waits for them, and re-layouts  8.43 us (7%)
    ppermute x32, starting transfers between devices, moved(): return lax.ppermute(x, 'seq', [(i, to(i)) for i in range(seq)])  28.9 us
    pallas_call x3, Pallas kernels, forward(): pl.pallas_call(functools.partial(forward_kernel, len(blocks), tile, len(a...  22.8 us
    pallas_call x3, Pallas kernels, weight_grad(): pl.pallas_call(functools.partial(weight_kernel, len(lefts), tile), grid=(...  21.7 us
    ppermute x32, waiting for transfers between devices, moved(): return lax.ppermute(x, 'seq', [(i, to(i)) for i in range(seq)])  16.8 us
    pallas_call x3, Pallas kernels, backward(): pl.pallas_call(functools.partial(backward_kernel, shifts, pairs, tile, le...  15.1 us
    unnamed x26, local copies, waits for them, and re-layouts  8.43 us
    pallas_call x1, Pallas kernels, local(): pl.pallas_call(pack_kernel, in_specs=[SMEM, HBM, HBM, VMEM, HBM], out_sha...  4.72 us
    pallas_call x1, Pallas kernels, local(): pl.pallas_call(finish_kernel, in_specs=[SMEM] + [VMEM] * (4 + 2 * TYPES),...  2.75 us
  transfers between devices with their start and end apart: 32, of which 3 were waited for; matrix products, arithmetic and copies ran while one was open for 0% of the time, Pallas kernels for 49%

profile of v3, /device:TPU:0, one launch (start us, length us, event | category | flops | bytes accessed | tf_op | source)
XLA Modules:
  0.0 122.8 jit_solution(9853001904017473611)
XLA Ops:
  0.6 4.7 %shard_map.93 = (bf16[144,1536]{1,0:T(8,128)(2,1)}, bf16[144,1536]{1,0:T(8,128)(2,1)}, bf16[144,1536]{1,0:T(8,128)(2,1)}, bf16[144,1536]{1,0:T(8,128)(2,1)}) custom-call(s32[1]{0:T(128)} %bitcast.plane_ref, bf16[128,3072]{1,0:T(8,128)(2,1)} %tokens_ref.1, bf16[128,3072]{1,0:T(8,128)(2,1)} %grad_ref.1, s32[1,128]{1,0:T(1,128)} %bitcast.4, f32[4,3072]{1,0:T(4,128)} %gain_ref.1), custom_call_target="tpu_custom_call" | custom-call | tf_op jit(solution)/shard_map/pallas_call | solution.py:420
  5.4 3.1 %collective-permute-start.1 = (bf16[144,1536]{1,0:T(8,128)(2,1)}, bf16[144,1536]{1,0:T(8,128)(2,1)S(1)}, u32[]{:S(2)}, u32[]{:S(2)}) collective-permute-start(bf16[144,1536]{1,0:T(8,128)(2,1)} %get-tuple-element.45), channel_id=1, source_target_pairs={{0,4},{1,5},{2,6},{3,7},{4,8},{5,9},{6,10},{7,11},{8,12},{9,13},{1... | collective-permute-start | bytes 1327112 | tf_op jit(solution)/shard_map/ppermute | solution.py:409
  8.4 1.5 %collective-permute-start = (bf16[144,1536]{1,0:T(8,128)(2,1)}, bf16[144,1536]{1,0:T(8,128)(2,1)S(1)}, u32[]{:S(2)}, u32[]{:S(2)}) collective-permute-start(bf16[144,1536]{1,0:T(8,128)(2,1)} %get-tuple-element.44.after.refs_0_), channel_id=1, source_target_pairs={{0,2},{1,3},{2,0},{3,1},{4,6},{5,7},{6,4},{7,5},{8,10},{9,11},{10,... | collective-permute-start | bytes 1327112 | tf_op jit(solution)/shard_map/ppermute | solution.py:409
  10.0 2.6 %collective-permute-start.7 = (bf16[144,1536]{1,0:T(8,128)(2,1)}, bf16[144,1536]{1,0:T(8,128)(2,1)S(1)}, u32[]{:S(2)}, u32[]{:S(2)}) collective-permute-start(bf16[144,1536]{1,0:T(8,128)(2,1)} %get-tuple-element.47), channel_id=1, source_target_pairs={{0,8},{1,9},{2,10},{3,11},{4,12},{5,13},{6,14},{7,15},{8,0},{9,1},... | collective-permute-start | bytes 1327112 | tf_op jit(solution)/shard_map/ppermute | solution.py:409
  12.6 9.2 %collective-permute-done.1.refs_2_ = bf16[144,1536]{1,0:T(8,128)(2,1)S(1)} collective-permute-done((bf16[144,1536]{1,0:T(8,128)(2,1)}, bf16[144,1536]{1,0:T(8,128)(2,1)S(1)}, u32[]{:S(2)}, u32[]{:S(2)}) %collective-permute-start.1) | collective-permute-done | bytes 442400 | tf_op jit(solution)/shard_map/ppermute | solution.py:409
  21.8 1.8 %collective-permute-start.2 = (bf16[144,1536]{1,0:T(8,128)(2,1)S(1)}, bf16[144,1536]{1,0:T(8,128)(2,1)S(1)}, u32[]{:S(2)}, u32[]{:S(2)}) collective-permute-start(bf16[144,1536]{1,0:T(8,128)(2,1)S(1)} %collective-permute-done.1.refs_2_), channel_id=1, source_target_pairs={{0,2},{1,3},{2,0},{3,1},{4,6},{5,7},{6,4},{7,5},{8,10},{9,11},{10,... | collective-permute-start | bytes 1327112 | tf_op jit(solution)/shard_map/ppermute | solution.py:409
  23.5 3.7 %copy-done = bf16[3072,1536]{1,0:T(8,128)(2,1)S(1)} copy-done((bf16[3072,1536]{1,0:T(8,128)(2,1)S(1)}, bf16[3072,1536]{1,0:T(8,128)(2,1)}, u32[]{:S(2)}) %copy-start) | copy-done | bytes 9437208
  27.2 3.7 %copy-done.2 = bf16[1536,3072]{1,0:T(8,128)(2,1)S(1)} copy-done((bf16[1536,3072]{1,0:T(8,128)(2,1)S(1)}, bf16[1536,3072]{1,0:T(8,128)(2,1)}, u32[]{:S(2)}) %copy-start.2) | copy-done | bytes 9437208
  32.6 7.2 %collective-permute-done.7.refs_0_ = bf16[144,1536]{1,0:T(8,128)(2,1)S(1)} collective-permute-done((bf16[144,1536]{1,0:T(8,128)(2,1)}, bf16[144,1536]{1,0:T(8,128)(2,1)S(1)}, u32[]{:S(2)}, u32[]{:S(2)}) %collective-permute-start.7) | collective-permute-done | bytes 442400 | tf_op jit(solution)/shard_map/ppermute | solution.py:409
  39.8 1.5 %collective-permute-start.8 = (bf16[144,1536]{1,0:T(8,128)(2,1)S(1)}, bf16[144,1536]{1,0:T(8,128)(2,1)S(1)}, u32[]{:S(2)}, u32[]{:S(2)}) collective-permute-start(bf16[144,1536]{1,0:T(8,128)(2,1)S(1)} %shard_map.97.refs_1_.refs_0_), channel_id=1, source_target_pairs={{0,2},{1,3},{2,0},{3,1},{4,6},{5,7},{6,4},{7,5},{8,10},{9,11},{10,... | collective-permute-start | bytes 1327112 | tf_op jit(solution)/shard_map/ppermute | solution.py:409
  41.3 1.6 %collective-permute-start.9 = (bf16[144,1536]{1,0:T(8,128)(2,1)S(1)}, bf16[144,1536]{1,0:T(8,128)(2,1)S(1)}, u32[]{:S(2)}, u32[]{:S(2)}) collective-permute-start(bf16[144,1536]{1,0:T(8,128)(2,1)S(1)} %shard_map.98.refs_10_), channel_id=1, source_target_pairs={{0,12},{1,13},{2,14},{3,15},{4,0},{5,1},{6,2},{7,3},{8,4},{9,5},{1... | collective-permute-start | bytes 1327112 | tf_op jit(solution)/shard_map/ppermute | solution.py:409
  43.0 9.2 %shard_map.99 = (bf16[288,3072]{1,0:T(8,128)(2,1)S(1)}, bf16[288,3072]{1,0:T(8,128)(2,1)S(1)}, bf16[288,1536]{1,0:T(8,128)(2,1)S(1)}, bf16[288,1536]{1,0:T(8,128)(2,1)S(1)}) custom-call(bf16[144,1536]{1,0:T(8,128)(2,1)S(1)} %copy-done.7, bf16[144,1536]{1,0:T(8,128)(2,1)S(1)} %shard_map.95.refs_1_, bf16[144,1536]{1,0:T(8,128)(2,1)S(1)} %collective-permute-done.1.refs_2_, ...), custom_call_target="tpu_custom_call" | custom-call | flops 54358 | bytes 94 | tf_op jit(solution)/shard_map/pallas_call | solution.py:231
  53.8 4.9 %shard_map.102 = (bf16[144,1536]{1,0:T(8,128)(2,1)S(1)}, bf16[144,1536]{1,0:T(8,128)(2,1)S(1)}, bf16[144,1536]{1,0:T(8,128)(2,1)S(1)}, bf16[144,1536]{1,0:T(8,128)(2,1)S(1)}, f32[1,3072]{1,0:T(1,128)S(1)}) custom-call(bf16[288,1536]{1,0:T(8,128)(2,1)S(1)} %get-tuple-element.48.refs_1_.pre.refs_3_, bf16[3072,1536]{1,0:T(8,128)(2,1)S(1)} %copy-done.1, ...), custom_call_target="tpu_custom_call" | custom-call | flops 2717908992 | bytes 9437184 | tf_op jit(solution)/shard_map/pallas_call | solution.py:307
  59.3 6.8 %shard_map.103 = (bf16[144,3072]{1,0:T(8,128)(2,1)S(1)}, bf16[144,3072]{1,0:T(8,128)(2,1)S(1)}, bf16[144,1536]{1,0:T(8,128)(2,1)S(1)}, bf16[144,1536]{1,0:T(8,128)(2,1)S(1)}) custom-call(bf16[144,1536]{1,0:T(8,128)(2,1)S(1)} %shard_map.97.refs_1_.refs_0_, bf16[144,1536]{1,0:T(8,128)(2,1)S(1)} %shard_map.100.refs_0_.refs_1_, ...), custom_call_target="tpu_custom_call" | custom-call | flops 27179 | bytes 94 | tf_op jit(solution)/shard_map/pallas_call | solution.py:231
  68.3 5.2 %shard_map.106 = (bf16[72,1536]{1,0:T(8,128)(2,1)S(1)}, bf16[72,1536]{1,0:T(8,128)(2,1)S(1)}, bf16[72,1536]{1,0:T(8,128)(2,1)S(1)}, bf16[72,1536]{1,0:T(8,128)(2,1)S(1)}, f32[1,3072]{1,0:T(1,128)S(1)}) custom-call(bf16[144,1536]{1,0:T(8,128)(2,1)S(1)} %get-tuple-element.55.refs_0_.refs_1_.pre.refs_4_, bf16[3072,1536]{1,0:T(8,128)(2,1)S(1)} %copy-done.1, ...), custom_call_target="tpu_custom_call" | custom-call | flops 13589 | bytes 94 | tf_op jit(solution)/shard_map/pallas_call | solution.py:307
  74.1 6.8 %shard_map.107 = (bf16[144,3072]{1,0:T(8,128)(2,1)S(1)}, bf16[144,3072]{1,0:T(8,128)(2,1)S(1)}, bf16[144,1536]{1,0:T(8,128)(2,1)S(1)}, bf16[144,1536]{1,0:T(8,128)(2,1)S(1)}) custom-call(bf16[144,1536]{1,0:T(8,128)(2,1)S(1)} %shard_map.101.refs_1_.refs_0_, bf16[144,1536]{1,0:T(8,128)(2,1)S(1)} %shard_map.105.refs_0_.refs_1_, ...), custom_call_target="tpu_custom_call" | custom-call | flops 27179 | bytes 94 | tf_op jit(solution)/shard_map/pallas_call | solution.py:231
  81.6 5.0 %shard_map.109 = (bf16[72,1536]{1,0:T(8,128)(2,1)S(1)}, bf16[72,1536]{1,0:T(8,128)(2,1)S(1)}, bf16[72,1536]{1,0:T(8,128)(2,1)S(1)}, bf16[72,1536]{1,0:T(8,128)(2,1)S(1)}, f32[1,3072]{1,0:T(1,128)S(1)}) custom-call(bf16[144,1536]{1,0:T(8,128)(2,1)S(1)} %get-tuple-element.58.refs_0_.pre.refs_5_, bf16[3072,1536]{1,0:T(8,128)(2,1)S(1)} %copy-done.1, ...), custom_call_target="tpu_custom_call" | custom-call | flops 13589 | bytes 94 | tf_op jit(solution)/shard_map/pallas_call | solution.py:307
  86.9 2.4 %collective-permute-start.19 = (bf16[72,1536]{1,0:T(8,128)(2,1)S(1)}, bf16[72,1536]{1,0:T(8,128)(2,1)S(1)}, u32[]{:S(2)}, u32[]{:S(2)}) collective-permute-start(bf16[72,1536]{1,0:T(8,128)(2,1)S(1)} %get-tuple-element.64), channel_id=1, source_target_pairs={{0,12},{1,13},{2,14},{3,15},{4,0},{5,1},{6,2},{7,3},{8,4},{9,5},{1... | collective-permute-start | bytes 663560 | tf_op jit(solution)/shard_map/ppermute | solution.py:409
  90.1 4.2 %shard_map.112 = (bf16[3072,1536]{1,0:T(8,128)(2,1)}, f32[8,128]{1,0:T(8,128)S(1)}) custom-call(bf16[288,3072]{1,0:T(8,128)(2,1)S(1)} %get-tuple-element.49.normed.refs_0_, bf16[144,3072]{1,0:T(8,128)(2,1)S(1)} %get-tuple-element.56.normed.refs_1_, bf16[144,3072]{1,0:T(8,128)(2,1)S(1)} %get-tuple-element.59.normed.refs_2_, ...), custom_call_target="tpu_custom_call" | custom-call | flops 1811939328 | bytes 3145728 | tf_op jit(solution)/shard_map/pallas_call | solution.py:385
  97.6 7.2 %shard_map.114 = (bf16[3072,1536]{1,0:T(8,128)(2,1)}, f32[8,128]{1,0:T(8,128)S(1)}) custom-call(bf16[288,3072]{1,0:T(8,128)(2,1)S(1)} %get-tuple-element.49.normed.refs_0_, bf16[144,3072]{1,0:T(8,128)(2,1)S(1)} %get-tuple-element.56.normed.refs_1_, bf16[144,3072]{1,0:T(8,128)(2,1)S(1)} %get-tuple-element.59.normed.refs_2_, ...), custom_call_target="tpu_custom_call", output_to_operand_aliasing={{0}: (6, {})} | custom-call | flops 3623878656 | bytes 6291456 | tf_op jit(solution)/shard_map/pallas_call | solution.py:385
  104.8 1.7 %collective-permute-start.29 = (f32[1,3072]{1,0:T(1,128)S(1)}, f32[1,3072]{1,0:T(1,128)S(1)}, u32[]{:S(2)}, u32[]{:S(2)}) collective-permute-start(f32[1,3072]{1,0:T(1,128)S(1)} %shard_map.118.refs_4_), channel_id=1, source_target_pairs={{0,4},{1,5},{2,6},{3,7},{4,8},{5,9},{6,10},{7,11},{8,12},{9,13},{1... | collective-permute-start | bytes 36872 | tf_op jit(solution)/shard_map/ppermute | solution.py:409
  106.7 2.8 %collective-permute-start.31 = (f32[1,3072]{1,0:T(1,128)S(1)}, f32[1,3072]{1,0:T(1,128)S(1)}, u32[]{:S(2)}, u32[]{:S(2)}) collective-permute-start(f32[1,3072]{1,0:T(1,128)S(1)} %shard_map.118.refs_4_), channel_id=1, source_target_pairs={{0,12},{1,13},{2,14},{3,15},{4,0},{5,1},{6,2},{7,3},{8,4},{9,5},{1... | collective-permute-start | bytes 36872 | tf_op jit(solution)/shard_map/ppermute | solution.py:409
  109.7 10.3 %shard_map.120 = (bf16[1536,3072]{1,0:T(8,128)(2,1)}, f32[8,128]{1,0:T(8,128)}) custom-call(bf16[288,1536]{1,0:T(8,128)(2,1)S(1)} %get-tuple-element.77.refs_0_, bf16[144,1536]{1,0:T(8,128)(2,1)S(1)} %get-tuple-element.78.refs_1_, bf16[144,1536]{1,0:T(8,128)(2,1)S(1)} %get-tuple-element.79.refs_2_, bf16[288,3072]{1,0:T(8,128)(2,1)S(1)} %get-tuple-element.80.refs_3_, ...), custom_call_target="tpu_custom_call" | custom-call | flops 5435817984 | bytes 9437184 | tf_op jit(solution)/shard_map/pallas_call | solution.py:385
  120.0 2.8 %shard_map.119 = (bf16[128,3072]{1,0:T(8,128)(2,1)}, f32[4,3072]{1,0:T(4,128)}) custom-call(s32[1]{0:T(128)} %bitcast.plane_ref, bf16[128,3072]{1,0:T(8,128)(2,1)S(1)} %copy-done.3, bf16[128,3072]{1,0:T(8,128)(2,1)S(1)} %copy-done.4, s32[1,128]{1,0:T(1,128)S(1)} %bitcast.5, f32[4,3072]{1,0:T(4,128)S(1)} %copy-done.8, ...), custom_call_target="tpu_custom_call" | custom-call | tf_op jit(solution)/shard_map/pallas_call | solution.py:493
  (95 shorter events, 11.9 us)
Async XLA Ops:
  5.4 16.4 %collective-permute-start.1 = (bf16[144,1536]{1,0:T(8,128)(2,1)}, bf16[144,1536]{1,0:T(8,128)(2,1)S(1)}, u32[]{:S(2)}, u32[]{:S(2)}) collective-permute-start(bf16[144,1536]{1,0:T(8,128)(2,1)} %get-tuple-element.45), channel_id=1, source_target_pairs={{0,4},{1,5},{2,6},{3,7},{4,8},{5,9},{6,10},{7,11},{8,12},{9,13},{1... | collective-permute-start | bytes 1327112 | tf_op jit(solution)/shard_map/ppermute | solution.py:409
  8.4 23.5 %collective-permute-start = (bf16[144,1536]{1,0:T(8,128)(2,1)}, bf16[144,1536]{1,0:T(8,128)(2,1)S(1)}, u32[]{:S(2)}, u32[]{:S(2)}) collective-permute-start(bf16[144,1536]{1,0:T(8,128)(2,1)} %get-tuple-element.44.after.refs_0_), channel_id=1, source_target_pairs={{0,2},{1,3},{2,0},{3,1},{4,6},{5,7},{6,4},{7,5},{8,10},{9,11},{10,... | collective-permute-start | bytes 1327112 | tf_op jit(solution)/shard_map/ppermute | solution.py:409
  10.0 31.4 %collective-permute-start.3 = (bf16[144,1536]{1,0:T(8,128)(2,1)}, bf16[144,1536]{1,0:T(8,128)(2,1)S(1)}, u32[]{:S(2)}, u32[]{:S(2)}) collective-permute-start(bf16[144,1536]{1,0:T(8,128)(2,1)} %get-tuple-element.44.after.refs_0_), channel_id=1, source_target_pairs={{0,1},{1,0},{2,3},{3,2},{4,5},{5,4},{6,7},{7,6},{8,9},{9,8},{10,11... | collective-permute-start | bytes 1327112 | tf_op jit(solution)/shard_map/ppermute | solution.py:409
  10.0 29.8 %collective-permute-start.7 = (bf16[144,1536]{1,0:T(8,128)(2,1)}, bf16[144,1536]{1,0:T(8,128)(2,1)S(1)}, u32[]{:S(2)}, u32[]{:S(2)}) collective-permute-start(bf16[144,1536]{1,0:T(8,128)(2,1)} %get-tuple-element.47), channel_id=1, source_target_pairs={{0,8},{1,9},{2,10},{3,11},{4,12},{5,13},{6,14},{7,15},{8,0},{9,1},... | collective-permute-start | bytes 1327112 | tf_op jit(solution)/shard_map/ppermute | solution.py:409
  21.8 10.7 %collective-permute-start.2 = (bf16[144,1536]{1,0:T(8,128)(2,1)S(1)}, bf16[144,1536]{1,0:T(8,128)(2,1)S(1)}, u32[]{:S(2)}, u32[]{:S(2)}) collective-permute-start(bf16[144,1536]{1,0:T(8,128)(2,1)S(1)} %collective-permute-done.1.refs_2_), channel_id=1, source_target_pairs={{0,2},{1,3},{2,0},{3,1},{4,6},{5,7},{6,4},{7,5},{8,10},{9,11},{10,... | collective-permute-start | bytes 1327112 | tf_op jit(solution)/shard_map/ppermute | solution.py:409
  31.9 11.0 %collective-permute-start.4 = (bf16[144,1536]{1,0:T(8,128)(2,1)S(1)}, bf16[144,1536]{1,0:T(8,128)(2,1)S(1)}, u32[]{:S(2)}, u32[]{:S(2)}) collective-permute-start(bf16[144,1536]{1,0:T(8,128)(2,1)S(1)} %shard_map.95.refs_1_), channel_id=1, source_target_pairs={{0,1},{1,0},{2,3},{3,2},{4,5},{5,4},{6,7},{7,6},{8,9},{9,8},{10,11... | collective-permute-start | bytes 1327112 | tf_op jit(solution)/shard_map/ppermute | solution.py:409
  32.0 10.9 %collective-permute-start.5 = (bf16[144,1536]{1,0:T(8,128)(2,1)S(1)}, bf16[144,1536]{1,0:T(8,128)(2,1)S(1)}, u32[]{:S(2)}, u32[]{:S(2)}) collective-permute-start(bf16[144,1536]{1,0:T(8,128)(2,1)S(1)} %collective-permute-done.1.refs_2_), channel_id=1, source_target_pairs={{0,1},{1,0},{2,3},{3,2},{4,5},{5,4},{6,7},{7,6},{8,9},{9,8},{10,11... | collective-permute-start | bytes 1327112 | tf_op jit(solution)/shard_map/ppermute | solution.py:409
  32.5 10.5 %collective-permute-start.6 = (bf16[144,1536]{1,0:T(8,128)(2,1)S(1)}, bf16[144,1536]{1,0:T(8,128)(2,1)S(1)}, u32[]{:S(2)}, u32[]{:S(2)}) collective-permute-start(bf16[144,1536]{1,0:T(8,128)(2,1)S(1)} %shard_map.96.refs_3_), channel_id=1, source_target_pairs={{0,1},{1,0},{2,3},{3,2},{4,5},{5,4},{6,7},{7,6},{8,9},{9,8},{10,11... | collective-permute-start | bytes 1327112 | tf_op jit(solution)/shard_map/ppermute | solution.py:409
  39.8 12.5 %collective-permute-start.8 = (bf16[144,1536]{1,0:T(8,128)(2,1)S(1)}, bf16[144,1536]{1,0:T(8,128)(2,1)S(1)}, u32[]{:S(2)}, u32[]{:S(2)}) collective-permute-start(bf16[144,1536]{1,0:T(8,128)(2,1)S(1)} %shard_map.97.refs_1_.refs_0_), channel_id=1, source_target_pairs={{0,2},{1,3},{2,0},{3,1},{4,6},{5,7},{6,4},{7,5},{8,10},{9,11},{10,... | collective-permute-start | bytes 1327112 | tf_op jit(solution)/shard_map/ppermute | solution.py:409
  41.3 11.9 %collective-permute-start.9 = (bf16[144,1536]{1,0:T(8,128)(2,1)S(1)}, bf16[144,1536]{1,0:T(8,128)(2,1)S(1)}, u32[]{:S(2)}, u32[]{:S(2)}) collective-permute-start(bf16[144,1536]{1,0:T(8,128)(2,1)S(1)} %shard_map.98.refs_10_), channel_id=1, source_target_pairs={{0,12},{1,13},{2,14},{3,15},{4,0},{5,1},{6,2},{7,3},{8,4},{9,5},{1... | collective-permute-start | bytes 1327112 | tf_op jit(solution)/shard_map/ppermute | solution.py:409
  43.0 16.3 %collective-permute-start.12 = (bf16[144,1536]{1,0:T(8,128)(2,1)S(1)}, bf16[144,1536]{1,0:T(8,128)(2,1)S(1)}, u32[]{:S(2)}, u32[]{:S(2)}) collective-permute-start(bf16[144,1536]{1,0:T(8,128)(2,1)S(1)} %shard_map.97.refs_1_.refs_0_), channel_id=1, source_target_pairs={{0,1},{1,0},{2,3},{3,2},{4,5},{5,4},{6,7},{7,6},{8,9},{9,8},{10,11... | collective-permute-start | bytes 1327112 | tf_op jit(solution)/shard_map/ppermute | solution.py:409
  53.2 12.9 %collective-permute-start.15 = (bf16[144,1536]{1,0:T(8,128)(2,1)S(1)}, bf16[144,1536]{1,0:T(8,128)(2,1)S(1)}, u32[]{:S(2)}, u32[]{:S(2)}) collective-permute-start(bf16[144,1536]{1,0:T(8,128)(2,1)S(1)} %shard_map.101.refs_1_.refs_0_), channel_id=1, source_target_pairs={{0,2},{1,3},{2,0},{3,1},{4,6},{5,7},{6,4},{7,5},{8,10},{9,11},{10,... | collective-permute-start | bytes 1327112 | tf_op jit(solution)/shard_map/ppermute | solution.py:409
  58.8 14.8 %collective-permute-start.16 = (bf16[144,1536]{1,0:T(8,128)(2,1)S(1)}, bf16[144,1536]{1,0:T(8,128)(2,1)S(1)}, u32[]{:S(2)}, u32[]{:S(2)}) collective-permute-start(bf16[144,1536]{1,0:T(8,128)(2,1)S(1)} %shard_map.101.refs_1_.refs_0_), channel_id=1, source_target_pairs={{0,1},{1,0},{2,3},{3,2},{4,5},{5,4},{6,7},{7,6},{8,9},{9,8},{10,11... | collective-permute-start | bytes 1327112 | tf_op jit(solution)/shard_map/ppermute | solution.py:409
  66.2 20.5 %collective-permute-start.10 = (bf16[144,1536]{1,0:T(8,128)(2,1)S(1)}, bf16[144,1536]{1,0:T(8,128)(2,1)S(1)}, u32[]{:S(2)}, u32[]{:S(2)}) collective-permute-start(bf16[144,1536]{1,0:T(8,128)(2,1)S(1)} %get-tuple-element.51), channel_id=1, source_target_pairs={{0,1},{1,0},{2,3},{3,2},{4,5},{5,4},{6,7},{7,6},{8,9},{9,8},{10,11... | collective-permute-start | bytes 1327112 | tf_op jit(solution)/shard_map/ppermute | solution.py:409
  66.8 20.0 %collective-permute-start.14 = (bf16[144,1536]{1,0:T(8,128)(2,1)S(1)}, bf16[144,1536]{1,0:T(8,128)(2,1)S(1)}, u32[]{:S(2)}, u32[]{:S(2)}) collective-permute-start(bf16[144,1536]{1,0:T(8,128)(2,1)S(1)} %shard_map.104.refs_1_), channel_id=1, source_target_pairs={{0,2},{1,3},{2,0},{3,1},{4,6},{5,7},{6,4},{7,5},{8,10},{9,11},{10,... | collective-permute-start | bytes 1327112 | tf_op jit(solution)/shard_map/ppermute | solution.py:409
  73.6 16.0 %collective-permute-start.20 = (bf16[72,1536]{1,0:T(8,128)(2,1)S(1)}, bf16[72,1536]{1,0:T(8,128)(2,1)S(1)}, u32[]{:S(2)}, u32[]{:S(2)}) collective-permute-start(bf16[72,1536]{1,0:T(8,128)(2,1)S(1)} %get-tuple-element.66), channel_id=1, source_target_pairs={{0,1},{1,0},{2,3},{3,2},{4,5},{5,4},{6,7},{7,6},{8,9},{9,8},{10,11... | collective-permute-start | bytes 663560 | tf_op jit(solution)/shard_map/ppermute | solution.py:409
  86.9 10.7 %collective-permute-start.19 = (bf16[72,1536]{1,0:T(8,128)(2,1)S(1)}, bf16[72,1536]{1,0:T(8,128)(2,1)S(1)}, u32[]{:S(2)}, u32[]{:S(2)}) collective-permute-start(bf16[72,1536]{1,0:T(8,128)(2,1)S(1)} %get-tuple-element.64), channel_id=1, source_target_pairs={{0,12},{1,13},{2,14},{3,15},{4,0},{5,1},{6,2},{7,3},{8,4},{9,5},{1... | collective-permute-start | bytes 663560 | tf_op jit(solution)/shard_map/ppermute | solution.py:409
  89.4 17.4 %collective-permute-start.23 = (bf16[72,1536]{1,0:T(8,128)(2,1)S(1)}, bf16[72,1536]{1,0:T(8,128)(2,1)S(1)}, u32[]{:S(2)}, u32[]{:S(2)}) collective-permute-start(bf16[72,1536]{1,0:T(8,128)(2,1)S(1)} %get-tuple-element.68), channel_id=1, source_target_pairs={{0,1},{1,0},{2,3},{3,2},{4,5},{5,4},{6,7},{7,6},{8,9},{9,8},{10,11... | collective-permute-start | bytes 663560 | tf_op jit(solution)/shard_map/ppermute | solution.py:409
  94.3 15.4 %collective-permute-start.22 = (bf16[72,1536]{1,0:T(8,128)(2,1)S(1)}, bf16[72,1536]{1,0:T(8,128)(2,1)S(1)}, u32[]{:S(2)}, u32[]{:S(2)}) collective-permute-start(bf16[72,1536]{1,0:T(8,128)(2,1)S(1)} %shard_map.111.refs_6_.refs_3_), channel_id=1, source_target_pairs={{0,8},{1,9},{2,10},{3,11},{4,12},{5,13},{6,14},{7,15},{8,0},{9,1},... | collective-permute-start | bytes 663560 | tf_op jit(solution)/shard_map/ppermute | solution.py:409
  95.5 14.0 %collective-permute-start.25 = (bf16[72,1536]{1,0:T(8,128)(2,1)S(1)}, bf16[72,1536]{1,0:T(8,128)(2,1)S(1)}, u32[]{:S(2)}, u32[]{:S(2)}) collective-permute-start(bf16[72,1536]{1,0:T(8,128)(2,1)S(1)} %shard_map.113.refs_7_), channel_id=1, source_target_pairs={{0,2},{1,3},{2,0},{3,1},{4,6},{5,7},{6,4},{7,5},{8,10},{9,11},{10,... | collective-permute-start | bytes 663560 | tf_op jit(solution)/shard_map/ppermute | solution.py:409
  104.8 15.2 %collective-permute-start.29 = (f32[1,3072]{1,0:T(1,128)S(1)}, f32[1,3072]{1,0:T(1,128)S(1)}, u32[]{:S(2)}, u32[]{:S(2)}) collective-permute-start(f32[1,3072]{1,0:T(1,128)S(1)} %shard_map.118.refs_4_), channel_id=1, source_target_pairs={{0,4},{1,5},{2,6},{3,7},{4,8},{5,9},{6,10},{7,11},{8,12},{9,13},{1... | collective-permute-start | bytes 36872 | tf_op jit(solution)/shard_map/ppermute | solution.py:409
  106.5 13.5 %collective-permute-start.30 = (f32[1,3072]{1,0:T(1,128)S(1)}, f32[1,3072]{1,0:T(1,128)S(1)}, u32[]{:S(2)}, u32[]{:S(2)}) collective-permute-start(f32[1,3072]{1,0:T(1,128)S(1)} %shard_map.118.refs_4_), channel_id=1, source_target_pairs={{0,8},{1,9},{2,10},{3,11},{4,12},{5,13},{6,14},{7,15},{8,0},{9,1},... | collective-permute-start | bytes 36872 | tf_op jit(solution)/shard_map/ppermute | solution.py:409
  106.7 13.3 %collective-permute-start.31 = (f32[1,3072]{1,0:T(1,128)S(1)}, f32[1,3072]{1,0:T(1,128)S(1)}, u32[]{:S(2)}, u32[]{:S(2)}) collective-permute-start(f32[1,3072]{1,0:T(1,128)S(1)} %shard_map.118.refs_4_), channel_id=1, source_target_pairs={{0,12},{1,13},{2,14},{3,15},{4,0},{5,1},{6,2},{7,3},{8,4},{9,5},{1... | collective-permute-start | bytes 36872 | tf_op jit(solution)/shard_map/ppermute | solution.py:409
  109.6 10.4 %collective-permute-start.26 = (bf16[72,1536]{1,0:T(8,128)(2,1)S(1)}, bf16[72,1536]{1,0:T(8,128)(2,1)S(1)}, u32[]{:S(2)}, u32[]{:S(2)}) collective-permute-start(bf16[72,1536]{1,0:T(8,128)(2,1)S(1)} %shard_map.115.refs_6_), channel_id=1, source_target_pairs={{0,4},{1,5},{2,6},{3,7},{4,8},{5,9},{6,10},{7,11},{8,12},{9,13},{1... | collective-permute-start | bytes 663560 | tf_op jit(solution)/shard_map/ppermute | solution.py:409
  (21 other events, 183.7 us)

commit v4 on v3

--- a/solution.py
+++ b/solution.py
@@ -153,6 +153,24 @@
     )(value, *after)
 
 
+def turn_kernel(down, after, out):
+    out[...] = down[...].T
+
+
+def turned(down, after):
+    hidden, width = down.shape
+    tile = 256
+    return pl.pallas_call(
+        turn_kernel,
+        grid=(hidden // tile,),
+        in_specs=[pl.BlockSpec((tile, width), lambda j: (j, 0)), HBM],
+        out_specs=pl.BlockSpec((width, tile), lambda j: (0, j)),
+        out_shape=jax.ShapeDtypeStruct((width, hidden), BF16),
+        compiler_params=params(0, 0, 9 << 20),
+        cost_estimate=cost(8e9, 8),
+    )(down, after)
+
+
 def warm_kernel(up, down, after, out):
     out[...] = jnp.zeros_like(out)
 
@@ -206,7 +224,7 @@
     for t in range(hidden // tile):
         cols = slice(t * tile, (t + 1) * tile)
         preact = jnp.dot(n_v[...], up[:, cols], preferred_element_type=F32)
-        grad_act = lax.dot_general(g_v[...], down[cols, :], NT, preferred_element_type=F32)
+        grad_act = jnp.dot(g_v[...], down[:, cols], preferred_element_type=F32)
         sig = jax.nn.sigmoid(preact)
         act_v[:, cols] = (preact * sig).astype(BF16)
         pre_v[:, cols] = (grad_act * (sig * (1.0 + preact * (1.0 - sig)))).astype(BF16)
@@ -432,7 +450,7 @@
     acts, pres, norms, grads, gain_parts, returned = [], [], [], [], [], {}
 
     def work(rows, cross, after):
-        normed, grad, act, pre = forward(rows + cross, up_weight, down_weight, after)
+        normed, grad, act, pre = forward(rows + cross, up_weight, down_turned, after)
         acts.append(act)
         pres.append(pre)
         norms.append(normed)
@@ -459,8 +477,9 @@
         row = [x] + [gated(to_pair(x, j), after) for j in range(1, pairs)]
         return row, [to_core(y) for y in row]
 
+    down_turned = turned(down_weight, packed[0])
     one, two = to_plane(packed[1], 1), to_plane(packed[2], 2)
-    warm = warmed(up_weight, down_weight, packed[0])
+    warm = warmed(up_weight, down_turned, packed[0])
     row0, cross0 = spread(packed[0], [warm])
     row1, cross1 = spread(one, [warm])
     two = gated(two, [warm])

time: 123 us -> 119 us (0.967)
  local copies, waits for them, and re-layouts: 8.43 us -> 4.83 us
    unnamed x26 -> x22, local copies, waits for them, and re-layouts: 8.43 us -> 4.83 us
    pallas_call x0 -> x1, Pallas kernels: none -> 3.51 us  [turned(): pl.pallas_call(turn_kernel, grid=(hidden // tile,), in_specs=[pl.BlockSpe...]
    pallas_call x3, Pallas kernels: 22.8 us -> 19.5 us  [forward(): pl.pallas_call(functools.partial(forward_kernel, len(blocks), tile, len(a...]
  transfers between devices with their start and end apart: 32 -> 32, of which waited for: 3 -> 5; matrix products, arithmetic and copies ran while one was open for 0% -> 0% of each run, Pallas kernels for 49% -> 51%
where the time goes in v4:
time: 119 us
  Pallas kernels  67.6 us (57%)
  starting transfers between devices  27.8 us (23%)
  waiting for transfers between devices  17.7 us (15%)
  local copies, waits for them, and re-layouts  4.83 us (4%)
    ppermute x32, starting transfers between devices, moved(): return lax.ppermute(x, 'seq', [(i, to(i)) for i in range(seq)])  27.8 us
    pallas_call x3, Pallas kernels, weight_grad(): pl.pallas_call(functools.partial(weight_kernel, len(lefts), tile), grid=(...  21.4 us
    pallas_call x3, Pallas kernels, forward(): pl.pallas_call(functools.partial(forward_kernel, len(blocks), tile, len(a...  19.5 us
    ppermute x32, waiting for transfers between devices, moved(): return lax.ppermute(x, 'seq', [(i, to(i)) for i in range(seq)])  17.7 us
    pallas_call x3, Pallas kernels, backward(): pl.pallas_call(functools.partial(backward_kernel, shifts, pairs, tile, le...  15.1 us
    unnamed x22, local copies, waits for them, and re-layouts  4.83 us
    pallas_call x1, Pallas kernels, local(): pl.pallas_call(pack_kernel, in_specs=[SMEM, HBM, HBM, VMEM, HBM], out_sha...  4.71 us
    pallas_call x1, Pallas kernels, turned(): pl.pallas_call(turn_kernel, grid=(hidden // tile,), in_specs=[pl.BlockSpe...  3.51 us
  transfers between devices with their start and end apart: 32, of which 5 were waited for; matrix products, arithmetic and copies ran while one was open for 0% of the time, Pallas kernels for 51%

profile of v4, /device:TPU:0, one launch (start us, length us, event | category | flops | bytes accessed | tf_op | source)
XLA Modules:
  0.0 119.0 jit_solution(1542469502251385098)
XLA Ops:
  0.6 4.7 %shard_map.93 = (bf16[144,1536]{1,0:T(8,128)(2,1)}, bf16[144,1536]{1,0:T(8,128)(2,1)}, bf16[144,1536]{1,0:T(8,128)(2,1)}, bf16[144,1536]{1,0:T(8,128)(2,1)}) custom-call(s32[1]{0:T(128)} %bitcast.plane_ref, bf16[128,3072]{1,0:T(8,128)(2,1)} %tokens_ref.1, bf16[128,3072]{1,0:T(8,128)(2,1)} %grad_ref.1, s32[1,128]{1,0:T(1,128)} %bitcast.4, f32[4,3072]{1,0:T(4,128)} %gain_ref.1), custom_call_target="tpu_custom_call" | custom-call | tf_op jit(solution)/shard_map/pallas_call | solution.py:438
  5.4 3.1 %collective-permute-start.1 = (bf16[144,1536]{1,0:T(8,128)(2,1)}, bf16[144,1536]{1,0:T(8,128)(2,1)S(1)}, u32[]{:S(2)}, u32[]{:S(2)}) collective-permute-start(bf16[144,1536]{1,0:T(8,128)(2,1)} %get-tuple-element.45), channel_id=1, source_target_pairs={{0,4},{1,5},{2,6},{3,7},{4,8},{5,9},{6,10},{7,11},{8,12},{9,13},{1... | collective-permute-start | bytes 1327112 | tf_op jit(solution)/shard_map/ppermute | solution.py:427
  8.4 1.5 %collective-permute-start = (bf16[144,1536]{1,0:T(8,128)(2,1)}, bf16[144,1536]{1,0:T(8,128)(2,1)S(1)}, u32[]{:S(2)}, u32[]{:S(2)}) collective-permute-start(bf16[144,1536]{1,0:T(8,128)(2,1)} %get-tuple-element.44.after.refs_0_), channel_id=1, source_target_pairs={{0,2},{1,3},{2,0},{3,1},{4,6},{5,7},{6,4},{7,5},{8,10},{9,11},{10,... | collective-permute-start | bytes 1327112 | tf_op jit(solution)/shard_map/ppermute | solution.py:427
  10.0 2.7 %collective-permute-start.7 = (bf16[144,1536]{1,0:T(8,128)(2,1)}, bf16[144,1536]{1,0:T(8,128)(2,1)S(1)}, u32[]{:S(2)}, u32[]{:S(2)}) collective-permute-start(bf16[144,1536]{1,0:T(8,128)(2,1)} %get-tuple-element.47), channel_id=1, source_target_pairs={{0,8},{1,9},{2,10},{3,11},{4,12},{5,13},{6,14},{7,15},{8,0},{9,1},... | collective-permute-start | bytes 1327112 | tf_op jit(solution)/shard_map/ppermute | solution.py:427
  12.6 3.8 %copy-done = bf16[1536,3072]{1,0:T(8,128)(2,1)S(1)} copy-done((bf16[1536,3072]{1,0:T(8,128)(2,1)S(1)}, bf16[1536,3072]{1,0:T(8,128)(2,1)}, u32[]{:S(2)}) %copy-start) | copy-done | bytes 9437208
  17.4 3.5 %shard_map.94.down.refs_9_.refs_5_ = bf16[3072,1536]{1,0:T(8,128)(2,1)S(1)} custom-call(bf16[1536,3072]{1,0:T(8,128)(2,1)S(1)} %copy-done, bf16[144,1536]{1,0:T(8,128)(2,1)S(1)} %copy-done.4), custom_call_target="tpu_custom_call" | custom-call | flops 80000 | tf_op jit(solution)/shard_map/pallas_call | solution.py:163
  21.8 1.8 %collective-permute-start.2 = (bf16[144,1536]{1,0:T(8,128)(2,1)S(1)}, bf16[144,1536]{1,0:T(8,128)(2,1)S(1)}, u32[]{:S(2)}, u32[]{:S(2)}) collective-permute-start(bf16[144,1536]{1,0:T(8,128)(2,1)S(1)} %collective-permute-done.1.refs_2_), channel_id=1, source_target_pairs={{0,2},{1,3},{2,0},{3,1},{4,6},{5,7},{6,4},{7,5},{8,10},{9,11},{10,... | collective-permute-start | bytes 1327112 | tf_op jit(solution)/shard_map/ppermute | solution.py:427
  24.1 9.5 %collective-permute-done.2.refs_0_ = bf16[144,1536]{1,0:T(8,128)(2,1)S(1)} collective-permute-done((bf16[144,1536]{1,0:T(8,128)(2,1)S(1)}, bf16[144,1536]{1,0:T(8,128)(2,1)S(1)}, u32[]{:S(2)}, u32[]{:S(2)}) %collective-permute-start.2) | collective-permute-done | bytes 442400 | tf_op jit(solution)/shard_map/ppermute | solution.py:427
  33.6 6.2 %collective-permute-done.7.refs_0_ = bf16[144,1536]{1,0:T(8,128)(2,1)S(1)} collective-permute-done((bf16[144,1536]{1,0:T(8,128)(2,1)}, bf16[144,1536]{1,0:T(8,128)(2,1)S(1)}, u32[]{:S(2)}, u32[]{:S(2)}) %collective-permute-start.7) | collective-permute-done | bytes 442400 | tf_op jit(solution)/shard_map/ppermute | solution.py:427
  39.8 1.5 %collective-permute-start.8 = (bf16[144,1536]{1,0:T(8,128)(2,1)S(1)}, bf16[144,1536]{1,0:T(8,128)(2,1)S(1)}, u32[]{:S(2)}, u32[]{:S(2)}) collective-permute-start(bf16[144,1536]{1,0:T(8,128)(2,1)S(1)} %shard_map.98.refs_1_.refs_0_), channel_id=1, source_target_pairs={{0,2},{1,3},{2,0},{3,1},{4,6},{5,7},{6,4},{7,5},{8,10},{9,11},{10,... | collective-permute-start | bytes 1327112 | tf_op jit(solution)/shard_map/ppermute | solution.py:427
  41.3 1.6 %collective-permute-start.9 = (bf16[144,1536]{1,0:T(8,128)(2,1)S(1)}, bf16[144,1536]{1,0:T(8,128)(2,1)S(1)}, u32[]{:S(2)}, u32[]{:S(2)}) collective-permute-start(bf16[144,1536]{1,0:T(8,128)(2,1)S(1)} %shard_map.99.refs_10_), channel_id=1, source_target_pairs={{0,12},{1,13},{2,14},{3,15},{4,0},{5,1},{6,2},{7,3},{8,4},{9,5},{1... | collective-permute-start | bytes 1327112 | tf_op jit(solution)/shard_map/ppermute | solution.py:427
  43.0 9.4 %shard_map.100 = (bf16[288,3072]{1,0:T(8,128)(2,1)S(1)}, bf16[288,3072]{1,0:T(8,128)(2,1)S(1)}, bf16[288,1536]{1,0:T(8,128)(2,1)S(1)}, bf16[288,1536]{1,0:T(8,128)(2,1)S(1)}) custom-call(bf16[144,1536]{1,0:T(8,128)(2,1)S(1)} %copy-done.5, bf16[144,1536]{1,0:T(8,128)(2,1)S(1)} %shard_map.96.refs_1_, bf16[144,1536]{1,0:T(8,128)(2,1)S(1)} %collective-permute-done.1.refs_2_, ...), custom_call_target="tpu_custom_call" | custom-call | flops 54358 | bytes 94 | tf_op jit(solution)/shard_map/pallas_call | solution.py:249
  53.7 4.9 %shard_map.103 = (bf16[144,1536]{1,0:T(8,128)(2,1)S(1)}, bf16[144,1536]{1,0:T(8,128)(2,1)S(1)}, bf16[144,1536]{1,0:T(8,128)(2,1)S(1)}, bf16[144,1536]{1,0:T(8,128)(2,1)S(1)}, f32[1,3072]{1,0:T(1,128)S(1)}) custom-call(bf16[288,1536]{1,0:T(8,128)(2,1)S(1)} %get-tuple-element.48.refs_1_.pre.refs_3_, bf16[3072,1536]{1,0:T(8,128)(2,1)S(1)} %bitcast.3, ...), custom_call_target="tpu_custom_call" | custom-call | flops 2717908992 | bytes 9437184 | tf_op jit(solution)/shard_map/pallas_call | solution.py:325
  59.1 5.1 %shard_map.104 = (bf16[144,3072]{1,0:T(8,128)(2,1)S(1)}, bf16[144,3072]{1,0:T(8,128)(2,1)S(1)}, bf16[144,1536]{1,0:T(8,128)(2,1)S(1)}, bf16[144,1536]{1,0:T(8,128)(2,1)S(1)}) custom-call(bf16[144,1536]{1,0:T(8,128)(2,1)S(1)} %shard_map.98.refs_1_.refs_0_, bf16[144,1536]{1,0:T(8,128)(2,1)S(1)} %shard_map.101.refs_0_.refs_1_, ...), custom_call_target="tpu_custom_call" | custom-call | flops 27179 | bytes 94 | tf_op jit(solution)/shard_map/pallas_call | solution.py:249
  66.7 5.2 %shard_map.107 = (bf16[72,1536]{1,0:T(8,128)(2,1)S(1)}, bf16[72,1536]{1,0:T(8,128)(2,1)S(1)}, bf16[72,1536]{1,0:T(8,128)(2,1)S(1)}, bf16[72,1536]{1,0:T(8,128)(2,1)S(1)}, f32[1,3072]{1,0:T(1,128)S(1)}) custom-call(bf16[144,1536]{1,0:T(8,128)(2,1)S(1)} %get-tuple-element.55.refs_0_.refs_1_.pre.refs_4_, bf16[3072,1536]{1,0:T(8,128)(2,1)S(1)} %bitcast.3, ...), custom_call_target="tpu_custom_call" | custom-call | flops 13589 | bytes 94 | tf_op jit(solution)/shard_map/pallas_call | solution.py:325
  72.6 5.1 %shard_map.108 = (bf16[144,3072]{1,0:T(8,128)(2,1)S(1)}, bf16[144,3072]{1,0:T(8,128)(2,1)S(1)}, bf16[144,1536]{1,0:T(8,128)(2,1)S(1)}, bf16[144,1536]{1,0:T(8,128)(2,1)S(1)}) custom-call(bf16[144,1536]{1,0:T(8,128)(2,1)S(1)} %shard_map.102.refs_1_.refs_0_, bf16[144,1536]{1,0:T(8,128)(2,1)S(1)} %shard_map.106.refs_0_.refs_1_, ...), custom_call_target="tpu_custom_call" | custom-call | flops 27179 | bytes 94 | tf_op jit(solution)/shard_map/pallas_call | solution.py:249
  78.9 5.0 %shard_map.110 = (bf16[72,1536]{1,0:T(8,128)(2,1)S(1)}, bf16[72,1536]{1,0:T(8,128)(2,1)S(1)}, bf16[72,1536]{1,0:T(8,128)(2,1)S(1)}, bf16[72,1536]{1,0:T(8,128)(2,1)S(1)}, f32[1,3072]{1,0:T(1,128)S(1)}) custom-call(bf16[144,1536]{1,0:T(8,128)(2,1)S(1)} %get-tuple-element.58.refs_0_.pre.refs_5_, bf16[3072,1536]{1,0:T(8,128)(2,1)S(1)} %bitcast.3, ...), custom_call_target="tpu_custom_call" | custom-call | flops 13589 | bytes 94 | tf_op jit(solution)/shard_map/pallas_call | solution.py:325
  84.2 1.6 %collective-permute-start.19 = (bf16[72,1536]{1,0:T(8,128)(2,1)S(1)}, bf16[72,1536]{1,0:T(8,128)(2,1)S(1)}, u32[]{:S(2)}, u32[]{:S(2)}) collective-permute-start(bf16[72,1536]{1,0:T(8,128)(2,1)S(1)} %get-tuple-element.64), channel_id=1, source_target_pairs={{0,12},{1,13},{2,14},{3,15},{4,0},{5,1},{6,2},{7,3},{8,4},{9,5},{1... | collective-permute-start | bytes 663560 | tf_op jit(solution)/shard_map/ppermute | solution.py:427
  86.5 4.2 %shard_map.113 = (bf16[3072,1536]{1,0:T(8,128)(2,1)}, f32[8,128]{1,0:T(8,128)S(1)}) custom-call(bf16[288,3072]{1,0:T(8,128)(2,1)S(1)} %get-tuple-element.49.normed.refs_0_, bf16[144,3072]{1,0:T(8,128)(2,1)S(1)} %get-tuple-element.56.normed.refs_1_, bf16[144,3072]{1,0:T(8,128)(2,1)S(1)} %get-tuple-element.59.normed.refs_2_, ...), custom_call_target="tpu_custom_call" | custom-call | flops 1811939328 | bytes 3145728 | tf_op jit(solution)/shard_map/pallas_call | solution.py:403
  93.2 7.2 %shard_map.115 = (bf16[3072,1536]{1,0:T(8,128)(2,1)}, f32[8,128]{1,0:T(8,128)S(1)}) custom-call(bf16[288,3072]{1,0:T(8,128)(2,1)S(1)} %get-tuple-element.49.normed.refs_0_, bf16[144,3072]{1,0:T(8,128)(2,1)S(1)} %get-tuple-element.56.normed.refs_1_, bf16[144,3072]{1,0:T(8,128)(2,1)S(1)} %get-tuple-element.59.normed.refs_2_, ...), custom_call_target="tpu_custom_call", output_to_operand_aliasing={{0}: (6, {})} | custom-call | flops 3623878656 | bytes 6291456 | tf_op jit(solution)/shard_map/pallas_call | solution.py:403
  101.7 1.8 %collective-permute-start.30 = (f32[1,3072]{1,0:T(1,128)S(1)}, f32[1,3072]{1,0:T(1,128)S(1)}, u32[]{:S(2)}, u32[]{:S(2)}) collective-permute-start(f32[1,3072]{1,0:T(1,128)S(1)} %shard_map.119.refs_4_), channel_id=1, source_target_pairs={{0,8},{1,9},{2,10},{3,11},{4,12},{5,13},{6,14},{7,15},{8,0},{9,1},... | collective-permute-start | bytes 36872 | tf_op jit(solution)/shard_map/ppermute | solution.py:427
  103.5 2.4 %collective-permute-start.31 = (f32[1,3072]{1,0:T(1,128)S(1)}, f32[1,3072]{1,0:T(1,128)S(1)}, u32[]{:S(2)}, u32[]{:S(2)}) collective-permute-start(f32[1,3072]{1,0:T(1,128)S(1)} %shard_map.119.refs_4_), channel_id=1, source_target_pairs={{0,12},{1,13},{2,14},{3,15},{4,0},{5,1},{6,2},{7,3},{8,4},{9,5},{1... | collective-permute-start | bytes 36872 | tf_op jit(solution)/shard_map/ppermute | solution.py:427
  106.1 10.0 %shard_map.121 = (bf16[1536,3072]{1,0:T(8,128)(2,1)}, f32[8,128]{1,0:T(8,128)}) custom-call(bf16[288,1536]{1,0:T(8,128)(2,1)S(1)} %get-tuple-element.77.refs_0_, bf16[144,1536]{1,0:T(8,128)(2,1)S(1)} %get-tuple-element.78.refs_1_, bf16[144,1536]{1,0:T(8,128)(2,1)S(1)} %get-tuple-element.79.refs_2_, bf16[288,3072]{1,0:T(8,128)(2,1)S(1)} %get-tuple-element.80.refs_3_, ...), custom_call_target="tpu_custom_call" | custom-call | flops 5435817984 | bytes 9437184 | tf_op jit(solution)/shard_map/pallas_call | solution.py:403
  116.2 2.8 %shard_map.120 = (bf16[128,3072]{1,0:T(8,128)(2,1)}, f32[4,3072]{1,0:T(4,128)}) custom-call(s32[1]{0:T(128)} %bitcast.plane_ref, bf16[128,3072]{1,0:T(8,128)(2,1)S(1)} %copy-done.1, bf16[128,3072]{1,0:T(8,128)(2,1)S(1)} %copy-done.2, s32[1,128]{1,0:T(1,128)S(1)} %bitcast.5, f32[4,3072]{1,0:T(4,128)S(1)} %copy-done.6, ...), custom_call_target="tpu_custom_call" | custom-call | tf_op jit(solution)/shard_map/pallas_call | solution.py:512
  (92 shorter events, 13.5 us)
Async XLA Ops:
  5.4 16.4 %collective-permute-start.1 = (bf16[144,1536]{1,0:T(8,128)(2,1)}, bf16[144,1536]{1,0:T(8,128)(2,1)S(1)}, u32[]{:S(2)}, u32[]{:S(2)}) collective-permute-start(bf16[144,1536]{1,0:T(8,128)(2,1)} %get-tuple-element.45), channel_id=1, source_target_pairs={{0,4},{1,5},{2,6},{3,7},{4,8},{5,9},{6,10},{7,11},{8,12},{9,13},{1... | collective-permute-start | bytes 1327112 | tf_op jit(solution)/shard_map/ppermute | solution.py:427
  8.4 15.1 %collective-permute-start = (bf16[144,1536]{1,0:T(8,128)(2,1)}, bf16[144,1536]{1,0:T(8,128)(2,1)S(1)}, u32[]{:S(2)}, u32[]{:S(2)}) collective-permute-start(bf16[144,1536]{1,0:T(8,128)(2,1)} %get-tuple-element.44.after.refs_0_), channel_id=1, source_target_pairs={{0,2},{1,3},{2,0},{3,1},{4,6},{5,7},{6,4},{7,5},{8,10},{9,11},{10,... | collective-permute-start | bytes 1327112 | tf_op jit(solution)/shard_map/ppermute | solution.py:427
  10.0 31.4 %collective-permute-start.3 = (bf16[144,1536]{1,0:T(8,128)(2,1)}, bf16[144,1536]{1,0:T(8,128)(2,1)S(1)}, u32[]{:S(2)}, u32[]{:S(2)}) collective-permute-start(bf16[144,1536]{1,0:T(8,128)(2,1)} %get-tuple-element.44.after.refs_0_), channel_id=1, source_target_pairs={{0,1},{1,0},{2,3},{3,2},{4,5},{5,4},{6,7},{7,6},{8,9},{9,8},{10,11... | collective-permute-start | bytes 1327112 | tf_op jit(solution)/shard_map/ppermute | solution.py:427
  10.0 29.8 %collective-permute-start.7 = (bf16[144,1536]{1,0:T(8,128)(2,1)}, bf16[144,1536]{1,0:T(8,128)(2,1)S(1)}, u32[]{:S(2)}, u32[]{:S(2)}) collective-permute-start(bf16[144,1536]{1,0:T(8,128)(2,1)} %get-tuple-element.47), channel_id=1, source_target_pairs={{0,8},{1,9},{2,10},{3,11},{4,12},{5,13},{6,14},{7,15},{8,0},{9,1},... | collective-permute-start | bytes 1327112 | tf_op jit(solution)/shard_map/ppermute | solution.py:427
  21.8 11.8 %collective-permute-start.2 = (bf16[144,1536]{1,0:T(8,128)(2,1)S(1)}, bf16[144,1536]{1,0:T(8,128)(2,1)S(1)}, u32[]{:S(2)}, u32[]{:S(2)}) collective-permute-start(bf16[144,1536]{1,0:T(8,128)(2,1)S(1)} %collective-permute-done.1.refs_2_), channel_id=1, source_target_pairs={{0,2},{1,3},{2,0},{3,1},{4,6},{5,7},{6,4},{7,5},{8,10},{9,11},{10,... | collective-permute-start | bytes 1327112 | tf_op jit(solution)/shard_map/ppermute | solution.py:427
  23.6 19.4 %collective-permute-start.4 = (bf16[144,1536]{1,0:T(8,128)(2,1)S(1)}, bf16[144,1536]{1,0:T(8,128)(2,1)S(1)}, u32[]{:S(2)}, u32[]{:S(2)}) collective-permute-start(bf16[144,1536]{1,0:T(8,128)(2,1)S(1)} %shard_map.96.refs_1_), channel_id=1, source_target_pairs={{0,1},{1,0},{2,3},{3,2},{4,5},{5,4},{6,7},{7,6},{8,9},{9,8},{10,11... | collective-permute-start | bytes 1327112 | tf_op jit(solution)/shard_map/ppermute | solution.py:427
  23.6 19.3 %collective-permute-start.5 = (bf16[144,1536]{1,0:T(8,128)(2,1)S(1)}, bf16[144,1536]{1,0:T(8,128)(2,1)S(1)}, u32[]{:S(2)}, u32[]{:S(2)}) collective-permute-start(bf16[144,1536]{1,0:T(8,128)(2,1)S(1)} %collective-permute-done.1.refs_2_), channel_id=1, source_target_pairs={{0,1},{1,0},{2,3},{3,2},{4,5},{5,4},{6,7},{7,6},{8,9},{9,8},{10,11... | collective-permute-start | bytes 1327112 | tf_op jit(solution)/shard_map/ppermute | solution.py:427
  33.6 9.4 %collective-permute-start.6 = (bf16[144,1536]{1,0:T(8,128)(2,1)S(1)}, bf16[144,1536]{1,0:T(8,128)(2,1)S(1)}, u32[]{:S(2)}, u32[]{:S(2)}) collective-permute-start(bf16[144,1536]{1,0:T(8,128)(2,1)S(1)} %shard_map.97.refs_3_), channel_id=1, source_target_pairs={{0,1},{1,0},{2,3},{3,2},{4,5},{5,4},{6,7},{7,6},{8,9},{9,8},{10,11... | collective-permute-start | bytes 1327112 | tf_op jit(solution)/shard_map/ppermute | solution.py:427
  39.8 12.6 %collective-permute-start.8 = (bf16[144,1536]{1,0:T(8,128)(2,1)S(1)}, bf16[144,1536]{1,0:T(8,128)(2,1)S(1)}, u32[]{:S(2)}, u32[]{:S(2)}) collective-permute-start(bf16[144,1536]{1,0:T(8,128)(2,1)S(1)} %shard_map.98.refs_1_.refs_0_), channel_id=1, source_target_pairs={{0,2},{1,3},{2,0},{3,1},{4,6},{5,7},{6,4},{7,5},{8,10},{9,11},{10,... | collective-permute-start | bytes 1327112 | tf_op jit(solution)/shard_map/ppermute | solution.py:427
  41.3 11.9 %collective-permute-start.9 = (bf16[144,1536]{1,0:T(8,128)(2,1)S(1)}, bf16[144,1536]{1,0:T(8,128)(2,1)S(1)}, u32[]{:S(2)}, u32[]{:S(2)}) collective-permute-start(bf16[144,1536]{1,0:T(8,128)(2,1)S(1)} %shard_map.99.refs_10_), channel_id=1, source_target_pairs={{0,12},{1,13},{2,14},{3,15},{4,0},{5,1},{6,2},{7,3},{8,4},{9,5},{1... | collective-permute-start | bytes 1327112 | tf_op jit(solution)/shard_map/ppermute | solution.py:427
  43.0 16.2 %collective-permute-start.12 = (bf16[144,1536]{1,0:T(8,128)(2,1)S(1)}, bf16[144,1536]{1,0:T(8,128)(2,1)S(1)}, u32[]{:S(2)}, u32[]{:S(2)}) collective-permute-start(bf16[144,1536]{1,0:T(8,128)(2,1)S(1)} %shard_map.98.refs_1_.refs_0_), channel_id=1, source_target_pairs={{0,1},{1,0},{2,3},{3,2},{4,5},{5,4},{6,7},{7,6},{8,9},{9,8},{10,11... | collective-permute-start | bytes 1327112 | tf_op jit(solution)/shard_map/ppermute | solution.py:427
  53.2 11.9 %collective-permute-start.15 = (bf16[144,1536]{1,0:T(8,128)(2,1)S(1)}, bf16[144,1536]{1,0:T(8,128)(2,1)S(1)}, u32[]{:S(2)}, u32[]{:S(2)}) collective-permute-start(bf16[144,1536]{1,0:T(8,128)(2,1)S(1)} %shard_map.102.refs_1_.refs_0_), channel_id=1, source_target_pairs={{0,2},{1,3},{2,0},{3,1},{4,6},{5,7},{6,4},{7,5},{8,10},{9,11},{10,... | collective-permute-start | bytes 1327112 | tf_op jit(solution)/shard_map/ppermute | solution.py:427
  58.6 13.4 %collective-permute-start.16 = (bf16[144,1536]{1,0:T(8,128)(2,1)S(1)}, bf16[144,1536]{1,0:T(8,128)(2,1)S(1)}, u32[]{:S(2)}, u32[]{:S(2)}) collective-permute-start(bf16[144,1536]{1,0:T(8,128)(2,1)S(1)} %shard_map.102.refs_1_.refs_0_), channel_id=1, source_target_pairs={{0,1},{1,0},{2,3},{3,2},{4,5},{5,4},{6,7},{7,6},{8,9},{9,8},{10,11... | collective-permute-start | bytes 1327112 | tf_op jit(solution)/shard_map/ppermute | solution.py:427
  65.1 18.9 %collective-permute-start.10 = (bf16[144,1536]{1,0:T(8,128)(2,1)S(1)}, bf16[144,1536]{1,0:T(8,128)(2,1)S(1)}, u32[]{:S(2)}, u32[]{:S(2)}) collective-permute-start(bf16[144,1536]{1,0:T(8,128)(2,1)S(1)} %get-tuple-element.51), channel_id=1, source_target_pairs={{0,1},{1,0},{2,3},{3,2},{4,5},{5,4},{6,7},{7,6},{8,9},{9,8},{10,11... | collective-permute-start | bytes 1327112 | tf_op jit(solution)/shard_map/ppermute | solution.py:427
  65.7 18.3 %collective-permute-start.14 = (bf16[144,1536]{1,0:T(8,128)(2,1)S(1)}, bf16[144,1536]{1,0:T(8,128)(2,1)S(1)}, u32[]{:S(2)}, u32[]{:S(2)}) collective-permute-start(bf16[144,1536]{1,0:T(8,128)(2,1)S(1)} %shard_map.105.refs_1_), channel_id=1, source_target_pairs={{0,2},{1,3},{2,0},{3,1},{4,6},{5,7},{6,4},{7,5},{8,10},{9,11},{10,... | collective-permute-start | bytes 1327112 | tf_op jit(solution)/shard_map/ppermute | solution.py:427
  72.1 13.9 %collective-permute-start.20 = (bf16[72,1536]{1,0:T(8,128)(2,1)S(1)}, bf16[72,1536]{1,0:T(8,128)(2,1)S(1)}, u32[]{:S(2)}, u32[]{:S(2)}) collective-permute-start(bf16[72,1536]{1,0:T(8,128)(2,1)S(1)} %get-tuple-element.66), channel_id=1, source_target_pairs={{0,1},{1,0},{2,3},{3,2},{4,5},{5,4},{6,7},{7,6},{8,9},{9,8},{10,11... | collective-permute-start | bytes 663560 | tf_op jit(solution)/shard_map/ppermute | solution.py:427
  84.2 9.0 %collective-permute-start.19 = (bf16[72,1536]{1,0:T(8,128)(2,1)S(1)}, bf16[72,1536]{1,0:T(8,128)(2,1)S(1)}, u32[]{:S(2)}, u32[]{:S(2)}) collective-permute-start(bf16[72,1536]{1,0:T(8,128)(2,1)S(1)} %get-tuple-element.64), channel_id=1, source_target_pairs={{0,12},{1,13},{2,14},{3,15},{4,0},{5,1},{6,2},{7,3},{8,4},{9,5},{1... | collective-permute-start | bytes 663560 | tf_op jit(solution)/shard_map/ppermute | solution.py:427
  85.8 17.7 %collective-permute-start.23 = (bf16[72,1536]{1,0:T(8,128)(2,1)S(1)}, bf16[72,1536]{1,0:T(8,128)(2,1)S(1)}, u32[]{:S(2)}, u32[]{:S(2)}) collective-permute-start(bf16[72,1536]{1,0:T(8,128)(2,1)S(1)} %get-tuple-element.68), channel_id=1, source_target_pairs={{0,1},{1,0},{2,3},{3,2},{4,5},{5,4},{6,7},{7,6},{8,9},{9,8},{10,11... | collective-permute-start | bytes 663560 | tf_op jit(solution)/shard_map/ppermute | solution.py:427
  90.7 15.4 %collective-permute-start.22 = (bf16[72,1536]{1,0:T(8,128)(2,1)S(1)}, bf16[72,1536]{1,0:T(8,128)(2,1)S(1)}, u32[]{:S(2)}, u32[]{:S(2)}) collective-permute-start(bf16[72,1536]{1,0:T(8,128)(2,1)S(1)} %shard_map.112.refs_6_.refs_3_), channel_id=1, source_target_pairs={{0,8},{1,9},{2,10},{3,11},{4,12},{5,13},{6,14},{7,15},{8,0},{9,1},... | collective-permute-start | bytes 663560 | tf_op jit(solution)/shard_map/ppermute | solution.py:427
  91.1 14.8 %collective-permute-start.25 = (bf16[72,1536]{1,0:T(8,128)(2,1)S(1)}, bf16[72,1536]{1,0:T(8,128)(2,1)S(1)}, u32[]{:S(2)}, u32[]{:S(2)}) collective-permute-start(bf16[72,1536]{1,0:T(8,128)(2,1)S(1)} %shard_map.114.refs_7_), channel_id=1, source_target_pairs={{0,2},{1,3},{2,0},{3,1},{4,6},{5,7},{6,4},{7,5},{8,10},{9,11},{10,... | collective-permute-start | bytes 663560 | tf_op jit(solution)/shard_map/ppermute | solution.py:427
  100.4 15.8 %collective-permute-start.29 = (f32[1,3072]{1,0:T(1,128)S(1)}, f32[1,3072]{1,0:T(1,128)S(1)}, u32[]{:S(2)}, u32[]{:S(2)}) collective-permute-start(f32[1,3072]{1,0:T(1,128)S(1)} %shard_map.119.refs_4_), channel_id=1, source_target_pairs={{0,4},{1,5},{2,6},{3,7},{4,8},{5,9},{6,10},{7,11},{8,12},{9,13},{1... | collective-permute-start | bytes 36872 | tf_op jit(solution)/shard_map/ppermute | solution.py:427
  101.7 14.4 %collective-permute-start.30 = (f32[1,3072]{1,0:T(1,128)S(1)}, f32[1,3072]{1,0:T(1,128)S(1)}, u32[]{:S(2)}, u32[]{:S(2)}) collective-permute-start(f32[1,3072]{1,0:T(1,128)S(1)} %shard_map.119.refs_4_), channel_id=1, source_target_pairs={{0,8},{1,9},{2,10},{3,11},{4,12},{5,13},{6,14},{7,15},{8,0},{9,1},... | collective-permute-start | bytes 36872 | tf_op jit(solution)/shard_map/ppermute | solution.py:427
  103.5 12.7 %collective-permute-start.31 = (f32[1,3072]{1,0:T(1,128)S(1)}, f32[1,3072]{1,0:T(1,128)S(1)}, u32[]{:S(2)}, u32[]{:S(2)}) collective-permute-start(f32[1,3072]{1,0:T(1,128)S(1)} %shard_map.119.refs_4_), channel_id=1, source_target_pairs={{0,12},{1,13},{2,14},{3,15},{4,0},{5,1},{6,2},{7,3},{8,4},{9,5},{1... | collective-permute-start | bytes 36872 | tf_op jit(solution)/shard_map/ppermute | solution.py:427
  106.0 10.2 %collective-permute-start.26 = (bf16[72,1536]{1,0:T(8,128)(2,1)S(1)}, bf16[72,1536]{1,0:T(8,128)(2,1)S(1)}, u32[]{:S(2)}, u32[]{:S(2)}) collective-permute-start(bf16[72,1536]{1,0:T(8,128)(2,1)S(1)} %shard_map.116.refs_6_), channel_id=1, source_target_pairs={{0,4},{1,5},{2,6},{3,7},{4,8},{5,9},{6,10},{7,11},{8,12},{9,13},{1... | collective-permute-start | bytes 663560 | tf_op jit(solution)/shard_map/ppermute | solution.py:427
  (19 other events, 184.9 us)
